TPU v7x, 32 devices: a whole 2x2x4 slice. The times are simulated.
32 devices in a mesh: member: 8 (over y, x, core), tile: 4 (over z).
Axes of the slice: x: 2, y: 2, z: 4, core: 2. Of those that a mesh axis runs over, the one named last changes fastest.
Arguments:
- atmos_state: float32 [8, 4, 32, 72, 256], P('member', None, 'tile'), may hold values from -6 to 6
- ocean_slots: float32 [8, 4, 32, 62, 256], P('member', None, 'tile'), may hold values from -6 to 6
- owner_map: int32 [4], P('tile'), may hold values from 0 to 7
- land_mask: int32 [32, 256], P('tile'), may hold values 0 or 1
- transfer_coefficient: float32 [32, 256], P('tile'), may hold values from 0.5 to 2
- air_mixing: float32 [72, 72], replicated, may hold values from -0.75 to 0.75
- sea_mixing: float32 [62, 62], replicated, may hold values from -0.75 to 0.75
Outputs:
- atmos_next: float32 [8, 4, 32, 72, 256], P('member', None, 'tile')
- ocean_next: float32 [8, 4, 32, 62, 256], P('member', None, 'tile')
Inputs may be any that keep to these rules, and one draw needn't show every extreme that they name: owner_map[t] is the member whose slot holds tile t's ocean; the other slots of that tile are not read.
All inputs are finite; a program needn't handle non-finite values. No bound on the sum of `land_mask` on one device may be relied on, other than what follows from the above.
Results may differ from a plain program's by a relative error of at most 0.0001.
Values sent between devices are 32-bit elements; how exact they have to be, the bound alone decides.
No kernel may reach another device: no remote copies, remote signals or barrier semaphores. Data moves between devices by JAX's collectives and lax.ppermute only.
A program may use at most 64 MiB of HBM per device.

v0:
```python
import functools
import math

import jax
import jax.numpy as jnp
from jax import lax
from jax.experimental import pallas as pl
from jax.experimental.pallas import tpu as pltpu
from jax.sharding import PartitionSpec as P

NSUB = 4
DIFFUSE = 0.2
ADVECT_RATE = 0.15
CORIOLIS_MAX = 0.2
AIR_STEP = 0.05
SEA_STEP = 0.25
SIGNS = (1.0, 1.0, -1.0, -1.0)
FIELDS = 4

F32 = jnp.float32
BF16 = jnp.bfloat16
AXES = ("member", "tile")
VMEM = pl.BlockSpec(memory_space=pltpu.VMEM)
SMEM = pl.BlockSpec(memory_space=pltpu.SMEM)
ANY = pl.BlockSpec(memory_space=pl.ANY)
VMEM_LIMIT = 12 * 2**20


def ceil_to(count, unit):
    return -(-count // unit) * unit


def split_parts(values):
    high = values.astype(BF16).astype(F32)
    return high, (values - high).astype(BF16).astype(F32)


def mixing_parts(mixing, scale):
    levels = mixing.shape[0]
    rows = lax.broadcasted_iota(jnp.int32, mixing.shape, 0)
    columns = lax.broadcasted_iota(jnp.int32, mixing.shape, 1)
    both = scale * mixing + jnp.where(rows == columns, scale, 0.0)
    high, low = split_parts(both)
    pad = jnp.zeros((levels, ceil_to(levels, 16) - levels), F32)
    parts = [high, pad, high, pad, low, pad]
    if pad.shape[1] == 0:
        parts = [high, high, low]
    return jnp.concatenate(parts, axis=1).astype(BF16)


def stage(cells, staged, offset, depth):
    count, lon = cells.shape
    if count < 16:
        cells = jnp.concatenate([cells, jnp.zeros((16 - count, lon), F32)], axis=0)
    high = cells.astype(BF16)
    low = (cells - high.astype(F32)).astype(BF16)
    staged[offset : offset + 16] = high
    staged[depth + offset : depth + offset + 16] = low
    staged[2 * depth + offset : 2 * depth + offset + 16] = high


def stage_dynamics(center, outer, inner, sign, coriolis, staged):
    levels, lon = center.shape[1:]
    depth = ceil_to(levels, 16)
    rate = 0.5 * ADVECT_RATE / DIFFUSE
    for offset in range(0, levels, 16):
        part = slice(offset, min(offset + 16, levels))
        cells = [center[f, part] for f in range(FIELDS)]
        east_wind = rate * cells[2]
        north_wind = (rate * sign) * cells[3]
        for f in range(FIELDS):
            outer_row, inner_row = outer[f, part], inner[f, part]
            east = pltpu.roll(cells[f], lon - 1, 1)
            west = pltpu.roll(cells[f], 1, 1)
            total = ((east + west) + (outer_row + inner_row)) + cells[f]
            if f < 2:
                total = total - (east_wind * (east - west) + north_wind * (outer_row - inner_row))
            elif f == 2:
                total = total + coriolis * cells[3]
            else:
                total = total - coriolis * cells[2]
            stage(total, staged.at[f], offset, depth)


def surface_flux(center, surface, place):
    sst, sst_tanh, cur_east, cur_north, rate = [surface[k, place] for k in range(5)]
    east = center[2, 0:1] - cur_east
    north = center[3, 0:1] - cur_north
    factor = rate * jnp.sqrt(1.0 + east * east + north * north)
    return (
        factor * (sst - center[0, 0:1]),
        factor * (sst_tanh - center[1, 0:1]),
        factor * east,
        factor * north,
    )


def tile_state(rows):
    tile = lax.axis_index("tile")
    return lax.rem(tile, 2) == 0, tile * rows


def own_row(north_first, rows, place):
    return jnp.where(north_first, rows - 1 - place, place)


def place_values(coriolis, rows, place):
    north_first, first_row = tile_state(rows)
    index = first_row + own_row(north_first, rows, place - NSUB)
    total = coriolis.shape[0] - 2 * NSUB
    valid = jnp.where((index >= 0) & (index < total), 1.0, 0.0)
    return coriolis[index + NSUB], valid


def advance(state, surface, total, weights, staged, coriolis, step, places, targets):
    rows = state.shape[1] - 2 * NSUB
    sign = jnp.where(tile_state(rows)[0], 1.0, -1.0)
    for k, place in enumerate(places):
        center, outer, inner = [state.at[step, place + shift] for shift in (0, -1, 1)]
        turn, _ = place_values(coriolis, rows, place)
        stage_dynamics(center, outer, inner, sign, turn, staged.at[k])
    for k, place in enumerate(places):
        center = state.at[step, place]
        target = targets[k]
        flux = surface_flux(center, surface, place)
        _, valid = place_values(coriolis, rows, place)
        for f in range(FIELDS):
            total[place, f] = total[place, f] + flux[f]
            mixed = jnp.dot(weights[...], staged[k, f], preferred_element_type=F32)
            target[f] = valid * mixed
            target[f, 0:1] = valid * (mixed[0:1] + (AIR_STEP * SIGNS[f]) * flux[f])


def pack_kernel(depth, owner, air, sea, first, second, top, sems, top_sems):
    rows = air.shape[2]
    north_first, _ = tile_state(rows)
    copies = []
    for d in range(depth):
        for side, out in enumerate((first, second)):
            row = own_row(north_first, rows, d if side == 0 else rows - 1 - d)
            copies.append(
                pltpu.make_async_copy(air.at[0, :, row], out.at[d], sems.at[2 * d + side])
            )
    for k, f in enumerate((0, 2, 3)):
        copies.append(pltpu.make_async_copy(sea.at[0, f, 0], top.at[k], top_sems.at[k]))
    for copy in copies:
        copy.start()
    for copy in copies:
        copy.wait()

    @pl.when(lax.axis_index("member") != owner[0])
    def _():
        top[...] = jnp.zeros_like(top)


def ocean_kernel(owner, air, sea, land, air_mixing, sea_mixing, state, weights, base, sea_next,
                 staged, sea_weights, sems, sea_sem):
    rows = air.shape[2]
    levels = sea.shape[2]
    depth = ceil_to(levels, 16)
    north_first, _ = tile_state(rows)
    copies = []
    for place in range(rows):
        row = own_row(north_first, rows, place)
        copies.append(
            pltpu.make_async_copy(air.at[0, :, row], state.at[0, NSUB + place], sems.at[place])
        )
    for copy in copies:
        copy.start()
    weights[...] = mixing_parts(air_mixing[...], 0.5 * DIFFUSE)

    @pl.when(lax.axis_index("member") == owner[0])
    def _():
        copy = pltpu.make_async_copy(sea.at[0], base, sea_sem)
        copy.start()
        sea_weights[...] = mixing_parts(sea_mixing[...], 0.5)
        copy.wait()

        def body(row, carry):
            for f in range(FIELDS):
                cells = base[f, :, row]
                for offset in range(0, levels, 16):
                    part = slice(offset, min(offset + 16, levels))
                    stage(cells[part], staged.at[f], offset, depth)
            at_sea = land[pl.ds(row, 1)] == 1
            for f in range(FIELDS):
                mixed = jnp.dot(sea_weights[...], staged[f], preferred_element_type=F32)
                base[f, :, row] = jnp.where(at_sea, mixed, base[f, :, row])
            return carry

        lax.fori_loop(0, rows, body, 0)

    @pl.when(lax.axis_index("member") != owner[0])
    def _():
        copy = pltpu.make_async_copy(sea, sea_next, sea_sem)
        copy.start()
        copy.wait()

    for copy in copies:
        copy.wait()


def interior_kernel(coriolis, top_a, top_b, top_c, top_d, land, transfer, weights, state_in,
                    state, surface, total, first, second, first_top, second_top, staged, sems):
    del state_in
    rows = land.shape[0]
    last = NSUB + rows - 1
    north_first, _ = tile_state(rows)
    copies = [
        pltpu.make_async_copy(state.at[0, NSUB + 2], first.at[0], sems.at[0]),
        pltpu.make_async_copy(state.at[0, last - 2], second.at[0], sems.at[1]),
    ]
    for copy in copies:
        copy.start()
    total[...] = jnp.zeros_like(total)
    for place in range(rows):
        row = pl.ds(own_row(north_first, rows, place), 1)
        for k, kept in enumerate((0, 2, 3)):
            value = (top_a[k, row] + top_b[k, row]) + (top_c[k, row] + top_d[k, row])
            surface[kept, NSUB + place] = value
        surface[1, NSUB + place] = jnp.tanh(surface[0, NSUB + place])
        surface[4, NSUB + place] = transfer[row] * land[row].astype(F32)
    for d in range(NSUB - 1):
        for k, kept in enumerate((0, 2, 3, 4)):
            first_top[k, d : d + 1] = surface[kept, NSUB + d]
            second_top[k, d : d + 1] = surface[kept, last - d]

    for step in range(NSUB - 1):
        def body(d, carry):
            places = (NSUB + d, last - d)
            targets = [state.at[step + 1, place] for place in places]
            advance(state, surface, total, weights, staged, coriolis, step, places, targets)
            return carry

        lax.fori_loop(step + 1, rows // 2, body, 0)
    for copy in copies:
        copy.wait()


def chain(number, state, surface, total, weights, staged, coriolis, final, arrived, arrived_at):
    places = state.shape[1]
    for side in range(2):
        place = NSUB - number if side == 0 else places - 1 - NSUB + number
        _, valid = place_values(coriolis, places - 2 * NSUB, place)
        for f in range(FIELDS):
            state[0, place, f] = valid * arrived[side][arrived_at, f]

    def step_places(step):
        low = NSUB + step + 1 - number
        return low, places - 1 - low

    def body(step, carry):
        pair = step_places(step)
        targets = [state.at[step + 1, place] for place in pair]
        advance(state, surface, total, weights, staged, coriolis, step, pair, targets)
        return carry

    lax.fori_loop(0, NSUB - 1, body, 0)
    pair = step_places(NSUB - 1)
    targets = [final.at[side] for side in range(2)]
    advance(state, surface, total, weights, staged, coriolis, NSUB - 1, pair, targets)


def send_rows(number, final, air_next, sems):
    rows = air_next.shape[2]
    north_first, _ = tile_state(rows)
    copies = []
    for side in range(2):
        row = own_row(north_first, rows, NSUB - number if side == 0 else rows - 1 - NSUB + number)
        copies.append(pltpu.make_async_copy(final.at[side], air_next.at[0, :, row], sems.at[side]))
    for copy in copies:
        copy.start()
    return copies


def halo_surface(surface, beside):
    places = surface.shape[1]
    for side in range(2):
        for d in range(NSUB - 1):
            place = NSUB - 1 - d if side == 0 else places - NSUB + d
            for k, kept in enumerate((0, 2, 3, 4)):
                surface[kept, place] = beside[side][k, d : d + 1]
            surface[1, place] = jnp.tanh(surface[0, place])


def first_chains_kernel(coriolis, weights, near, far, near_surface, far_surface,
                        state_in, surface_in, total_in, state, surface, total, air_next,
                        first, second, staged, final, sems, send_sems):
    del state_in, surface_in, total_in
    places = state.shape[1]
    sends = [
        pltpu.make_async_copy(state.at[0, NSUB + 3], first.at[0], send_sems.at[0]),
        pltpu.make_async_copy(state.at[0, places - 1 - NSUB - 3], second.at[0], send_sems.at[1]),
    ]
    for copy in sends:
        copy.start()
    halo_surface(surface, (near_surface, far_surface))
    copies = []
    for number in (1, 2):
        chain(number, state, surface, total, weights, staged, coriolis,
              final.at[number - 1], (near, far), number - 1)
        copies += send_rows(number, final.at[number - 1], air_next, sems.at[number - 1])
    for copy in sends + copies:
        copy.wait()


def third_chain_kernel(coriolis, weights, near, far, surface, state_in, total_in, air_in,
                       state, total, air_next, flux, staged, final, sems):
    del state_in, total_in, air_in
    rows = state.shape[1] - 2 * NSUB
    chain(3, state, surface, total, weights, staged, coriolis, final, (near, far), 0)
    copies = send_rows(3, final, air_next, sems)
    for place in (NSUB, NSUB + rows - 1):
        last = surface_flux(state.at[NSUB - 1, place], surface, place)
        for f in range(FIELDS):
            total[place, f] = total[place, f] + last[f]
    for place in range(rows):
        for f in range(FIELDS):
            flux[f, place : place + 1] = total[NSUB + place, f]
    for copy in copies:
        copy.wait()


def last_chain_kernel(coriolis, weights, near, far, surface, state_in, total_in, air_in,
                      air_next, state, total, staged, final, sems):
    del state_in, total_in, air_in
    chain(4, state, surface, total, weights, staged, coriolis, final, (near, far), 0)
    for copy in send_rows(4, final, air_next, sems):
        copy.wait()


def sea_kernel(scale, owner, column, flux_a, flux_b, flux_c, flux_d, land, base, sea_in, after,
               sea_next, result, mean, sems):
    del sea_in, after

    @pl.when(lax.axis_index("member") == owner[0])
    def _():
        rows, levels = land.shape[0], base.shape[1]
        north_first, _ = tile_state(rows)
        at_sea = land[...] == 1
        for f in range(FIELDS):
            for place in range(rows):
                part = slice(place, place + 1)
                value = (flux_a[f, part] + flux_b[f, part]) + (flux_c[f, part] + flux_d[f, part])
                mean[f, pl.ds(own_row(north_first, rows, place), 1)] = value
        copies = []
        for f in range(FIELDS):
            forcing = jnp.where(at_sea, (0.5 * scale) * mean[f], 0.0)
            for level in range(levels):
                factor = column[level] + 1.0 if level == 0 else column[level]
                result[f, level] = base[f, level] + factor * forcing
            copies.append(pltpu.make_async_copy(result.at[f], sea_next.at[0, f], sems.at[f]))
            copies[-1].start()
        for copy in copies:
            copy.wait()


def pairings(members, tiles):
    both = []
    for side in range(2):
        pairs = []
        for member in range(members):
            for tile in range(tiles):
                other = tile + 1 if (tile + side) % 2 == 0 else tile - 1
                if 0 <= other < tiles:
                    to = member * tiles + other
                else:
                    to = (member ^ 1) * tiles + tile
                pairs.append((member * tiles + tile, to))
        both.append(pairs)
    return both


def params(**more):
    return pltpu.CompilerParams(vmem_limit_bytes=VMEM_LIMIT, **more)


def cost(flops, moved):
    return pl.CostEstimate(flops=int(flops), bytes_accessed=int(moved), transcendentals=0)


def exchange(values, swaps):
    return [lax.ppermute(value, AXES, swap) for value, swap in zip(values, swaps)]


def member_parts(values, members):
    def swapped(block, k):
        return lax.ppermute(block, "member", [(i, i ^ k) for i in range(members)])

    k = 1
    while members > 4 * k:
        values = values + swapped(values, k)
        k *= 2
    parts = [values]
    for other in range(k, members, k):
        parts.append(swapped(values, other))
    return parts


def shards(
    atmos_state, ocean_slots, owner_map, land_mask, transfer_coefficient, air_mixing, sea_mixing
):
    members, tiles = lax.axis_size("member"), lax.axis_size("tile")
    _, _, rows, levels, lon = atmos_state.shape
    sea_levels = ocean_slots.shape[3]
    places = rows + 2 * NSUB
    depth, sea_depth = ceil_to(levels, 16), ceil_to(sea_levels, 16)
    swaps = pairings(members, tiles)
    sea_slots = jnp.swapaxes(ocean_slots, 2, 3)

    row_total = rows * tiles
    row_index = jnp.arange(-NSUB, row_total + NSUB)
    latitude = math.pi * ((row_index.astype(F32) + 0.5) / row_total - 0.5)
    coriolis = (CORIOLIS_MAX / DIFFUSE) * jnp.sin(latitude)

    def rows_of(count):
        return jax.ShapeDtypeStruct((count, FIELDS, levels, lon), F32)

    state_type = pltpu.VMEM((NSUB, places, FIELDS, levels, lon), F32)
    surface_type = pltpu.VMEM((5, places, 1, lon), F32)
    total_type = pltpu.VMEM((places, FIELDS, 1, lon), F32)
    staged = pltpu.VMEM((2, FIELDS, 3 * depth, lon), BF16)
    final = pltpu.VMEM((2, FIELDS, levels, lon), F32)
    air_type = pltpu.HBM(atmos_state.shape, F32)
    sea_type = pltpu.HBM(sea_slots.shape, F32)
    top_type = pltpu.VMEM((4, NSUB - 1, lon), F32)
    atmos_state = pltpu.with_memory_space_constraint(atmos_state, pltpu.HBM)
    sea_slots = pltpu.with_memory_space_constraint(sea_slots, pltpu.HBM)

    *near_rows, sea_top = pl.pallas_call(
        functools.partial(pack_kernel, 2),
        name="pack_rows",
        out_shape=(rows_of(2), rows_of(2), pltpu.VMEM((3, rows, lon), F32)),
        in_specs=[SMEM, ANY, ANY],
        out_specs=(ANY, ANY, VMEM),
        scratch_shapes=[pltpu.SemaphoreType.DMA((4,)), pltpu.SemaphoreType.DMA((3,))],
        compiler_params=params(),
    )(owner_map, atmos_state, sea_slots)
    arrived = exchange(near_rows, swaps)
    top_parts = member_parts(sea_top, members)

    state, weights, base, sea_next = pl.pallas_call(
        ocean_kernel,
        name="sea_mixing",
        out_shape=(
            state_type,
            pltpu.VMEM((levels, 3 * depth), BF16),
            pltpu.VMEM(sea_slots.shape[1:], F32),
            sea_type,
        ),
        in_specs=[SMEM, ANY, ANY, VMEM, VMEM, VMEM],
        out_specs=(VMEM, VMEM, VMEM, ANY),
        scratch_shapes=[
            pltpu.VMEM((FIELDS, 3 * sea_depth, lon), BF16),
            pltpu.VMEM((sea_levels, 3 * sea_depth), BF16),
            pltpu.SemaphoreType.DMA((rows,)),
            pltpu.SemaphoreType.DMA,
        ],
        compiler_params=params(),
    )(owner_map, atmos_state, sea_slots, land_mask, air_mixing, sea_mixing)

    state, surface, total, *more = pl.pallas_call(
        interior_kernel,
        name="interior",
        out_shape=(
            state_type, surface_type, total_type, rows_of(1), rows_of(1), top_type, top_type
        ),
        in_specs=[SMEM] + [VMEM] * 8,
        out_specs=(VMEM, VMEM, VMEM, ANY, ANY, VMEM, VMEM),
        input_output_aliases={8: 0},
        scratch_shapes=[staged, pltpu.SemaphoreType.DMA((2,))],
        compiler_params=params(),
    )(coriolis, *top_parts, land_mask, transfer_coefficient, weights, state)
    beside = exchange(more[2:], swaps)
    arrived_third = exchange(more[:2], swaps)

    state, surface, total, air_next, *fourth_rows = pl.pallas_call(
        first_chains_kernel,
        name="first_chains",
        out_shape=(state_type, surface_type, total_type, air_type, rows_of(1), rows_of(1)),
        in_specs=[SMEM] + [VMEM] * 8,
        out_specs=(VMEM, VMEM, VMEM, ANY, ANY, ANY),
        input_output_aliases={6: 0, 7: 1, 8: 2},
        scratch_shapes=[
            staged,
            pltpu.VMEM((2, 2, FIELDS, levels, lon), F32),
            pltpu.SemaphoreType.DMA((2, 2)),
            pltpu.SemaphoreType.DMA((2,)),
        ],
        compiler_params=params(),
    )(coriolis, weights, *arrived, *beside, state, surface, total)
    arrived_fourth = exchange(fourth_rows, swaps)

    state, total, air_next, flux = pl.pallas_call(
        third_chain_kernel,
        name="third_chain",
        out_shape=(state_type, total_type, air_type, pltpu.VMEM((FIELDS, rows, lon), F32)),
        in_specs=[SMEM] + [VMEM] * 6 + [ANY],
        out_specs=(VMEM, VMEM, ANY, VMEM),
        input_output_aliases={5: 0, 6: 1, 7: 2},
        scratch_shapes=[staged, final, pltpu.SemaphoreType.DMA((2,))],
        compiler_params=params(),
    )(coriolis, weights, *arrived_third, surface, state, total, air_next)
    flux_parts = member_parts(flux, members)

    air_next, _, _ = pl.pallas_call(
        last_chain_kernel,
        name="last_chain",
        out_shape=(air_type, state_type, total_type),
        in_specs=[SMEM] + [VMEM] * 6 + [ANY],
        out_specs=(ANY, VMEM, VMEM),
        input_output_aliases={5: 1, 6: 2, 7: 0},
        scratch_shapes=[staged, final, pltpu.SemaphoreType.DMA((2,))],
        compiler_params=params(),
    )(coriolis, weights, *arrived_fourth, surface, state, total, air_next)

    after = pltpu.with_memory_space_constraint(air_next, pltpu.HBM)
    sea_next = pl.pallas_call(
        functools.partial(sea_kernel, SEA_STEP / (NSUB * members)),
        name="sea_step",
        out_shape=sea_type,
        in_specs=[SMEM, SMEM] + [VMEM] * 6 + [ANY, ANY],
        out_specs=ANY,
        input_output_aliases={8: 0},
        scratch_shapes=[
            pltpu.VMEM(sea_slots.shape[1:], F32),
            pltpu.VMEM((FIELDS, rows, lon), F32),
            pltpu.SemaphoreType.DMA((FIELDS,)),
        ],
        compiler_params=params(),
    )(owner_map, sea_mixing[:, 0], *flux_parts, land_mask, base, sea_next, after)
    return (air_next, jnp.swapaxes(sea_next, 2, 3))


def solution(mesh):
    placed = (
        P("member", None, "tile", None, None),
        P("member", None, "tile", None, None),
        P("tile"),
        P("tile", None),
        P("tile", None),
        P(),
        P(),
    )
    return jax.shard_map(
        shards,
        mesh=mesh,
        in_specs=placed,
        out_specs=(P("member", None, "tile", None, None), P("member", None, "tile", None, None)),
        check_vma=False,
    )
```

profile of v0, /device:TPU:0, one launch (start us, length us, event | category | flops | bytes accessed | tf_op | source)
XLA Modules:
  0.0 113.2 jit_solution(8188442164799687351)
XLA Ops:
  0.6 0.0 copy-start.1
  0.6 0.0 copy-start.2
  0.7 0.0 copy-start
  1.3 1.3 %pack_rows.1 = (f32[2,4,72,256]{3,2,1,0:T(8,128)S(1)}, f32[2,4,72,256]{3,2,1,0:T(8,128)S(1)}, f32[3,8,256]{2,1,0:T(8,128)S(1)}) custom-call(s32[1]{0:T(128)S(6)} %copy.31.owner, f32[1,4,8,72,256]{4,3,2,1,0:T(8,128)} %air.3, f32[1,4,62,8,256]{4,3,2,1,0:T(8,128)} %bitcast.2), custom_call_target="tpu_custom_call" | custom-call | tf_op jit(solution)/shard_map/pack_rows/pallas_call | solution.py:430
  2.7 0.0 copy-start.3
  2.7 3.1 %collective-permute-start = (f32[2,4,72,256]{3,2,1,0:T(8,128)S(1)}, f32[2,4,72,256]{3,2,1,0:T(8,128)S(1)}, u32[]{:S(2)}, u32[]{:S(2)}) collective-permute-start(f32[2,4,72,256]{3,2,1,0:T(8,128)S(1)} %get-tuple-element.28), channel_id=1, source_target_pairs={{0,1},{1,0},{2,3},{3,2},{4,5},{5,4},{6,7},{7,6},{8,9},{9,8},{10,11... | collective-permute-start | bytes 1769480 | tf_op jit(solution)/shard_map/ppermute | solution.py:383
  5.8 0.0 collective-permute-start.1
  5.8 0.5 collective-permute-start.2
  6.3 1.5 %collective-permute-done.2 = f32[3,8,256]{2,1,0:T(8,128)S(1)} collective-permute-done((f32[3,8,256]{2,1,0:T(8,128)S(1)}, f32[3,8,256]{2,1,0:T(8,128)S(1)}, u32[]{:S(2)}, u32[]{:S(2)}) %collective-permute-start.2) | collective-permute-done | bytes 24608 | tf_op jit(solution)/shard_map/ppermute | solution.py:388
  7.8 1.5 %collective-permute-start.3 = (f32[3,8,256]{2,1,0:T(8,128)S(1)}, f32[3,8,256]{2,1,0:T(8,128)S(1)}, u32[]{:S(2)}, u32[]{:S(2)}) collective-permute-start(f32[3,8,256]{2,1,0:T(8,128)S(1)} %add.31.top_a), channel_id=1, source_target_pairs={{0,8},{4,12},{8,0},{12,4},{16,24},{20,28},{24,16},{28,20},{1,9},{5... | collective-permute-start | bytes 73736 | tf_op jit(solution)/shard_map/ppermute | solution.py:388
  9.3 1.5 %collective-permute-start.4 = (f32[3,8,256]{2,1,0:T(8,128)S(1)}, f32[3,8,256]{2,1,0:T(8,128)S(1)}, u32[]{:S(2)}, u32[]{:S(2)}) collective-permute-start(f32[3,8,256]{2,1,0:T(8,128)S(1)} %add.31.top_a), channel_id=1, source_target_pairs={{0,16},{4,20},{8,24},{12,28},{16,0},{20,4},{24,8},{28,12},{1,17},{... | collective-permute-start | bytes 73736 | tf_op jit(solution)/shard_map/ppermute | solution.py:388
  10.8 0.5 collective-permute-start.5
  11.3 0.0 copy-done.1
  11.4 0.0 copy-done.2
  11.4 0.0 copy-done
  11.4 62.8 %sea_mixing.2 = (f32[4,16,4,72,256]{4,3,2,1,0:T(8,128)S(1)}, bf16[72,240]{1,0:T(8,128)(2,1)S(1)}, f32[4,62,8,256]{3,2,1,0:T(8,128)S(1)}, f32[1,4,62,8,256]{4,3,2,1,0:T(8,128)}) custom-call(s32[1]{0:T(128)S(6)} %copy.31.owner, f32[1,4,8,72,256]{4,3,2,1,0:T(8,128)} %air.3, f32[1,4,62,8,256]{4,3,2,1,0:T(8,128)} %bitcast.3, s32[8,256]{1,0:T(8,128)S(1)} %copy-done.1, ...), custom_call_target="tpu_custom_call" | custom-call | tf_op jit(solution)/shard_map/sea_mixing/pallas_call | solution.py:442
  74.2 0.0 collective-permute-done.3.top_b
  74.2 0.0 collective-permute-done.4.top_c
  74.2 0.0 collective-permute-done.5.top_d
  74.2 0.0 copy-done.3
  74.3 4.4 %interior.1 = (f32[4,16,4,72,256]{4,3,2,1,0:T(8,128)S(1)}, f32[5,16,1,256]{3,2,1,0:T(1,128)S(1)}, f32[16,4,1,256]{3,2,1,0:T(1,128)S(1)}, f32[1,4,72,256]{3,2,1,0...) custom-call(f32[40]{0:T(128)S(1)} %multiply_sine_fusion.coriolis, ...), custom_call_target="tpu_custom_call", output_to_operand_aliasing={{0}: (8, {})} | custom-call | tf_op jit(solution)/shard_map/interior/pallas_call | solution.py:462
  78.6 2.4 %collective-permute-start.10 = (f32[1,4,72,256]{3,2,1,0:T(8,128)S(1)}, f32[1,4,72,256]{3,2,1,0:T(8,128)S(1)}, u32[]{:S(2)}, u32[]{:S(2)}) collective-permute-start(f32[1,4,72,256]{3,2,1,0:T(8,128)S(1)} %get-tuple-element.40), channel_id=1, source_target_pairs={{0,1},{1,0},{2,3},{3,2},{4,5},{5,4},{6,7},{7,6},{8,9},{9,8},{10,11... | collective-permute-start | bytes 884744 | tf_op jit(solution)/shard_map/ppermute | solution.py:383
  81.0 0.0 collective-permute-start.11
  81.0 0.2 collective-permute-start.6
  81.2 6.7 %collective-permute-done.6.near_surface = f32[4,3,256]{2,1,0:T(4,128)S(1)} collective-permute-done((f32[4,3,256]{2,1,0:T(4,128)S(1)}, f32[4,3,256]{2,1,0:T(4,128)S(1)}, u32[]{:S(2)}, u32[]{:S(2)}) %collective-permute-start.6) | collective-permute-done | bytes 12320 | tf_op jit(solution)/shard_map/ppermute | solution.py:383
  87.9 0.0 collective-permute-start.7
  87.9 1.2 %collective-permute-done.7.far_surface = f32[4,3,256]{2,1,0:T(4,128)S(1)} collective-permute-done((f32[4,3,256]{2,1,0:T(4,128)S(1)}, f32[4,3,256]{2,1,0:T(4,128)S(1)}, u32[]{:S(2)}, u32[]{:S(2)}) %collective-permute-start.7) | collective-permute-done | bytes 12320 | tf_op jit(solution)/shard_map/ppermute | solution.py:383
  89.0 0.0 collective-permute-done.near
  89.0 0.0 collective-permute-done.1.far
  89.0 6.4 %first_chains.1 = (f32[4,16,4,72,256]{4,3,2,1,0:T(8,128)S(1)}, f32[5,16,1,256]{3,2,1,0:T(1,128)S(1)}, f32[16,4,1,256]{3,2,1,0:T(1,128)S(1)}, f32[1,4,8,72,256]{4...) custom-call(f32[40]{0:T(128)S(1)} %multiply_sine_fusion.coriolis, ...), custom_call_target="tpu_custom_call", output_to_operand_aliasing={{0}: (6, {}), {1}: (7, {}), {2}: (8, {})} | custom-call | tf_op jit(solution)/shard_map/first_chains/pallas_call | solution.py:477
  95.4 4.4 %collective-permute-start.8 = (f32[1,4,72,256]{3,2,1,0:T(8,128)S(1)}, f32[1,4,72,256]{3,2,1,0:T(8,128)S(1)}, u32[]{:S(2)}, u32[]{:S(2)}) collective-permute-start(f32[1,4,72,256]{3,2,1,0:T(8,128)S(1)} %get-tuple-element.37), channel_id=1, source_target_pairs={{0,1},{1,0},{2,3},{3,2},{4,5},{5,4},{6,7},{7,6},{8,9},{9,8},{10,11... | collective-permute-start | bytes 884744 | tf_op jit(solution)/shard_map/ppermute | solution.py:383
  99.8 0.0 collective-permute-start.9
  99.8 0.0 collective-permute-done.10.near
  99.8 0.0 collective-permute-done.11.far
  99.8 3.8 %third_chain.1 = (f32[4,16,4,72,256]{4,3,2,1,0:T(8,128)S(1)}, f32[16,4,1,256]{3,2,1,0:T(1,128)S(1)}, f32[1,4,8,72,256]{4,3,2,1,0:T(8,128)}, f32[4,8,256]{2,1,0:T(8,128)S(1)}) custom-call(f32[40]{0:T(128)S(1)} %multiply_sine_fusion.coriolis, ...), custom_call_target="tpu_custom_call", output_to_operand_aliasing={{0}: (5, {}), {1}: (6, {}), {2}: (7, {})} | custom-call | tf_op jit(solution)/shard_map/third_chain/pallas_call | solution.py:494
  103.7 0.6 collective-permute-start.12
  104.2 0.9 collective-permute-done.12
  105.1 1.5 %collective-permute-start.13 = (f32[4,8,256]{2,1,0:T(8,128)S(1)}, f32[4,8,256]{2,1,0:T(8,128)S(1)}, u32[]{:S(2)}, u32[]{:S(2)}) collective-permute-start(f32[4,8,256]{2,1,0:T(8,128)S(1)} %add.32.flux_a), channel_id=1, source_target_pairs={{0,8},{4,12},{8,0},{12,4},{16,24},{20,28},{24,16},{28,20},{1,9},{5... | collective-permute-start | bytes 98312 | tf_op jit(solution)/shard_map/ppermute | solution.py:388
  106.6 0.2 collective-permute-start.14
  106.8 1.7 %collective-permute-start.15 = (f32[4,8,256]{2,1,0:T(8,128)S(1)}, f32[4,8,256]{2,1,0:T(8,128)S(1)}, u32[]{:S(2)}, u32[]{:S(2)}) collective-permute-start(f32[4,8,256]{2,1,0:T(8,128)S(1)} %add.32.flux_a), channel_id=1, source_target_pairs={{0,24},{4,28},{8,16},{12,20},{16,8},{20,12},{24,0},{28,4},{1,25},{... | collective-permute-start | bytes 98312 | tf_op jit(solution)/shard_map/ppermute | solution.py:388
  108.6 0.1 slice_reduce_fusion.column
  108.7 0.0 collective-permute-done.8.near
  108.7 0.0 collective-permute-done.9.far
  108.7 3.8 %last_chain.1 = (f32[1,4,8,72,256]{4,3,2,1,0:T(8,128)}, f32[4,16,4,72,256]{4,3,2,1,0:T(8,128)S(1)}, f32[16,4,1,256]{3,2,1,0:T(1,128)S(1)}) custom-call(f32[40]{0:T(128)S(1)} %multiply_sine_fusion.coriolis, bf16[72,240]{1,0:T(8,128)(2,1)S(1)} %get-tuple-element.27.weights, ...), custom_call_target="tpu_custom_call", output_to_operand_aliasing={{1}: (5, {}), {2}: (6, {}), {0}: (7, {})} | custom-call | tf_op jit(solution)/shard_map/last_chain/pallas_call | solution.py:506
  112.5 0.0 collective-permute-done.13.flux_b
  112.5 0.0 collective-permute-done.14.flux_c
  112.6 0.0 collective-permute-done.15.flux_d
  112.6 0.6 sea_step.1
  (3 shorter events, 0.1 us)
Async XLA Ops:
  0.6 10.7 %copy-start.1 = (s32[8,256]{1,0:T(8,128)S(1)}, s32[8,256]{1,0:T(8,128)}, u32[]{:S(2)}) copy-start(s32[8,256]{1,0:T(8,128)} %land.5) | copy-start | bytes 24580
  0.6 10.7 %copy-start.2 = (f32[72,72]{1,0:T(8,128)S(1)}, f32[72,72]{1,0:T(8,128)}, u32[]{:S(2)}) copy-start(f32[72,72]{1,0:T(8,128)} %air_mixing.1) | copy-start | bytes 62212
  0.7 10.7 %copy-start = (f32[62,62]{1,0:T(8,128)S(1)}, f32[62,62]{1,0:T(8,128)}, u32[]{:S(2)}) copy-start(f32[62,62]{1,0:T(8,128)} %sea_mixing.3) | copy-start | bytes 46132
  2.7 71.6 %copy-start.3 = (f32[8,256]{1,0:T(8,128)S(1)}, f32[8,256]{1,0:T(8,128)}, u32[]{:S(2)}) copy-start(f32[8,256]{1,0:T(8,128)} %transfer.1) | copy-start | bytes 24580
  2.7 86.4 %collective-permute-start = (f32[2,4,72,256]{3,2,1,0:T(8,128)S(1)}, f32[2,4,72,256]{3,2,1,0:T(8,128)S(1)}, u32[]{:S(2)}, u32[]{:S(2)}) collective-permute-start(f32[2,4,72,256]{3,2,1,0:T(8,128)S(1)} %get-tuple-element.28), channel_id=1, source_target_pairs={{0,1},{1,0},{2,3},{3,2},{4,5},{5,4},{6,7},{7,6},{8,9},{9,8},{10,11... | collective-permute-start | bytes 1769480 | tf_op jit(solution)/shard_map/ppermute | solution.py:383
  5.8 83.3 %collective-permute-start.1 = (f32[2,4,72,256]{3,2,1,0:T(8,128)S(1)}, f32[2,4,72,256]{3,2,1,0:T(8,128)S(1)}, u32[]{:S(2)}, u32[]{:S(2)}) collective-permute-start(f32[2,4,72,256]{3,2,1,0:T(8,128)S(1)} %get-tuple-element.29), channel_id=1, source_target_pairs={{0,4},{1,2},{2,1},{3,7},{4,0},{5,6},{6,5},{7,3},{8,12},{9,10},{10,... | collective-permute-start | bytes 1769480 | tf_op jit(solution)/shard_map/ppermute | solution.py:383
  5.8 2.0 %collective-permute-start.2 = (f32[3,8,256]{2,1,0:T(8,128)S(1)}, f32[3,8,256]{2,1,0:T(8,128)S(1)}, u32[]{:S(2)}, u32[]{:S(2)}) collective-permute-start(f32[3,8,256]{2,1,0:T(8,128)S(1)} %get-tuple-element.30), channel_id=1, source_target_pairs={{0,4},{4,0},{8,12},{12,8},{16,20},{20,16},{24,28},{28,24},{1,5},{5... | collective-permute-start | bytes 73736 | tf_op jit(solution)/shard_map/ppermute | solution.py:388
  7.8 66.4 %collective-permute-start.3 = (f32[3,8,256]{2,1,0:T(8,128)S(1)}, f32[3,8,256]{2,1,0:T(8,128)S(1)}, u32[]{:S(2)}, u32[]{:S(2)}) collective-permute-start(f32[3,8,256]{2,1,0:T(8,128)S(1)} %add.31.top_a), channel_id=1, source_target_pairs={{0,8},{4,12},{8,0},{12,4},{16,24},{20,28},{24,16},{28,20},{1,9},{5... | collective-permute-start | bytes 73736 | tf_op jit(solution)/shard_map/ppermute | solution.py:388
  9.3 64.9 %collective-permute-start.4 = (f32[3,8,256]{2,1,0:T(8,128)S(1)}, f32[3,8,256]{2,1,0:T(8,128)S(1)}, u32[]{:S(2)}, u32[]{:S(2)}) collective-permute-start(f32[3,8,256]{2,1,0:T(8,128)S(1)} %add.31.top_a), channel_id=1, source_target_pairs={{0,16},{4,20},{8,24},{12,28},{16,0},{20,4},{24,8},{28,12},{1,17},{... | collective-permute-start | bytes 73736 | tf_op jit(solution)/shard_map/ppermute | solution.py:388
  10.8 63.4 %collective-permute-start.5 = (f32[3,8,256]{2,1,0:T(8,128)S(1)}, f32[3,8,256]{2,1,0:T(8,128)S(1)}, u32[]{:S(2)}, u32[]{:S(2)}) collective-permute-start(f32[3,8,256]{2,1,0:T(8,128)S(1)} %add.31.top_a), channel_id=1, source_target_pairs={{0,24},{4,28},{8,16},{12,20},{16,8},{20,12},{24,0},{28,4},{1,25},{... | collective-permute-start | bytes 73736 | tf_op jit(solution)/shard_map/ppermute | solution.py:388
  78.6 21.2 %collective-permute-start.10 = (f32[1,4,72,256]{3,2,1,0:T(8,128)S(1)}, f32[1,4,72,256]{3,2,1,0:T(8,128)S(1)}, u32[]{:S(2)}, u32[]{:S(2)}) collective-permute-start(f32[1,4,72,256]{3,2,1,0:T(8,128)S(1)} %get-tuple-element.40), channel_id=1, source_target_pairs={{0,1},{1,0},{2,3},{3,2},{4,5},{5,4},{6,7},{7,6},{8,9},{9,8},{10,11... | collective-permute-start | bytes 884744 | tf_op jit(solution)/shard_map/ppermute | solution.py:383
  81.0 18.8 %collective-permute-start.11 = (f32[1,4,72,256]{3,2,1,0:T(8,128)S(1)}, f32[1,4,72,256]{3,2,1,0:T(8,128)S(1)}, u32[]{:S(2)}, u32[]{:S(2)}) collective-permute-start(f32[1,4,72,256]{3,2,1,0:T(8,128)S(1)} %get-tuple-element.41), channel_id=1, source_target_pairs={{0,4},{1,2},{2,1},{3,7},{4,0},{5,6},{6,5},{7,3},{8,12},{9,10},{10,... | collective-permute-start | bytes 884744 | tf_op jit(solution)/shard_map/ppermute | solution.py:383
  81.0 6.8 %collective-permute-start.6 = (f32[4,3,256]{2,1,0:T(4,128)S(1)}, f32[4,3,256]{2,1,0:T(4,128)S(1)}, u32[]{:S(2)}, u32[]{:S(2)}) collective-permute-start(f32[4,3,256]{2,1,0:T(4,128)S(1)} %get-tuple-element.32), channel_id=1, source_target_pairs={{0,1},{1,0},{2,3},{3,2},{4,5},{5,4},{6,7},{7,6},{8,9},{9,8},{10,11... | collective-permute-start | bytes 36872 | tf_op jit(solution)/shard_map/ppermute | solution.py:383
  87.9 1.2 %collective-permute-start.7 = (f32[4,3,256]{2,1,0:T(4,128)S(1)}, f32[4,3,256]{2,1,0:T(4,128)S(1)}, u32[]{:S(2)}, u32[]{:S(2)}) collective-permute-start(f32[4,3,256]{2,1,0:T(4,128)S(1)} %get-tuple-element.33), channel_id=1, source_target_pairs={{0,4},{1,2},{2,1},{3,7},{4,0},{5,6},{6,5},{7,3},{8,12},{9,10},{10,... | collective-permute-start | bytes 36872 | tf_op jit(solution)/shard_map/ppermute | solution.py:383
  95.4 13.2 %collective-permute-start.8 = (f32[1,4,72,256]{3,2,1,0:T(8,128)S(1)}, f32[1,4,72,256]{3,2,1,0:T(8,128)S(1)}, u32[]{:S(2)}, u32[]{:S(2)}) collective-permute-start(f32[1,4,72,256]{3,2,1,0:T(8,128)S(1)} %get-tuple-element.37), channel_id=1, source_target_pairs={{0,1},{1,0},{2,3},{3,2},{4,5},{5,4},{6,7},{7,6},{8,9},{9,8},{10,11... | collective-permute-start | bytes 884744 | tf_op jit(solution)/shard_map/ppermute | solution.py:383
  99.8 8.9 %collective-permute-start.9 = (f32[1,4,72,256]{3,2,1,0:T(8,128)S(1)}, f32[1,4,72,256]{3,2,1,0:T(8,128)S(1)}, u32[]{:S(2)}, u32[]{:S(2)}) collective-permute-start(f32[1,4,72,256]{3,2,1,0:T(8,128)S(1)} %get-tuple-element.38), channel_id=1, source_target_pairs={{0,4},{1,2},{2,1},{3,7},{4,0},{5,6},{6,5},{7,3},{8,12},{9,10},{10,... | collective-permute-start | bytes 884744 | tf_op jit(solution)/shard_map/ppermute | solution.py:383
  103.7 1.4 %collective-permute-start.12 = (f32[4,8,256]{2,1,0:T(8,128)S(1)}, f32[4,8,256]{2,1,0:T(8,128)S(1)}, u32[]{:S(2)}, u32[]{:S(2)}) collective-permute-start(f32[4,8,256]{2,1,0:T(8,128)S(1)} %get-tuple-element.49), channel_id=1, source_target_pairs={{0,4},{4,0},{8,12},{12,8},{16,20},{20,16},{24,28},{28,24},{1,5},{5... | collective-permute-start | bytes 98312 | tf_op jit(solution)/shard_map/ppermute | solution.py:388
  105.1 7.4 %collective-permute-start.13 = (f32[4,8,256]{2,1,0:T(8,128)S(1)}, f32[4,8,256]{2,1,0:T(8,128)S(1)}, u32[]{:S(2)}, u32[]{:S(2)}) collective-permute-start(f32[4,8,256]{2,1,0:T(8,128)S(1)} %add.32.flux_a), channel_id=1, source_target_pairs={{0,8},{4,12},{8,0},{12,4},{16,24},{20,28},{24,16},{28,20},{1,9},{5... | collective-permute-start | bytes 98312 | tf_op jit(solution)/shard_map/ppermute | solution.py:388
  106.6 6.0 %collective-permute-start.14 = (f32[4,8,256]{2,1,0:T(8,128)S(1)}, f32[4,8,256]{2,1,0:T(8,128)S(1)}, u32[]{:S(2)}, u32[]{:S(2)}) collective-permute-start(f32[4,8,256]{2,1,0:T(8,128)S(1)} %add.32.flux_a), channel_id=1, source_target_pairs={{0,16},{4,20},{8,24},{12,28},{16,0},{20,4},{24,8},{28,12},{1,17},{... | collective-permute-start | bytes 98312 | tf_op jit(solution)/shard_map/ppermute | solution.py:388
  106.8 5.7 %collective-permute-start.15 = (f32[4,8,256]{2,1,0:T(8,128)S(1)}, f32[4,8,256]{2,1,0:T(8,128)S(1)}, u32[]{:S(2)}, u32[]{:S(2)}) collective-permute-start(f32[4,8,256]{2,1,0:T(8,128)S(1)} %add.32.flux_a), channel_id=1, source_target_pairs={{0,24},{4,28},{8,16},{12,20},{16,8},{20,12},{24,0},{28,4},{1,25},{... | collective-permute-start | bytes 98312 | tf_op jit(solution)/shard_map/ppermute | solution.py:388
where the time goes:
time: 114 us; the launch traced here: 113 us
  Pallas kernels  83.2 us (73%)
  starting transfers between devices  18 us (16%)
  waiting for transfers between devices  10.3 us (9%)
  between operations  1.49 us (1%)
    pallas_call x1, Pallas kernels, shards(): pl.pallas_call(ocean_kernel, name='sea_mixing', out_shape=(state_type, pl...  62.8 us
    ppermute x8, starting transfers between devices, exchange(): lax.ppermute(value, AXES, swap)  9.99 us
    ppermute x8, starting transfers between devices, swapped(): return lax.ppermute(block, 'member', [(i, i ^ k) for i in range(members)])  8.05 us
    ppermute x8, waiting for transfers between devices, exchange(): lax.ppermute(value, AXES, swap)  7.89 us
    pallas_call x1, Pallas kernels, shards(): pl.pallas_call(first_chains_kernel, name='first_chains', out_shape=(state...  6.39 us
    pallas_call x1, Pallas kernels, shards(): pl.pallas_call(interior_kernel, name='interior', out_shape=(state_type, s...  4.38 us
    pallas_call x1, Pallas kernels, shards(): pl.pallas_call(third_chain_kernel, name='third_chain', out_shape=(state_t...  3.83 us
    pallas_call x1, Pallas kernels, shards(): pl.pallas_call(last_chain_kernel, name='last_chain', out_shape=(air_type,...  3.82 us
  transfers between devices with their start and end apart: 16, of which 4 were waited for; matrix products, arithmetic and copies ran while one was open for 0% of the time, Pallas kernels for 72%

commit v1 on v0

v1 whole, which is shorter than its diff:
```python
import functools
import math

import jax
import jax.numpy as jnp
from jax import lax
from jax.experimental import pallas as pl
from jax.experimental.pallas import tpu as pltpu
from jax.sharding import PartitionSpec as P

NSUB = 4
DIFFUSE = 0.2
ADVECT_RATE = 0.15
CORIOLIS_MAX = 0.2
AIR_STEP = 0.05
SEA_STEP = 0.25
SIGNS = (1.0, 1.0, -1.0, -1.0)
FIELDS = 4
LANES = 128

F32 = jnp.float32
BF16 = jnp.bfloat16
AXES = ("member", "tile")
VMEM = pl.BlockSpec(memory_space=pltpu.VMEM)
SMEM = pl.BlockSpec(memory_space=pltpu.SMEM)
ANY = pl.BlockSpec(memory_space=pl.ANY)
VMEM_LIMIT = 12 * 2**20


def ceil_to(count, unit):
    return -(-count // unit) * unit


def split_parts(values):
    high = values.astype(BF16).astype(F32)
    return high, (values - high).astype(BF16).astype(F32)


def mixing_parts(mixing, scale):
    levels = mixing.shape[0]
    rows = lax.broadcasted_iota(jnp.int32, mixing.shape, 0)
    columns = lax.broadcasted_iota(jnp.int32, mixing.shape, 1)
    both = scale * mixing + jnp.where(rows == columns, scale, 0.0)
    extra = ceil_to(levels, 8) - levels
    if extra:
        both = jnp.concatenate([both, jnp.zeros((extra, levels), F32)], axis=0)
    high, low = split_parts(both)
    pad = jnp.zeros((both.shape[0], ceil_to(levels, 16) - levels), F32)
    parts = [high, pad, high, pad, low, pad] if pad.shape[1] else [high, high, low]
    return jnp.concatenate(parts, axis=1).astype(BF16)


def stage(cells, staged, offset, depth):
    count, lon = cells.shape
    if count < 16:
        cells = jnp.concatenate([cells, jnp.zeros((16 - count, lon), F32)], axis=0)
    high = cells.astype(BF16)
    low = (cells - high.astype(F32)).astype(BF16)
    staged[offset : offset + 16] = high
    staged[depth + offset : depth + offset + 16] = low
    staged[2 * depth + offset : 2 * depth + offset + 16] = high


def stage_dynamics(center, outer, inner, sign, coriolis, staged):
    levels, lon = center.shape[1:]
    depth = ceil_to(levels, 16)
    rate = 0.5 * ADVECT_RATE / DIFFUSE
    for offset in range(0, levels, 16):
        part = slice(offset, min(offset + 16, levels))
        cells = [center[f, part] for f in range(FIELDS)]
        east_wind = rate * cells[2]
        north_wind = (rate * sign) * cells[3]
        for f in range(FIELDS):
            outer_row, inner_row = outer[f, part], inner[f, part]
            east = pltpu.roll(cells[f], lon - 1, 1)
            west = pltpu.roll(cells[f], 1, 1)
            total = ((east + west) + (outer_row + inner_row)) + cells[f]
            if f < 2:
                total = total - (east_wind * (east - west) + north_wind * (outer_row - inner_row))
            elif f == 2:
                total = total + coriolis * cells[3]
            else:
                total = total - coriolis * cells[2]
            stage(total, staged.at[f], offset, depth)


def surface_flux(center, surface, place):
    sst, sst_tanh, cur_east, cur_north, rate = [surface[k, place] for k in range(5)]
    east = center[2, 0:1] - cur_east
    north = center[3, 0:1] - cur_north
    factor = rate * jnp.sqrt(1.0 + east * east + north * north)
    return (
        factor * (sst - center[0, 0:1]),
        factor * (sst_tanh - center[1, 0:1]),
        factor * east,
        factor * north,
    )


def tile_state(rows):
    tile = lax.axis_index("tile")
    return lax.rem(tile, 2) == 0, tile * rows


def own_row(north_first, rows, place):
    return jnp.where(north_first, rows - 1 - place, place)


def advance(state, surface, total, weights, staged, turn, valid, updates, count_flux=True):
    places = state.shape[1]
    rows = places - 2 * NSUB
    sign = jnp.where(tile_state(rows)[0], 1.0, -1.0)
    for k, (step, place) in enumerate(updates):
        slot = staged.at[k % staged.shape[0]]
        center, outer, inner = [state.at[step, place + shift] for shift in (0, -1, 1)]
        target = state.at[step + 1, place]
        stage_dynamics(center, outer, inner, sign, turn[place], slot)
        flux = surface_flux(center, surface, place)
        own = NSUB <= place < NSUB + rows
        for f in range(FIELDS):
            mixed = jnp.dot(weights[...], slot[f], preferred_element_type=F32)
            surface_level = mixed[0:1] + (AIR_STEP * SIGNS[f]) * flux[f]
            if own:
                if count_flux:
                    total[place, f] = total[place, f] + flux[f]
                target[f] = mixed
                target[f, 0:1] = surface_level
            else:
                target[f] = valid[place] * mixed
                target[f, 0:1] = valid[place] * surface_level


def pack_kernel(depth, owner, air, sea, first, second, top, sems, top_sems):
    rows = air.shape[2]
    north_first, _ = tile_state(rows)
    copies = []
    for d in range(depth):
        for side, out in enumerate((first, second)):
            row = own_row(north_first, rows, d if side == 0 else rows - 1 - d)
            copies.append(
                pltpu.make_async_copy(air.at[0, :, row], out.at[d], sems.at[2 * d + side])
            )
    tops = [
        pltpu.make_async_copy(sea.at[0, f, 0], top.at[k], top_sems.at[k])
        for k, f in enumerate((0, 2, 3))
    ]
    for copy in tops + copies:
        copy.start()
    for copy in tops:
        copy.wait()

    @pl.when(lax.axis_index("member") != owner[0])
    def _():
        top[...] = jnp.zeros_like(top)

    for copy in copies:
        copy.wait()


def ocean_kernel(scale, owner, coriolis, air, sea, land, air_mixing, sea_mixing, state, weights,
                 base, column, turn, valid, staged, sea_weights, sems, sea_sems):
    rows, lon = air.shape[2], air.shape[4]
    levels = sea.shape[2]
    held, halves = base.shape[2], base.shape[1]
    depth = ceil_to(levels, 16)
    places = rows + 2 * NSUB
    north_first, first_row = tile_state(rows)
    copies = []
    for place in range(rows):
        row = own_row(north_first, rows, place)
        copies.append(
            pltpu.make_async_copy(air.at[0, :, row], state.at[0, NSUB + place], sems.at[place])
        )
    loads = [
        pltpu.make_async_copy(
            sea.at[0, :, :, :, pl.ds(h * LANES, LANES)],
            base.at[:, h, pl.ds(0, levels)],
            sea_sems.at[h],
        )
        for h in range(halves)
    ]
    for copy in loads + copies:
        copy.start()
    weights[...] = mixing_parts(air_mixing[...], 0.5 * DIFFUSE)
    sea_weights[...] = mixing_parts(sea_mixing[...], 0.5)
    total = coriolis.shape[0] - 2 * NSUB
    for place in range(places):
        index = first_row + own_row(north_first, rows, place - NSUB)
        inside = jnp.where((index >= 0) & (index < total), 1.0, 0.0)
        turn[place] = jnp.full((1, lon), coriolis[index + NSUB], F32)
        valid[place] = jnp.full((1, lon), inside, F32)
    owns = lax.axis_index("member") == owner[0]
    factor = jnp.where(owns, 0.5 * scale, 0.0)
    first_column = jnp.broadcast_to(sea_mixing[:, 0:1], (levels, LANES))
    for level in range(levels):
        value = first_column[level : level + 1] + (1.0 if level == 0 else 0.0)
        column[level] = factor * jnp.broadcast_to(value, (rows, LANES))
    if held > levels:
        base[:, :, levels:] = jnp.zeros((FIELDS, halves, held - levels, rows, LANES), F32)
    for load in loads:
        load.wait()

    @pl.when(owns)
    def _():
        flat = base.reshape(FIELDS, halves, held * rows, LANES)

        def body(row, carry):
            own = pl.ds(row, held, stride=rows)
            at_sea = land[pl.ds(row, 1)] == 1
            for f in range(FIELDS):
                cells = jnp.concatenate([flat[f, h, own] for h in range(halves)], axis=1)
                for offset in range(0, held, 16):
                    part = slice(offset, min(offset + 16, held))
                    stage(cells[part], staged.at[f], offset, depth)
                mixed = jnp.dot(sea_weights[...], staged[f], preferred_element_type=F32)
                kept = jnp.where(at_sea, mixed, cells)
                for h in range(halves):
                    flat[f, h, own] = kept[:, h * LANES : (h + 1) * LANES]
            return carry

        lax.fori_loop(0, rows, body, 0)

    for copy in copies:
        copy.wait()


def surface_kernel(top_a, top_b, top_c, top_d, land, transfer, state, surface, first, second):
    rows, lon = land.shape
    levels = state.shape[3]
    last = NSUB + rows - 1
    north_first, _ = tile_state(rows)
    for place in range(rows):
        row = pl.ds(own_row(north_first, rows, place), 1)
        for k, kept in enumerate((0, 2, 3)):
            value = (top_a[k, row] + top_b[k, row]) + (top_c[k, row] + top_d[k, row])
            surface[kept, NSUB + place] = value
        surface[1, NSUB + place] = jnp.tanh(surface[0, NSUB + place])
        surface[4, NSUB + place] = transfer[row] * land[row].astype(F32)
    for side, out in enumerate((first, second)):
        for f in range(FIELDS):
            place = NSUB + 2 if side == 0 else last - 2
            out[f * levels : (f + 1) * levels] = state[0, place, f]
        out[FIELDS * levels :] = jnp.zeros((out.shape[0] - FIELDS * levels, lon), F32)
        for d in range(NSUB - 1):
            place = NSUB + d if side == 0 else last - d
            for k, kept in enumerate((0, 2, 3, 4)):
                at = FIELDS * levels + 4 * d + k
                out[at : at + 1] = surface[kept, place]


def interior_kernel(weights, turn, valid, surface, state_in, state, total, first, second, staged, sems):
    del state_in
    rows = state.shape[1] - 2 * NSUB
    last = NSUB + rows - 1
    copies = [
        pltpu.make_async_copy(state.at[0, NSUB + 3], first, sems.at[0]),
        pltpu.make_async_copy(state.at[0, last - 3], second, sems.at[1]),
    ]
    for copy in copies:
        copy.start()
    total[...] = jnp.zeros_like(total)
    updates = []
    for step in range(NSUB - 1):
        for d in range(step + 1, rows // 2):
            updates += [(step, NSUB + d), (step, last - d)]
    advance(state, surface, total, weights, staged, turn, valid, updates)
    for copy in copies:
        copy.wait()


def take_rows(number, state, valid, row_of):
    places = state.shape[1]
    for side in range(2):
        place = NSUB - number if side == 0 else places - 1 - NSUB + number
        for f in range(FIELDS):
            state[0, place, f] = valid[place] * row_of(side, f)


def chain_step(number, step, state):
    low = NSUB + step + 1 - number
    return [(step, low), (step, state.shape[1] - 1 - low)]


def first_chain_kernel(weights, turn, valid, surface, near, far, state_in, total_in, state, total, staged):
    del state_in, total_in
    for number in (1, 2):
        take_rows(number, state, valid, lambda side, f: (near, far)[side][number - 1, f])
    updates = []
    for step in range(NSUB):
        updates += chain_step(1, step, state)
    advance(state, surface, total, weights, staged, turn, valid, updates)


def flux_chains_kernel(weights, turn, valid, near, far, surface_in, state_in, total_in,
                       surface, state, total, flux, staged):
    del surface_in, state_in, total_in
    places, levels = state.shape[1], state.shape[3]
    rows = places - 2 * NSUB
    arrived = (near, far)
    take_rows(3, state, valid, lambda side, f: arrived[side][f * levels : (f + 1) * levels])
    for side in range(2):
        for d in range(NSUB - 1):
            place = NSUB - 1 - d if side == 0 else places - NSUB + d
            for k, kept in enumerate((0, 2, 3, 4)):
                at = FIELDS * levels + 4 * d + k
                surface[kept, place] = arrived[side][at : at + 1]
            surface[1, place] = jnp.tanh(surface[0, place])
    updates = []
    for step in range(NSUB - 1):
        updates += chain_step(2, step, state) + chain_step(3, step, state)
    advance(state, surface, total, weights, staged, turn, valid, updates)
    for place in range(NSUB, NSUB + rows):
        d = min(place - NSUB, NSUB + rows - 1 - place)
        last = surface_flux(state.at[NSUB - 1, place], surface, place) if d < NSUB - 1 else None
        for f in range(FIELDS):
            value = total[place, f] if last is None else total[place, f] + last[f]
            flux[f, place - NSUB : place - NSUB + 1] = value


def last_chain_kernel(weights, turn, valid, surface, near, far, state_in, state, air_next, staged, sems):
    del state_in
    rows = air_next.shape[2]
    north_first, _ = tile_state(rows)
    arrived = (near, far)

    def send(place):
        row = own_row(north_first, rows, place)
        copy = pltpu.make_async_copy(
            state.at[NSUB, NSUB + place], air_next.at[0, :, row], sems.at[place]
        )
        copy.start()
        return copy

    copies = [send(place) for place in (NSUB - 1, rows - NSUB)]
    take_rows(4, state, valid, lambda side, f: arrived[side][f])
    for d in (2, 1):
        updates = chain_step(NSUB - d, NSUB - 1, state) + chain_step(4, 2 - d, state)
        advance(state, surface, None, weights, staged, turn, valid, updates, False)
        copies += [send(place) for place in (d, rows - 1 - d)]
    updates = chain_step(4, 2, state) + chain_step(4, 3, state)
    advance(state, surface, None, weights, staged, turn, valid, updates, False)
    copies += [send(place) for place in (0, rows - 1)]
    for copy in copies:
        copy.wait()


def sea_kernel(base, column, flux_a, flux_b, flux_c, flux_d, land, after, sea_next, result, mean, sems):
    del after
    rows, levels = land.shape[0], column.shape[0]
    north_first, _ = tile_state(rows)
    at_sea = land[...] == 1
    for f in range(FIELDS):
        for place in range(rows):
            part = slice(place, place + 1)
            value = (flux_a[f, part] + flux_b[f, part]) + (flux_c[f, part] + flux_d[f, part])
            mean[f, pl.ds(own_row(north_first, rows, place), 1)] = value
    copies = []
    for f in range(FIELDS):
        forcing = jnp.where(at_sea, mean[f], 0.0)
        for h in range(base.shape[1]):
            part = forcing[:, h * LANES : (h + 1) * LANES]
            for level in range(levels):
                result[f, h, level] = base[f, h, level] + column[level] * part
            place = sea_next.at[0, f, :, :, pl.ds(h * LANES, LANES)]
            copies.append(pltpu.make_async_copy(result.at[f, h], place, sems.at[f, h]))
            copies[-1].start()
    for copy in copies:
        copy.wait()


def pairings(members, tiles):
    both = []
    for side in range(2):
        pairs = []
        for member in range(members):
            for tile in range(tiles):
                other = tile + 1 if (tile + side) % 2 == 0 else tile - 1
                if 0 <= other < tiles:
                    to = member * tiles + other
                else:
                    to = (member ^ 1) * tiles + tile
                pairs.append((member * tiles + tile, to))
        both.append(pairs)
    return both


def params(**more):
    return pltpu.CompilerParams(vmem_limit_bytes=VMEM_LIMIT, **more)


def cost(microseconds):
    return pl.CostEstimate(flops=0, bytes_accessed=int(microseconds * 3.5e6), transcendentals=0)


def exchange(values, swaps):
    return [lax.ppermute(value, AXES, swap) for value, swap in zip(values, swaps)]


def member_parts(values, members):
    def swapped(block, k):
        return lax.ppermute(block, "member", [(i, i ^ k) for i in range(members)])

    k = 1
    while members > 4 * k:
        values = values + swapped(values, k)
        k *= 2
    parts = [values]
    for other in range(k, members, k):
        parts.append(swapped(values, other))
    return parts


def shards(
    atmos_state, ocean_slots, owner_map, land_mask, transfer_coefficient, air_mixing, sea_mixing
):
    members, tiles = lax.axis_size("member"), lax.axis_size("tile")
    _, _, rows, levels, lon = atmos_state.shape
    sea_levels = ocean_slots.shape[3]
    places = rows + 2 * NSUB
    depth, sea_depth = ceil_to(levels, 16), ceil_to(sea_levels, 16)
    swaps = pairings(members, tiles)
    sea_slots = jnp.swapaxes(ocean_slots, 2, 3)

    row_total = rows * tiles
    row_index = jnp.arange(-NSUB, row_total + NSUB)
    latitude = math.pi * ((row_index.astype(F32) + 0.5) / row_total - 0.5)
    coriolis = (CORIOLIS_MAX / DIFFUSE) * jnp.sin(latitude)

    def rows_of(*count):
        return jax.ShapeDtypeStruct((*count, FIELDS, levels, lon), F32)

    halves, held = lon // LANES, ceil_to(sea_levels, 8)
    state_type = pltpu.VMEM((NSUB + 1, places, FIELDS, levels, lon), F32)
    surface_type = pltpu.VMEM((5, places, 1, lon), F32)
    total_type = pltpu.VMEM((places, FIELDS, 1, lon), F32)
    table_type = pltpu.VMEM((places, 1, lon), F32)
    base_type = pltpu.VMEM((FIELDS, halves, held, rows, LANES), F32)
    topped = jax.ShapeDtypeStruct((ceil_to(FIELDS * levels + 4 * (NSUB - 1), 8), lon), F32)
    staged = pltpu.VMEM((2, FIELDS, 3 * depth, lon), BF16)
    atmos_state = pltpu.with_memory_space_constraint(atmos_state, pltpu.HBM)
    sea_slots = pltpu.with_memory_space_constraint(sea_slots, pltpu.HBM)

    near, far, top = pl.pallas_call(
        functools.partial(pack_kernel, 2),
        name="pack_rows",
        cost_estimate=cost(1.3),
        out_shape=(rows_of(2), rows_of(2), pltpu.VMEM((3, rows, lon), F32)),
        in_specs=[SMEM, ANY, ANY],
        out_specs=(ANY, ANY, VMEM),
        scratch_shapes=[
            pltpu.SemaphoreType.DMA((4,)),
            pltpu.SemaphoreType.DMA((3,)),
        ],
        compiler_params=params(),
    )(owner_map, atmos_state, sea_slots)
    arrived = exchange((near, far), swaps)
    top_parts = member_parts(top, members)

    state, weights, base, column, turn, valid = pl.pallas_call(
        functools.partial(ocean_kernel, SEA_STEP / (NSUB * members)),
        name="sea_mixing",
        cost_estimate=cost(3),
        out_shape=(
            state_type,
            pltpu.VMEM((ceil_to(levels, 8), 3 * depth), BF16),
            base_type,
            pltpu.VMEM((sea_levels, rows, LANES), F32),
            table_type,
            table_type,
        ),
        in_specs=[SMEM, SMEM, ANY, ANY, VMEM, VMEM, VMEM],
        out_specs=(VMEM,) * 6,
        scratch_shapes=[
            pltpu.VMEM((FIELDS, 3 * sea_depth, lon), BF16),
            pltpu.VMEM((held, 3 * sea_depth), BF16),
            pltpu.SemaphoreType.DMA((rows,)),
            pltpu.SemaphoreType.DMA((halves,)),
        ],
        compiler_params=params(),
    )(owner_map, coriolis, atmos_state, sea_slots, land_mask, air_mixing, sea_mixing)
    tables = (weights, turn, valid)

    surface, *third_rows = pl.pallas_call(
        surface_kernel,
        name="surface",
        cost_estimate=cost(0.5),
        out_shape=(surface_type, topped, topped),
        in_specs=[VMEM] * 7,
        out_specs=(VMEM,) * 3,
        compiler_params=params(),
    )(*top_parts, land_mask, transfer_coefficient, state)
    arrived_third = exchange(third_rows, swaps)

    state, total, *fourth_rows = pl.pallas_call(
        interior_kernel,
        name="interior",
        cost_estimate=cost(3),
        out_shape=(state_type, total_type, rows_of(), rows_of()),
        in_specs=[VMEM] * 5,
        out_specs=(VMEM, VMEM, ANY, ANY),
        input_output_aliases={4: 0},
        scratch_shapes=[staged, pltpu.SemaphoreType.DMA((2,))],
        compiler_params=params(),
    )(*tables, surface, state)
    arrived_fourth = exchange(fourth_rows, swaps)

    state, total = pl.pallas_call(
        first_chain_kernel,
        name="first_chain",
        cost_estimate=cost(2),
        out_shape=(state_type, total_type),
        in_specs=[VMEM] * 8,
        out_specs=(VMEM, VMEM),
        input_output_aliases={6: 0, 7: 1},
        scratch_shapes=[staged],
        compiler_params=params(),
    )(*tables, surface, *arrived, state, total)

    surface, state, _, flux = pl.pallas_call(
        flux_chains_kernel,
        name="flux_chains",
        cost_estimate=cost(3),
        out_shape=(surface_type, state_type, total_type, pltpu.VMEM((FIELDS, rows, lon), F32)),
        in_specs=[VMEM] * 8,
        out_specs=(VMEM,) * 4,
        input_output_aliases={5: 0, 6: 1, 7: 2},
        scratch_shapes=[staged],
        compiler_params=params(),
    )(*tables, *arrived_third, surface, state, total)
    flux_parts = member_parts(flux, members)

    _, air_next = pl.pallas_call(
        last_chain_kernel,
        name="last_chain",
        cost_estimate=cost(3.5),
        out_shape=(state_type, pltpu.HBM(atmos_state.shape, F32)),
        in_specs=[VMEM] * 7,
        out_specs=(VMEM, ANY),
        input_output_aliases={6: 0},
        scratch_shapes=[staged, pltpu.SemaphoreType.DMA((rows,))],
        compiler_params=params(),
    )(*tables, surface, *arrived_fourth, state)

    after = pltpu.with_memory_space_constraint(air_next, pltpu.HBM)
    sea_next = pl.pallas_call(
        sea_kernel,
        name="sea_step",
        cost_estimate=cost(1.5),
        out_shape=pltpu.HBM(sea_slots.shape, F32),
        in_specs=[VMEM] * 7 + [ANY],
        out_specs=ANY,
        scratch_shapes=[
            pltpu.VMEM((FIELDS, halves, sea_levels, rows, LANES), F32),
            pltpu.VMEM((FIELDS, rows, lon), F32),
            pltpu.SemaphoreType.DMA((FIELDS, halves)),
        ],
        compiler_params=params(),
    )(base, column, *flux_parts, land_mask, after)
    return (air_next, jnp.swapaxes(sea_next, 2, 3))


def solution(mesh):
    placed = (
        P("member", None, "tile", None, None),
        P("member", None, "tile", None, None),
        P("tile"),
        P("tile", None),
        P("tile", None),
        P(),
        P(),
    )
    return jax.shard_map(
        shards,
        mesh=mesh,
        in_specs=placed,
        out_specs=(P("member", None, "tile", None, None), P("member", None, "tile", None, None)),
        check_vma=False,
    )
```

time: 114 us -> 41.6 us (0.36)
  Pallas kernels: 83.2 us -> 18.7 us
  waiting for transfers between devices: 10.3 us -> 5.22 us
  starting transfers between devices: 18 us -> 13 us
  local copies, waits for them, and re-layouts: 0.12 us -> 2.91 us
    pallas_call x7 -> x8, Pallas kernels: 83.2 us -> 18.7 us  [the longest x1 4.26 us: shards(): pl.pallas_call(functools.partial(ocean_kernel, SEA_STEP / (NSUB * members...]
    ppermute x8 -> x6, waiting for transfers between devices: 7.89 us -> 1.58 us  [exchange(): lax.ppermute(value, AXES, swap)]
    ppermute x8 -> x6, starting transfers between devices: 9.99 us -> 5.43 us  [exchange(): lax.ppermute(value, AXES, swap)]
    unnamed x8 -> x10, local copies, waits for them, and re-layouts: 0.02 us -> 2.91 us
    ppermute x8, waiting for transfers between devices: 2.4 us -> 3.64 us  [swapped(): return lax.ppermute(block, 'member', [(i, i ^ k) for i in range(members)])]
  transfers between devices with their start and end apart: 16 -> 14, of which waited for: 4 -> 4; matrix products, arithmetic and copies ran while one was open for 0% -> 0% of each run, Pallas kernels for 72% -> 39%
where the time goes in v1:
time: 41.6 us; the launch traced here: 41.3 us
  Pallas kernels  18.7 us (45%)
  starting transfers between devices  13 us (31%)
  waiting for transfers between devices  5.22 us (13%)
  local copies, waits for them, and re-layouts  2.91 us (7%)
  between operations  1.39 us (3%)
    ppermute x8, starting transfers between devices, swapped(): return lax.ppermute(block, 'member', [(i, i ^ k) for i in range(members)])  7.55 us
    ppermute x6, starting transfers between devices, exchange(): lax.ppermute(value, AXES, swap)  5.43 us
    pallas_call x1, Pallas kernels, shards(): pl.pallas_call(functools.partial(ocean_kernel, SEA_STEP / (NSUB * members...  4.26 us
    pallas_call x1, Pallas kernels, shards(): pl.pallas_call(last_chain_kernel, name='last_chain', cost_estimate=cost(3...  3.76 us
    ppermute x8, waiting for transfers between devices, swapped(): return lax.ppermute(block, 'member', [(i, i ^ k) for i in range(members)])  3.64 us
    pallas_call x1, Pallas kernels, shards(): pl.pallas_call(interior_kernel, name='interior', cost_estimate=cost(3), o...  2.97 us
    pallas_call x1, Pallas kernels, shards(): pl.pallas_call(flux_chains_kernel, name='flux_chains', cost_estimate=cost...  2.94 us
    unnamed x10, local copies, waits for them, and re-layouts  2.91 us
  transfers between devices with their start and end apart: 14, of which 4 were waited for; matrix products, arithmetic and copies ran while one was open for 0% of the time, Pallas kernels for 39%

profile of v1, /device:TPU:0, one launch (start us, length us, event | category | flops | bytes accessed | tf_op | source)
XLA Modules:
  0.0 41.3 jit_solution(6473013931918308448)
XLA Ops:
  1.3 1.3 %pack_rows.1 = (f32[2,4,72,256]{3,2,1,0:T(8,128)S(1)}, f32[2,4,72,256]{3,2,1,0:T(8,128)S(1)}, f32[3,8,256]{2,1,0:T(8,128)S(1)}) custom-call(s32[1]{0:T(128)S(6)} %copy.23.owner, f32[1,4,8,72,256]{4,3,2,1,0:T(8,128)} %air.3, f32[1,4,62,8,256]{4,3,2,1,0:T(8,128)} %bitcast.2), custom_call_target="tpu_custom_call" | custom-call | bytes 4550000 | tf_op jit(solution)/shard_map/pack_rows/pallas_call | solution.py:443
  2.6 3.1 %collective-permute-start.6 = (f32[2,4,72,256]{3,2,1,0:T(8,128)S(1)}, f32[2,4,72,256]{3,2,1,0:T(8,128)S(1)}, u32[]{:S(2)}, u32[]{:S(2)}) collective-permute-start(f32[2,4,72,256]{3,2,1,0:T(8,128)S(1)} %get-tuple-element.32), channel_id=1, source_target_pairs={{0,1},{1,0},{2,3},{3,2},{4,5},{5,4},{6,7},{7,6},{8,9},{9,8},{10,11... | collective-permute-start | bytes 1769480 | tf_op jit(solution)/shard_map/ppermute | solution.py:396
  5.7 0.0 collective-permute-start.7
  5.7 0.5 %collective-permute-start = (f32[3,8,256]{2,1,0:T(8,128)S(1)}, f32[3,8,256]{2,1,0:T(8,128)S(1)}, u32[]{:S(2)}, u32[]{:S(2)}) collective-permute-start(f32[3,8,256]{2,1,0:T(8,128)S(1)} %get-tuple-element.27), channel_id=1, source_target_pairs={{0,4},{4,0},{8,12},{12,8},{16,20},{20,16},{24,28},{28,24},{1,5},{5... | collective-permute-start | bytes 73736 | tf_op jit(solution)/shard_map/ppermute | solution.py:401
  6.2 1.5 %collective-permute-done = f32[3,8,256]{2,1,0:T(8,128)S(1)} collective-permute-done((f32[3,8,256]{2,1,0:T(8,128)S(1)}, f32[3,8,256]{2,1,0:T(8,128)S(1)}, u32[]{:S(2)}, u32[]{:S(2)}) %collective-permute-start) | collective-permute-done | bytes 24608 | tf_op jit(solution)/shard_map/ppermute | solution.py:401
  7.8 1.5 %collective-permute-start.1 = (f32[3,8,256]{2,1,0:T(8,128)S(1)}, f32[3,8,256]{2,1,0:T(8,128)S(1)}, u32[]{:S(2)}, u32[]{:S(2)}) collective-permute-start(f32[3,8,256]{2,1,0:T(8,128)S(1)} %add.19.top_a), channel_id=1, source_target_pairs={{0,8},{4,12},{8,0},{12,4},{16,24},{20,28},{24,16},{28,20},{1,9},{5... | collective-permute-start | bytes 73736 | tf_op jit(solution)/shard_map/ppermute | solution.py:401
  9.3 1.5 %collective-permute-start.2 = (f32[3,8,256]{2,1,0:T(8,128)S(1)}, f32[3,8,256]{2,1,0:T(8,128)S(1)}, u32[]{:S(2)}, u32[]{:S(2)}) collective-permute-start(f32[3,8,256]{2,1,0:T(8,128)S(1)} %add.19.top_a), channel_id=1, source_target_pairs={{0,16},{4,20},{8,24},{12,28},{16,0},{20,4},{24,8},{28,12},{1,17},{... | collective-permute-start | bytes 73736 | tf_op jit(solution)/shard_map/ppermute | solution.py:401
  10.8 0.5 %collective-permute-start.3 = (f32[3,8,256]{2,1,0:T(8,128)S(1)}, f32[3,8,256]{2,1,0:T(8,128)S(1)}, u32[]{:S(2)}, u32[]{:S(2)}) collective-permute-start(f32[3,8,256]{2,1,0:T(8,128)S(1)} %add.19.top_a), channel_id=1, source_target_pairs={{0,24},{4,28},{8,16},{12,20},{16,8},{20,12},{24,0},{28,4},{1,25},{... | collective-permute-start | bytes 73736 | tf_op jit(solution)/shard_map/ppermute | solution.py:401
  11.3 0.0 copy-start
  11.3 0.7 %copy-done = s32[8,256]{1,0:T(8,128)S(1)} copy-done((s32[8,256]{1,0:T(8,128)S(1)}, s32[8,256]{1,0:T(8,128)}, u32[]{:S(2)}) %copy-start) | copy-done | bytes 8216
  12.0 0.0 copy-start.2
  12.0 0.8 %copy-done.2 = f32[72,72]{1,0:T(8,128)S(1)} copy-done((f32[72,72]{1,0:T(8,128)S(1)}, f32[72,72]{1,0:T(8,128)}, u32[]{:S(2)}) %copy-start.2) | copy-done | bytes 20760
  12.8 0.0 copy-start.3
  12.8 0.8 %copy-done.3 = f32[62,62]{1,0:T(8,128)S(1)} copy-done((f32[62,62]{1,0:T(8,128)S(1)}, f32[62,62]{1,0:T(8,128)}, u32[]{:S(2)}) %copy-start.3) | copy-done | bytes 15400
  13.5 4.3 %sea_mixing.2 = (f32[5,16,4,72,256]{4,3,2,1,0:T(8,128)S(1)}, bf16[72,240]{1,0:T(8,128)(2,1)S(1)}, f32[4,2,64,8,128]{4,3,2,1,0:T(8,128)S(1)}, f32[62,8,128]{2,1,0...) custom-call(s32[1]{0:T(128)S(6)} %copy.23.owner, f32[40]{0:T(128)S(1)} %multiply_sine_fusion.coriolis, ...), custom_call_target="tpu_custom_call" | custom-call | bytes 10500000 | tf_op jit(solution)/shard_map/sea_mixing/pallas_call | solution.py:459
  17.8 0.0 collective-permute-done.1.top_b
  17.8 0.0 collective-permute-done.2.top_c
  17.8 0.0 collective-permute-done.3.top_d
  17.8 0.0 copy-start.4
  17.8 0.7 %copy-done.4 = f32[8,256]{1,0:T(8,128)S(1)} copy-done((f32[8,256]{1,0:T(8,128)S(1)}, f32[8,256]{1,0:T(8,128)}, u32[]{:S(2)}) %copy-start.4) | copy-done | bytes 8216
  18.5 0.1 surface.1
  18.6 1.0 %collective-permute-start.4 = (f32[304,256]{1,0:T(8,128)S(1)}, f32[304,256]{1,0:T(8,128)S(1)}, u32[]{:S(2)}, u32[]{:S(2)}) collective-permute-start(f32[304,256]{1,0:T(8,128)S(1)} %get-tuple-element.29), channel_id=1, source_target_pairs={{0,1},{1,0},{2,3},{3,2},{4,5},{5,4},{6,7},{7,6},{8,9},{9,8},{10,11... | collective-permute-start | bytes 933896 | tf_op jit(solution)/shard_map/ppermute | solution.py:396
  19.6 0.0 collective-permute-start.5
  19.6 3.0 %interior.1 = (f32[5,16,4,72,256]{4,3,2,1,0:T(8,128)S(1)}, f32[16,4,1,256]{3,2,1,0:T(1,128)S(1)}, f32[4,72,256]{2,1,0:T(8,128)S(1)}, f32[4,72,256]{2,1,0:T(8,128)S(1)}) custom-call(bf16[72,240]{1,0:T(8,128)(2,1)S(1)} %get-tuple-element.24.weights, f32[16,1,256]{2,1,0:T(1,128)S(1)} %get-tuple-element.25.turn, ...), custom_call_target="tpu_custom_call", output_to_operand_aliasing={{0}: (4, {})} | custom-call | bytes 10500000 | tf_op jit(solution)/shard_map/interior/pallas_call | solution.py:494
  22.6 1.4 %collective-permute-start.8 = (f32[4,72,256]{2,1,0:T(8,128)S(1)}, f32[4,72,256]{2,1,0:T(8,128)S(1)}, u32[]{:S(2)}, u32[]{:S(2)}) collective-permute-start(f32[4,72,256]{2,1,0:T(8,128)S(1)} %get-tuple-element.39), channel_id=1, source_target_pairs={{0,1},{1,0},{2,3},{3,2},{4,5},{5,4},{6,7},{7,6},{8,9},{9,8},{10,11... | collective-permute-start | bytes 884744 | tf_op jit(solution)/shard_map/ppermute | solution.py:396
  23.9 0.0 collective-permute-done.6.near
  24.0 0.0 collective-permute-start.9
  24.0 0.0 collective-permute-done.7.far
  24.0 1.9 %first_chain.1 = (f32[5,16,4,72,256]{4,3,2,1,0:T(8,128)S(1)}, f32[16,4,1,256]{3,2,1,0:T(1,128)S(1)}) custom-call(bf16[72,240]{1,0:T(8,128)(2,1)S(1)} %get-tuple-element.24.weights, f32[16,1,256]{2,1,0:T(1,128)S(1)} %get-tuple-element.25.turn, f32[16,1,256]{2,1,0:T(1,128)S(1)} %get-tuple-element.26.valid, ...), custom_call_target="tpu_custom_call", output_to_operand_aliasing={{0}: (6, {}), {1}: (7, {})} | custom-call | bytes 7000000 | tf_op jit(solution)/shard_map/first_chain/pallas_call | solution.py:507
  25.9 1.6 %collective-permute-done.4.near = f32[304,256]{1,0:T(8,128)S(1)} collective-permute-done((f32[304,256]{1,0:T(8,128)S(1)}, f32[304,256]{1,0:T(8,128)S(1)}, u32[]{:S(2)}, u32[]{:S(2)}) %collective-permute-start.4) | collective-permute-done | bytes 311328 | tf_op jit(solution)/shard_map/ppermute | solution.py:396
  27.4 0.0 collective-permute-done.5.far
  27.4 0.0 copy-start.1
  27.4 2.9 %flux_chains.1 = (f32[5,16,1,256]{3,2,1,0:T(1,128)S(1)}, f32[5,16,4,72,256]{4,3,2,1,0:T(8,128)S(1)}, f32[16,4,1,256]{3,2,1,0:T(1,128)S(1)}, f32[4,8,256]{2,1,0:T(8,128)S(1)}) custom-call(bf16[72,240]{1,0:T(8,128)(2,1)S(1)} %get-tuple-element.24.weights, ...), custom_call_target="tpu_custom_call", output_to_operand_aliasing={{0}: (5, {}), {1}: (6, {}), {2}: (7, {})} | custom-call | bytes 10500000 | tf_op jit(solution)/shard_map/flux_chains/pallas_call | solution.py:519
  30.4 0.1 collective-permute-start.10
  30.4 1.2 %collective-permute-done.10 = f32[4,8,256]{2,1,0:T(8,128)S(1)} collective-permute-done((f32[4,8,256]{2,1,0:T(8,128)S(1)}, f32[4,8,256]{2,1,0:T(8,128)S(1)}, u32[]{:S(2)}, u32[]{:S(2)}) %collective-permute-start.10) | collective-permute-done | bytes 32800 | tf_op jit(solution)/shard_map/ppermute | solution.py:401
  31.6 1.5 %collective-permute-start.11 = (f32[4,8,256]{2,1,0:T(8,128)S(1)}, f32[4,8,256]{2,1,0:T(8,128)S(1)}, u32[]{:S(2)}, u32[]{:S(2)}) collective-permute-start(f32[4,8,256]{2,1,0:T(8,128)S(1)} %add.20.flux_a), channel_id=1, source_target_pairs={{0,8},{4,12},{8,0},{12,4},{16,24},{20,28},{24,16},{28,20},{1,9},{5... | collective-permute-start | bytes 98312 | tf_op jit(solution)/shard_map/ppermute | solution.py:401
  33.1 1.9 %collective-permute-start.12 = (f32[4,8,256]{2,1,0:T(8,128)S(1)}, f32[4,8,256]{2,1,0:T(8,128)S(1)}, u32[]{:S(2)}, u32[]{:S(2)}) collective-permute-start(f32[4,8,256]{2,1,0:T(8,128)S(1)} %add.20.flux_a), channel_id=1, source_target_pairs={{0,16},{4,20},{8,24},{12,28},{16,0},{20,4},{24,8},{28,12},{1,17},{... | collective-permute-start | bytes 98312 | tf_op jit(solution)/shard_map/ppermute | solution.py:401
  35.0 0.1 collective-permute-start.13
  35.1 0.0 collective-permute-done.8.near
  35.1 0.0 collective-permute-done.9.far
  35.1 3.8 %last_chain.1 = (f32[5,16,4,72,256]{4,3,2,1,0:T(8,128)S(1)}, f32[1,4,8,72,256]{4,3,2,1,0:T(8,128)}) custom-call(bf16[72,240]{1,0:T(8,128)(2,1)S(1)} %get-tuple-element.24.weights, f32[16,1,256]{2,1,0:T(1,128)S(1)} %get-tuple-element.25.turn, f32[16,1,256]{2,1,0:T(1,128)S(1)} %get-tuple-element.26.valid, ...), custom_call_target="tpu_custom_call", output_to_operand_aliasing={{0}: (6, {})} | custom-call | bytes 12250000 | tf_op jit(solution)/shard_map/last_chain/pallas_call | solution.py:532
  38.9 0.0 collective-permute-done.11.flux_b
  38.9 0.0 collective-permute-done.12.flux_c
  38.9 0.9 %collective-permute-done.13.flux_d = f32[4,8,256]{2,1,0:T(8,128)S(1)} collective-permute-done((f32[4,8,256]{2,1,0:T(8,128)S(1)}, f32[4,8,256]{2,1,0:T(8,128)S(1)}, u32[]{:S(2)}, u32[]{:S(2)}) %collective-permute-start.13) | collective-permute-done | bytes 32800 | tf_op jit(solution)/shard_map/ppermute | solution.py:401
  39.8 0.0 copy-done.1
  39.8 1.4 %sea_step.1 = f32[1,4,62,8,256]{4,3,2,1,0:T(8,128)} custom-call(f32[4,2,64,8,128]{4,3,2,1,0:T(8,128)S(1)} %get-tuple-element.43.base, f32[62,8,128]{2,1,0:T(8,128)S(1)} %get-tuple-element.44.column, f32[4,8,256]{2,1,0:T(8,128)S(1)} %add.20.flux_a, f32[4,8,256]{2,1,0:T(8,128)S(1)} %collective-permute-done.11.flux_b, ...), custom_call_target="tpu_custom_call" | custom-call | bytes 5250000 | tf_op jit(solution)/shard_map/sea_step/pallas_call | solution.py:545
  (3 shorter events, 0.1 us)
Async XLA Ops:
  2.6 21.3 %collective-permute-start.6 = (f32[2,4,72,256]{3,2,1,0:T(8,128)S(1)}, f32[2,4,72,256]{3,2,1,0:T(8,128)S(1)}, u32[]{:S(2)}, u32[]{:S(2)}) collective-permute-start(f32[2,4,72,256]{3,2,1,0:T(8,128)S(1)} %get-tuple-element.32), channel_id=1, source_target_pairs={{0,1},{1,0},{2,3},{3,2},{4,5},{5,4},{6,7},{7,6},{8,9},{9,8},{10,11... | collective-permute-start | bytes 1769480 | tf_op jit(solution)/shard_map/ppermute | solution.py:396
  5.7 18.2 %collective-permute-start.7 = (f32[2,4,72,256]{3,2,1,0:T(8,128)S(1)}, f32[2,4,72,256]{3,2,1,0:T(8,128)S(1)}, u32[]{:S(2)}, u32[]{:S(2)}) collective-permute-start(f32[2,4,72,256]{3,2,1,0:T(8,128)S(1)} %get-tuple-element.33), channel_id=1, source_target_pairs={{0,4},{1,2},{2,1},{3,7},{4,0},{5,6},{6,5},{7,3},{8,12},{9,10},{10,... | collective-permute-start | bytes 1769480 | tf_op jit(solution)/shard_map/ppermute | solution.py:396
  5.7 2.0 %collective-permute-start = (f32[3,8,256]{2,1,0:T(8,128)S(1)}, f32[3,8,256]{2,1,0:T(8,128)S(1)}, u32[]{:S(2)}, u32[]{:S(2)}) collective-permute-start(f32[3,8,256]{2,1,0:T(8,128)S(1)} %get-tuple-element.27), channel_id=1, source_target_pairs={{0,4},{4,0},{8,12},{12,8},{16,20},{20,16},{24,28},{28,24},{1,5},{5... | collective-permute-start | bytes 73736 | tf_op jit(solution)/shard_map/ppermute | solution.py:401
  7.8 10.0 %collective-permute-start.1 = (f32[3,8,256]{2,1,0:T(8,128)S(1)}, f32[3,8,256]{2,1,0:T(8,128)S(1)}, u32[]{:S(2)}, u32[]{:S(2)}) collective-permute-start(f32[3,8,256]{2,1,0:T(8,128)S(1)} %add.19.top_a), channel_id=1, source_target_pairs={{0,8},{4,12},{8,0},{12,4},{16,24},{20,28},{24,16},{28,20},{1,9},{5... | collective-permute-start | bytes 73736 | tf_op jit(solution)/shard_map/ppermute | solution.py:401
  9.3 8.6 %collective-permute-start.2 = (f32[3,8,256]{2,1,0:T(8,128)S(1)}, f32[3,8,256]{2,1,0:T(8,128)S(1)}, u32[]{:S(2)}, u32[]{:S(2)}) collective-permute-start(f32[3,8,256]{2,1,0:T(8,128)S(1)} %add.19.top_a), channel_id=1, source_target_pairs={{0,16},{4,20},{8,24},{12,28},{16,0},{20,4},{24,8},{28,12},{1,17},{... | collective-permute-start | bytes 73736 | tf_op jit(solution)/shard_map/ppermute | solution.py:401
  10.8 7.0 %collective-permute-start.3 = (f32[3,8,256]{2,1,0:T(8,128)S(1)}, f32[3,8,256]{2,1,0:T(8,128)S(1)}, u32[]{:S(2)}, u32[]{:S(2)}) collective-permute-start(f32[3,8,256]{2,1,0:T(8,128)S(1)} %add.19.top_a), channel_id=1, source_target_pairs={{0,24},{4,28},{8,16},{12,20},{16,8},{20,12},{24,0},{28,4},{1,25},{... | collective-permute-start | bytes 73736 | tf_op jit(solution)/shard_map/ppermute | solution.py:401
  11.3 0.7 %copy-start = (s32[8,256]{1,0:T(8,128)S(1)}, s32[8,256]{1,0:T(8,128)}, u32[]{:S(2)}) copy-start(s32[8,256]{1,0:T(8,128)} %land.5) | copy-start | bytes 24580
  12.0 0.8 %copy-start.2 = (f32[72,72]{1,0:T(8,128)S(1)}, f32[72,72]{1,0:T(8,128)}, u32[]{:S(2)}) copy-start(f32[72,72]{1,0:T(8,128)} %air_mixing.1) | copy-start | bytes 62212
  12.8 0.8 %copy-start.3 = (f32[62,62]{1,0:T(8,128)S(1)}, f32[62,62]{1,0:T(8,128)}, u32[]{:S(2)}) copy-start(f32[62,62]{1,0:T(8,128)} %sea_mixing.3) | copy-start | bytes 46132
  17.8 0.7 %copy-start.4 = (f32[8,256]{1,0:T(8,128)S(1)}, f32[8,256]{1,0:T(8,128)}, u32[]{:S(2)}) copy-start(f32[8,256]{1,0:T(8,128)} %transfer.1) | copy-start | bytes 24580
  18.6 8.8 %collective-permute-start.4 = (f32[304,256]{1,0:T(8,128)S(1)}, f32[304,256]{1,0:T(8,128)S(1)}, u32[]{:S(2)}, u32[]{:S(2)}) collective-permute-start(f32[304,256]{1,0:T(8,128)S(1)} %get-tuple-element.29), channel_id=1, source_target_pairs={{0,1},{1,0},{2,3},{3,2},{4,5},{5,4},{6,7},{7,6},{8,9},{9,8},{10,11... | collective-permute-start | bytes 933896 | tf_op jit(solution)/shard_map/ppermute | solution.py:396
  19.6 7.8 %collective-permute-start.5 = (f32[304,256]{1,0:T(8,128)S(1)}, f32[304,256]{1,0:T(8,128)S(1)}, u32[]{:S(2)}, u32[]{:S(2)}) collective-permute-start(f32[304,256]{1,0:T(8,128)S(1)} %get-tuple-element.30), channel_id=1, source_target_pairs={{0,4},{1,2},{2,1},{3,7},{4,0},{5,6},{6,5},{7,3},{8,12},{9,10},{10,... | collective-permute-start | bytes 933896 | tf_op jit(solution)/shard_map/ppermute | solution.py:396
  22.6 12.5 %collective-permute-start.8 = (f32[4,72,256]{2,1,0:T(8,128)S(1)}, f32[4,72,256]{2,1,0:T(8,128)S(1)}, u32[]{:S(2)}, u32[]{:S(2)}) collective-permute-start(f32[4,72,256]{2,1,0:T(8,128)S(1)} %get-tuple-element.39), channel_id=1, source_target_pairs={{0,1},{1,0},{2,3},{3,2},{4,5},{5,4},{6,7},{7,6},{8,9},{9,8},{10,11... | collective-permute-start | bytes 884744 | tf_op jit(solution)/shard_map/ppermute | solution.py:396
  24.0 11.2 %collective-permute-start.9 = (f32[4,72,256]{2,1,0:T(8,128)S(1)}, f32[4,72,256]{2,1,0:T(8,128)S(1)}, u32[]{:S(2)}, u32[]{:S(2)}) collective-permute-start(f32[4,72,256]{2,1,0:T(8,128)S(1)} %get-tuple-element.40), channel_id=1, source_target_pairs={{0,4},{1,2},{2,1},{3,7},{4,0},{5,6},{6,5},{7,3},{8,12},{9,10},{10,... | collective-permute-start | bytes 884744 | tf_op jit(solution)/shard_map/ppermute | solution.py:396
  27.4 12.4 %copy-start.1 = (s32[8,256]{1,0:T(8,128)S(1)}, s32[8,256]{1,0:T(8,128)}, u32[]{:S(2)}) copy-start(s32[8,256]{1,0:T(8,128)} %land.5) | copy-start | bytes 24580
  30.4 1.3 %collective-permute-start.10 = (f32[4,8,256]{2,1,0:T(8,128)S(1)}, f32[4,8,256]{2,1,0:T(8,128)S(1)}, u32[]{:S(2)}, u32[]{:S(2)}) collective-permute-start(f32[4,8,256]{2,1,0:T(8,128)S(1)} %get-tuple-element.45), channel_id=1, source_target_pairs={{0,4},{4,0},{8,12},{12,8},{16,20},{20,16},{24,28},{28,24},{1,5},{5... | collective-permute-start | bytes 98312 | tf_op jit(solution)/shard_map/ppermute | solution.py:401
  31.6 7.3 %collective-permute-start.11 = (f32[4,8,256]{2,1,0:T(8,128)S(1)}, f32[4,8,256]{2,1,0:T(8,128)S(1)}, u32[]{:S(2)}, u32[]{:S(2)}) collective-permute-start(f32[4,8,256]{2,1,0:T(8,128)S(1)} %add.20.flux_a), channel_id=1, source_target_pairs={{0,8},{4,12},{8,0},{12,4},{16,24},{20,28},{24,16},{28,20},{1,9},{5... | collective-permute-start | bytes 98312 | tf_op jit(solution)/shard_map/ppermute | solution.py:401
  33.1 5.8 %collective-permute-start.12 = (f32[4,8,256]{2,1,0:T(8,128)S(1)}, f32[4,8,256]{2,1,0:T(8,128)S(1)}, u32[]{:S(2)}, u32[]{:S(2)}) collective-permute-start(f32[4,8,256]{2,1,0:T(8,128)S(1)} %add.20.flux_a), channel_id=1, source_target_pairs={{0,16},{4,20},{8,24},{12,28},{16,0},{20,4},{24,8},{28,12},{1,17},{... | collective-permute-start | bytes 98312 | tf_op jit(solution)/shard_map/ppermute | solution.py:401
  35.0 4.8 %collective-permute-start.13 = (f32[4,8,256]{2,1,0:T(8,128)S(1)}, f32[4,8,256]{2,1,0:T(8,128)S(1)}, u32[]{:S(2)}, u32[]{:S(2)}) collective-permute-start(f32[4,8,256]{2,1,0:T(8,128)S(1)} %add.20.flux_a), channel_id=1, source_target_pairs={{0,24},{4,28},{8,16},{12,20},{16,8},{20,12},{24,0},{28,4},{1,25},{... | collective-permute-start | bytes 98312 | tf_op jit(solution)/shard_map/ppermute | solution.py:401

commit v2 on v1

v2 whole, which is shorter than its diff:
```python
import functools
import math

import jax
import jax.numpy as jnp
from jax import lax
from jax.experimental import pallas as pl
from jax.experimental.pallas import tpu as pltpu
from jax.sharding import PartitionSpec as P

NSUB = 4
DIFFUSE = 0.2
ADVECT_RATE = 0.15
CORIOLIS_MAX = 0.2
AIR_STEP = 0.05
SEA_STEP = 0.25
SIGNS = (1.0, 1.0, -1.0, -1.0)
FIELDS = 4
LANES = 128
AHEAD = 2
EARLY = 3

F32 = jnp.float32
BF16 = jnp.bfloat16
AXES = ("member", "tile")
VMEM = pl.BlockSpec(memory_space=pltpu.VMEM)
SMEM = pl.BlockSpec(memory_space=pltpu.SMEM)
ANY = pl.BlockSpec(memory_space=pl.ANY)
VMEM_LIMIT = 12 * 2**20


def ceil_to(count, unit):
    return -(-count // unit) * unit


def split_parts(values):
    high = values.astype(BF16).astype(F32)
    return high, (values - high).astype(BF16).astype(F32)


def mixing_parts(mixing, scale):
    levels = mixing.shape[0]
    rows = lax.broadcasted_iota(jnp.int32, mixing.shape, 0)
    columns = lax.broadcasted_iota(jnp.int32, mixing.shape, 1)
    both = scale * mixing + jnp.where(rows == columns, scale, 0.0)
    extra = ceil_to(levels, 8) - levels
    if extra:
        both = jnp.concatenate([both, jnp.zeros((extra, levels), F32)], axis=0)
    high, low = split_parts(both)
    pad = jnp.zeros((both.shape[0], ceil_to(levels, 16) - levels), F32)
    parts = [high, pad, high, pad, low, pad] if pad.shape[1] else [high, high, low]
    return jnp.concatenate(parts, axis=1).astype(BF16)


def stage(cells, staged, offset, depth):
    count, lon = cells.shape
    if count < 16:
        cells = jnp.concatenate([cells, jnp.zeros((16 - count, lon), F32)], axis=0)
    high = cells.astype(BF16)
    low = (cells - high.astype(F32)).astype(BF16)
    staged[offset : offset + 16] = high
    staged[depth + offset : depth + offset + 16] = low
    staged[2 * depth + offset : 2 * depth + offset + 16] = high


def stage_dynamics(center, outer, inner, sign, coriolis, staged):
    levels, lon = center.shape[1:]
    depth = ceil_to(levels, 16)
    rate = 0.5 * ADVECT_RATE / DIFFUSE
    for offset in range(0, levels, 16):
        part = slice(offset, min(offset + 16, levels))
        cells = [center[f, part] for f in range(FIELDS)]
        east_wind = rate * cells[2]
        north_wind = (rate * sign) * cells[3]
        for f in range(FIELDS):
            outer_row, inner_row = outer[f, part], inner[f, part]
            east = pltpu.roll(cells[f], lon - 1, 1)
            west = pltpu.roll(cells[f], 1, 1)
            total = ((east + west) + (outer_row + inner_row)) + cells[f]
            if f < 2:
                total = total - (east_wind * (east - west) + north_wind * (outer_row - inner_row))
            elif f == 2:
                total = total + coriolis * cells[3]
            else:
                total = total - coriolis * cells[2]
            stage(total, staged.at[f], offset, depth)


def surface_flux(center, surface, place):
    sst, sst_tanh, cur_east, cur_north, rate = [surface[k, place] for k in range(5)]
    east = center[2, 0:1] - cur_east
    north = center[3, 0:1] - cur_north
    factor = rate * jnp.sqrt(1.0 + east * east + north * north)
    return (
        factor * (sst - center[0, 0:1]),
        factor * (sst_tanh - center[1, 0:1]),
        factor * east,
        factor * north,
    )


def tile_state(rows):
    tile = lax.axis_index("tile")
    return lax.rem(tile, 2) == 0, tile * rows


def own_row(north_first, rows, place):
    return jnp.where(north_first, rows - 1 - place, place)


def advance(state, surface, total, weights, staged, turn, valid, updates, count_flux=True):
    places = state.shape[1]
    rows = places - 2 * NSUB
    sign = jnp.where(tile_state(rows)[0], 1.0, -1.0)
    for k, (step, place) in enumerate(updates):
        slot = staged.at[k % staged.shape[0]]
        center, outer, inner = [state.at[step, place + shift] for shift in (0, -1, 1)]
        target = state.at[step + 1, place]
        stage_dynamics(center, outer, inner, sign, turn[place], slot)
        flux = surface_flux(center, surface, place)
        own = NSUB <= place < NSUB + rows
        for f in range(FIELDS):
            mixed = jnp.dot(weights[...], slot[f], preferred_element_type=F32)
            surface_level = mixed[0:1] + (AIR_STEP * SIGNS[f]) * flux[f]
            if own:
                if count_flux:
                    total[place, f] = total[place, f] + flux[f]
                target[f] = mixed
                target[f, 0:1] = surface_level
            else:
                target[f] = valid[place] * mixed
                target[f, 0:1] = valid[place] * surface_level


def pack_kernel(air, sea, first, second, top, sems, top_sems):
    rows = air.shape[2]
    north_first, _ = tile_state(rows)
    copies = []
    for d, fields in enumerate((FIELDS, EARLY)):
        for side, out in enumerate((first, second)):
            row = own_row(north_first, rows, d if side == 0 else rows - 1 - d)
            copies.append(
                pltpu.make_async_copy(
                    air.at[0, pl.ds(0, fields), row],
                    out.at[pl.ds(d * FIELDS, fields)],
                    sems.at[2 * d + side],
                )
            )
    tops = [
        pltpu.make_async_copy(sea.at[0, f, 0], top.at[k], top_sems.at[k])
        for k, f in enumerate((0, 2, 3))
    ]
    for copy in copies + tops:
        copy.start()
    for copy in copies + tops:
        copy.wait()


def owner_kernel(owner, top, owned_top):
    owns = lax.axis_index("member") == owner[0]
    owned_top[...] = jnp.where(owns, top[...], 0.0)


def tables_kernel(row_total, scale, owner, air, sea, land_in, transfer, air_mixing_in, sea_mixing_in,
                  state, weights, base, sea_weights, column, turn, valid, rate, land,
                  land_here, transfer_here, air_mixing, sea_mixing, sems, sea_sems, small_sems):
    rows, lon = air.shape[2], air.shape[4]
    levels = sea.shape[2]
    held, halves = base.shape[2], base.shape[1]
    places = rows + 2 * NSUB
    north_first, first_row = tile_state(rows)
    small = [
        pltpu.make_async_copy(source, here, small_sems.at[k])
        for k, (source, here) in enumerate((
            (air_mixing_in, air_mixing), (sea_mixing_in, sea_mixing),
            (land_in, land_here), (transfer, transfer_here),
        ))
    ]
    copies = []
    for place in range(rows):
        row = own_row(north_first, rows, place)
        copies.append(
            pltpu.make_async_copy(air.at[0, :, row], state.at[0, NSUB + place], sems.at[place])
        )
    loads = [
        pltpu.make_async_copy(
            sea.at[0, :, :, :, pl.ds(h * LANES, LANES)],
            base.at[:, h, pl.ds(0, levels)],
            sea_sems.at[h],
        )
        for h in range(halves)
    ]
    for copy in small + copies + loads:
        copy.start()
    if held > levels:
        base[:, :, levels:] = jnp.zeros((FIELDS, halves, held - levels, rows, LANES), F32)
    line = lax.broadcasted_iota(jnp.int32, (places, LANES), 0) - NSUB
    index = first_row + jnp.where(north_first, rows - 1 - line, line)
    latitude = math.pi * ((index.astype(F32) + 0.5) / row_total - 0.5)
    turned = (CORIOLIS_MAX / DIFFUSE) * jnp.sin(latitude)
    inside = jnp.where((index >= 0) & (index < row_total), 1.0, 0.0)
    for place in range(places):
        part = slice(place, place + 1)
        turn[place] = jnp.concatenate([turned[part]] * halves, axis=1)
        valid[place] = jnp.concatenate([inside[part]] * halves, axis=1)
    for copy in small:
        copy.wait()
    weights[...] = mixing_parts(air_mixing[...], 0.5 * DIFFUSE)
    sea_weights[...] = mixing_parts(sea_mixing[...], 0.5)
    factor = jnp.where(lax.axis_index("member") == owner[0], 0.5 * scale, 0.0)
    first_column = jnp.broadcast_to(sea_mixing[:, 0:1], (levels, LANES))
    for level in range(levels):
        value = first_column[level : level + 1] + (1.0 if level == 0 else 0.0)
        column[level] = factor * jnp.broadcast_to(value, (rows, LANES))
    land[...] = land_here[...].astype(F32)
    rate[...] = transfer_here[...] * land[...]
    for copy in copies + loads:
        copy.wait()


def ocean_kernel(owner, land, sea_weights, base_in, after, base, staged):
    del base_in, after
    held, halves, rows = base.shape[2], base.shape[1], base.shape[3]
    depth = staged.shape[1] // 3

    @pl.when(lax.axis_index("member") == owner[0])
    def _():
        flat = base.reshape(FIELDS, halves, held * rows, LANES)

        def body(row, carry):
            own = pl.ds(row, held, stride=rows)
            at_sea = land[pl.ds(row, 1)] == 1.0
            for f in range(FIELDS):
                cells = jnp.concatenate([flat[f, h, own] for h in range(halves)], axis=1)
                for offset in range(0, held, 16):
                    part = slice(offset, min(offset + 16, held))
                    stage(cells[part], staged.at[f], offset, depth)
                mixed = jnp.dot(sea_weights[...], staged[f], preferred_element_type=F32)
                kept = jnp.where(at_sea, mixed, cells)
                for h in range(halves):
                    flat[f, h, own] = kept[:, h * LANES : (h + 1) * LANES]
            return carry

        lax.fori_loop(0, rows, body, 0)


def surface_kernel(top_a, top_b, top_c, top_d, rate, state, surface, first, second):
    levels = state.shape[3]
    rows = rate.shape[0]
    last = NSUB + rows - 1
    north_first, _ = tile_state(rows)
    for place in range(rows):
        row = pl.ds(own_row(north_first, rows, place), 1)
        for k, kept in enumerate((0, 2, 3)):
            value = (top_a[k, row] + top_b[k, row]) + (top_c[k, row] + top_d[k, row])
            surface[kept, NSUB + place] = value
        surface[1, NSUB + place] = jnp.tanh(surface[0, NSUB + place])
        surface[4, NSUB + place] = rate[row]
    for side, out in enumerate((first, second)):
        for f in range(EARLY, FIELDS):
            place = NSUB + 1 if side == 0 else last - 1
            out[(f - EARLY) * levels : (f - EARLY + 1) * levels] = state[0, place, f]
        out[(FIELDS - EARLY) * levels :] = jnp.zeros(
            (out.shape[0] - (FIELDS - EARLY) * levels, out.shape[1]), F32
        )
        for d in range(NSUB - 1):
            place = NSUB + d if side == 0 else last - d
            for k, kept in enumerate((0, 2, 3, 4)):
                at = (FIELDS - EARLY) * levels + 4 * d + k
                out[at : at + 1] = surface[kept, place]


def interior_updates(state, first_d):
    rows = state.shape[1] - 2 * NSUB
    last = NSUB + rows - 1
    updates = []
    for step in range(NSUB - 1):
        for d in range(step + 1, rows // 2):
            updates += [(step, NSUB + d), (step, last - d)]
    return updates[:first_d], updates[first_d:]


def first_interior_kernel(weights, turn, valid, surface, state_in, state, total, first, second, staged, sems):
    del state_in
    last = state.shape[1] - NSUB - 1
    copies = [
        pltpu.make_async_copy(state.at[0, NSUB + 2], first, sems.at[0]),
        pltpu.make_async_copy(state.at[0, last - 2], second, sems.at[1]),
    ]
    for copy in copies:
        copy.start()
    total[...] = jnp.zeros_like(total)
    updates, _ = interior_updates(state, AHEAD)
    advance(state, surface, total, weights, staged, turn, valid, updates)
    for copy in copies:
        copy.wait()


def interior_kernel(weights, turn, valid, surface, near, state_in, total_in, state, total, staged):
    del state_in, total_in
    take_rows(1, state, valid, (lambda f: near[f],))
    _, updates = interior_updates(state, AHEAD)
    advance(state, surface, total, weights, staged, turn, valid, updates)


def take_rows(number, state, valid, row_of, sides=(0, 1)):
    places = state.shape[1]
    for side, row in zip(sides, row_of):
        place = NSUB - number if side == 0 else places - 1 - NSUB + number
        for f in range(FIELDS):
            state[0, place, f] = valid[place] * row(f)


def rows_from(near, far):
    return (lambda f: near[f], lambda f: far[f])


def chain_step(number, step, state):
    low = NSUB + step + 1 - number
    return [(step, low), (step, state.shape[1] - 1 - low)]


def first_chain_kernel(weights, turn, valid, surface, far, state_in, total_in, state, total, staged):
    del state_in, total_in
    take_rows(1, state, valid, (lambda f: far[f],), (1,))
    updates = []
    for step in range(NSUB):
        updates += chain_step(1, step, state)
    advance(state, surface, total, weights, staged, turn, valid, updates)


def second_chain_kernel(weights, turn, valid, near, far, near_rest, far_rest, surface_in, state_in, total_in,
                        surface, state, total, first, second, staged, sems):
    del surface_in, state_in, total_in
    places, levels = state.shape[1], state.shape[3]
    rest = (near_rest, far_rest)
    copies = [
        pltpu.make_async_copy(state.at[0, NSUB + 3], first, sems.at[0]),
        pltpu.make_async_copy(state.at[0, places - NSUB - 4], second, sems.at[1]),
    ]
    for copy in copies:
        copy.start()

    def row_of(side, f):
        if f < EARLY:
            return (near, far)[side][FIELDS + f]
        return rest[side][(f - EARLY) * levels : (f - EARLY + 1) * levels]

    take_rows(2, state, valid, [functools.partial(row_of, side) for side in range(2)])
    for side in range(2):
        for d in range(NSUB - 1):
            place = NSUB - 1 - d if side == 0 else places - NSUB + d
            for k, kept in enumerate((0, 2, 3, 4)):
                at = (FIELDS - EARLY) * levels + 4 * d + k
                surface[kept, place] = rest[side][at : at + 1]
            surface[1, place] = jnp.tanh(surface[0, place])
    updates = []
    for step in range(NSUB - 1):
        updates += chain_step(2, step, state)
    advance(state, surface, total, weights, staged, turn, valid, updates)
    for copy in copies:
        copy.wait()


def third_chain_kernel(weights, turn, valid, surface, near, far, state_in, total_in, state, total, flux, staged):
    del state_in, total_in
    rows = state.shape[1] - 2 * NSUB
    north_first, _ = tile_state(rows)
    take_rows(3, state, valid, rows_from(near, far))
    updates = []
    for step in range(NSUB - 1):
        updates += chain_step(3, step, state)
    advance(state, surface, total, weights, staged, turn, valid, updates)
    for place in range(NSUB, NSUB + rows):
        d = min(place - NSUB, NSUB + rows - 1 - place)
        last = surface_flux(state.at[NSUB - 1, place], surface, place) if d < NSUB - 1 else None
        for f in range(FIELDS):
            value = total[place, f] if last is None else total[place, f] + last[f]
            flux[f, pl.ds(own_row(north_first, rows, place - NSUB), 1)] = value


def finish_kernel(weights, turn, valid, surface, flux_in, state_in, state, flux, staged):
    del state_in
    flux[...] = flux_in[...]
    updates = chain_step(2, NSUB - 1, state) + chain_step(3, NSUB - 1, state)
    advance(state, surface, None, weights, staged, turn, valid, updates, False)


def send_row(state, air_next, place, sem):
    rows = air_next.shape[2]
    row = own_row(tile_state(rows)[0], rows, place)
    copy = pltpu.make_async_copy(state.at[NSUB, NSUB + place], air_next.at[0, :, row], sem)
    copy.start()
    return copy


def last_chain_kernel(weights, turn, valid, surface, near, far, state_in, state, air_next, staged, sems):
    del state_in
    rows = air_next.shape[2]
    copies = [send_row(state, air_next, place, sems.at[place]) for place in range(1, rows - 1)]
    take_rows(4, state, valid, rows_from(near, far))
    updates = []
    for step in range(NSUB):
        updates += chain_step(4, step, state)
    advance(state, surface, None, weights, staged, turn, valid, updates, False)
    for copy in copies:
        copy.wait()


def sea_kernel(base, column, flux_a, flux_b, flux_c, flux_d, state, air_in, sea_next, air_next,
               result, sems, air_sems):
    del air_in
    rows, levels = air_next.shape[2], column.shape[0]
    copies = [
        send_row(state, air_next, place, air_sems.at[k]) for k, place in enumerate((0, rows - 1))
    ]
    for f in range(FIELDS):
        mean = (flux_a[f] + flux_b[f]) + (flux_c[f] + flux_d[f])
        for h in range(base.shape[1]):
            part = mean[:, h * LANES : (h + 1) * LANES]
            for level in range(levels):
                result[f, h, level] = base[f, h, level] + column[level] * part
            place = sea_next.at[0, f, :, :, pl.ds(h * LANES, LANES)]
            copies.append(pltpu.make_async_copy(result.at[f, h], place, sems.at[f, h]))
            copies[-1].start()
    for copy in copies:
        copy.wait()


def pairings(members, tiles):
    both = []
    for side in range(2):
        pairs = []
        for member in range(members):
            for tile in range(tiles):
                other = tile + 1 if (tile + side) % 2 == 0 else tile - 1
                if 0 <= other < tiles:
                    to = member * tiles + other
                else:
                    to = (member ^ 1) * tiles + tile
                pairs.append((member * tiles + tile, to))
        both.append(pairs)
    return both


def params(**more):
    return pltpu.CompilerParams(vmem_limit_bytes=VMEM_LIMIT, **more)


def cost(microseconds):
    return pl.CostEstimate(flops=0, bytes_accessed=int(microseconds * 3.5e6), transcendentals=0)


def exchange(values, swaps):
    return [lax.ppermute(value, AXES, swap) for value, swap in zip(values, swaps)]


def swapped(values, k):
    count = lax.axis_size("member")
    return lax.ppermute(values, "member", [(i, i ^ k) for i in range(count)])


def member_parts(values, then=None):
    k = 1
    while lax.axis_size("member") > 4 * k:
        other = swapped(values, k)
        values = (values if then is None or k > 1 else then()) + other
        k *= 2
    return [values] + [swapped(values, other) for other in range(k, lax.axis_size("member"), k)]


def shards(
    atmos_state, ocean_slots, owner_map, land_mask, transfer_coefficient, air_mixing, sea_mixing
):
    members, tiles = lax.axis_size("member"), lax.axis_size("tile")
    _, _, rows, levels, lon = atmos_state.shape
    sea_levels = ocean_slots.shape[3]
    places = rows + 2 * NSUB
    depth, sea_depth = ceil_to(levels, 16), ceil_to(sea_levels, 16)
    swaps = pairings(members, tiles)
    sea_slots = jnp.swapaxes(ocean_slots, 2, 3)

    def rows_of(*count):
        return jax.ShapeDtypeStruct((*count, FIELDS, levels, lon), F32)

    halves, held = lon // LANES, ceil_to(sea_levels, 8)
    state_type = pltpu.VMEM((NSUB + 1, places, FIELDS, levels, lon), F32)
    surface_type = pltpu.VMEM((5, places, 1, lon), F32)
    total_type = pltpu.VMEM((places, FIELDS, 1, lon), F32)
    table_type = pltpu.VMEM((places, 1, lon), F32)
    base_type = pltpu.VMEM((FIELDS, halves, held, rows, LANES), F32)
    column_type = pltpu.VMEM((sea_levels, rows, LANES), F32)
    sea_weight_type = pltpu.VMEM((held, 3 * sea_depth), BF16)
    cell_type = pltpu.VMEM((rows, lon), F32)
    flux_type = pltpu.VMEM((FIELDS, rows, lon), F32)
    air_type, sea_type = pltpu.HBM(atmos_state.shape, F32), pltpu.HBM(sea_slots.shape, F32)
    topped = pltpu.VMEM((ceil_to((FIELDS - EARLY) * levels + 4 * (NSUB - 1), 8), lon), F32)
    near_type = jax.ShapeDtypeStruct((FIELDS + EARLY, levels, lon), F32)
    staged = pltpu.VMEM((2, FIELDS, 3 * depth, lon), BF16)
    atmos_state, sea_slots, land_cells, transfer, air_square, sea_square = [
        pltpu.with_memory_space_constraint(value, pltpu.HBM)
        for value in (
            atmos_state, sea_slots, land_mask, transfer_coefficient, air_mixing, sea_mixing
        )
    ]

    near, far, top = pl.pallas_call(
        pack_kernel,
        name="pack_rows",
        cost_estimate=cost(1),
        out_shape=(near_type, near_type, pltpu.VMEM((3, rows, lon), F32)),
        in_specs=[ANY, ANY],
        out_specs=(ANY, ANY, VMEM),
        scratch_shapes=[pltpu.SemaphoreType.DMA((4,)), pltpu.SemaphoreType.DMA((3,))],
        compiler_params=params(),
    )(atmos_state, sea_slots)
    top = pl.pallas_call(
        owner_kernel,
        name="owner_surface",
        cost_estimate=cost(0.1),
        out_shape=pltpu.VMEM((3, rows, lon), F32),
        in_specs=[SMEM, VMEM],
        out_specs=VMEM,
        compiler_params=params(),
    )(owner_map, top)
    arrived = exchange((near, far), swaps)
    top_parts = member_parts(top)

    state, weights, base, sea_weights, column, turn, valid, rate, land = pl.pallas_call(
        functools.partial(tables_kernel, rows * tiles, SEA_STEP / (NSUB * members)),
        name="tables",
        cost_estimate=cost(2),
        out_shape=(
            state_type,
            pltpu.VMEM((ceil_to(levels, 8), 3 * depth), BF16),
            base_type,
            sea_weight_type,
            column_type,
            table_type,
            table_type,
            cell_type,
            cell_type,
        ),
        in_specs=[SMEM] + [ANY] * 6,
        out_specs=(VMEM,) * 9,
        scratch_shapes=[
            pltpu.VMEM((rows, lon), jnp.int32),
            pltpu.VMEM((rows, lon), F32),
            pltpu.VMEM(air_mixing.shape, F32),
            pltpu.VMEM(sea_mixing.shape, F32),
            pltpu.SemaphoreType.DMA((rows,)),
            pltpu.SemaphoreType.DMA((halves,)),
            pltpu.SemaphoreType.DMA((4,)),
        ],
        compiler_params=params(),
    )(owner_map, atmos_state, sea_slots, land_cells, transfer, air_square, sea_square)
    tables = (weights, turn, valid)

    surface, *rest_rows = pl.pallas_call(
        surface_kernel,
        name="surface",
        cost_estimate=cost(0.3),
        out_shape=(surface_type, topped, topped),
        in_specs=[VMEM] * 6,
        out_specs=(VMEM,) * 3,
        compiler_params=params(),
    )(*top_parts, rate, state)
    arrived_rest = exchange(rest_rows, swaps)

    state, total, *third_rows = pl.pallas_call(
        first_interior_kernel,
        name="first_interior",
        cost_estimate=cost(0.5),
        out_shape=(state_type, total_type, rows_of(), rows_of()),
        in_specs=[VMEM] * 5,
        out_specs=(VMEM, VMEM, ANY, ANY),
        input_output_aliases={4: 0},
        scratch_shapes=[staged, pltpu.SemaphoreType.DMA((2,))],
        compiler_params=params(),
    )(*tables, surface, state)
    arrived_third = exchange(third_rows, swaps)

    state, total = pl.pallas_call(
        interior_kernel,
        name="interior",
        cost_estimate=cost(2.5),
        out_shape=(state_type, total_type),
        in_specs=[VMEM] * 7,
        out_specs=(VMEM, VMEM),
        input_output_aliases={5: 0, 6: 1},
        scratch_shapes=[staged],
        compiler_params=params(),
    )(*tables, surface, arrived[0], state, total)

    state, total = pl.pallas_call(
        first_chain_kernel,
        name="first_chain",
        cost_estimate=cost(2),
        out_shape=(state_type, total_type),
        in_specs=[VMEM] * 7,
        out_specs=(VMEM, VMEM),
        input_output_aliases={5: 0, 6: 1},
        scratch_shapes=[staged],
        compiler_params=params(),
    )(*tables, surface, arrived[1], state, total)

    base = pl.pallas_call(
        ocean_kernel,
        name="ocean",
        cost_estimate=cost(1.5),
        out_shape=base_type,
        in_specs=[SMEM] + [VMEM] * 4,
        out_specs=VMEM,
        input_output_aliases={3: 0},
        scratch_shapes=[pltpu.VMEM((FIELDS, 3 * sea_depth, lon), BF16)],
        compiler_params=params(),
    )(owner_map, land, sea_weights, base, total)

    surface, state, total, *fourth_rows = pl.pallas_call(
        second_chain_kernel,
        name="second_chain",
        cost_estimate=cost(1.5),
        out_shape=(surface_type, state_type, total_type, rows_of(), rows_of()),
        in_specs=[VMEM] * 10,
        out_specs=(VMEM, VMEM, VMEM, ANY, ANY),
        input_output_aliases={7: 0, 8: 1, 9: 2},
        scratch_shapes=[staged, pltpu.SemaphoreType.DMA((2,))],
        compiler_params=params(),
    )(*tables, *arrived, *arrived_rest, surface, state, total)
    arrived_fourth = exchange(fourth_rows, swaps)

    state, _, flux = pl.pallas_call(
        third_chain_kernel,
        name="third_chain",
        cost_estimate=cost(1.5),
        out_shape=(state_type, total_type, flux_type),
        in_specs=[VMEM] * 8,
        out_specs=(VMEM,) * 3,
        input_output_aliases={6: 0, 7: 1},
        scratch_shapes=[staged],
        compiler_params=params(),
    )(*tables, surface, *arrived_third, state, total)

    def finish():
        nonlocal state
        state, again = pl.pallas_call(
            finish_kernel,
            name="finish",
            cost_estimate=cost(1),
            out_shape=(state_type, flux_type),
            in_specs=[VMEM] * 6,
            out_specs=(VMEM, VMEM),
            input_output_aliases={5: 0},
            scratch_shapes=[staged],
            compiler_params=params(),
        )(*tables, surface, flux, state)
        return again

    flux_parts = member_parts(flux, finish)

    state, air_next = pl.pallas_call(
        last_chain_kernel,
        name="last_chain",
        cost_estimate=cost(2.5),
        out_shape=(state_type, air_type),
        in_specs=[VMEM] * 7,
        out_specs=(VMEM, ANY),
        input_output_aliases={6: 0},
        scratch_shapes=[staged, pltpu.SemaphoreType.DMA((rows,))],
        compiler_params=params(),
    )(*tables, surface, *arrived_fourth, state)

    sea_next, air_next = pl.pallas_call(
        sea_kernel,
        name="sea_step",
        cost_estimate=cost(1.5),
        out_shape=(sea_type, air_type),
        in_specs=[VMEM] * 7 + [ANY],
        out_specs=(ANY, ANY),
        input_output_aliases={7: 1},
        scratch_shapes=[
            pltpu.VMEM((FIELDS, halves, sea_levels, rows, LANES), F32),
            pltpu.SemaphoreType.DMA((FIELDS, halves)),
            pltpu.SemaphoreType.DMA((2,)),
        ],
        compiler_params=params(),
    )(base, column, *flux_parts, state, air_next)
    return (air_next, jnp.swapaxes(sea_next, 2, 3))


def solution(mesh):
    placed = (
        P("member", None, "tile", None, None),
        P("member", None, "tile", None, None),
        P("tile"),
        P("tile", None),
        P("tile", None),
        P(),
        P(),
    )
    return jax.shard_map(
        shards,
        mesh=mesh,
        in_specs=placed,
        out_specs=(P("member", None, "tile", None, None), P("member", None, "tile", None, None)),
        check_vma=False,
    )
```

time: 41.6 us -> 41.4 us (level); the launches traced: 41.3 us -> 41.9 us
  starting transfers between devices: 13 us -> 17 us
  local copies, waits for them, and re-layouts: 2.91 us -> 0 us
  Pallas kernels: 18.7 us -> 16.7 us
  waiting for transfers between devices: 5.22 us -> 6.7 us
    ppermute x6 -> x8, starting transfers between devices: 5.43 us -> 8.48 us  [exchange(): lax.ppermute(value, AXES, swap)]
    unnamed x10 -> x0, local copies, waits for them, and re-layouts: 2.91 us -> none
    pallas_call x6 -> x11, Pallas kernels: 15.4 us -> 13.2 us  [the longest x1 2.47 us: shards(): pl.pallas_call(functools.partial(tables_kernel, rows * tiles, SEA_STEP /...]
    ppermute x8, waiting for transfers between devices: 3.64 us -> 5.49 us  [swapped(): return lax.ppermute(values, 'member', [(i, i ^ k) for i in range(count)])]
    ppermute x8, starting transfers between devices: 7.55 us -> 8.53 us  [swapped(): return lax.ppermute(values, 'member', [(i, i ^ k) for i in range(count)])]
    ppermute x6 -> x8, waiting for transfers between devices: 1.58 us -> 1.22 us  [exchange(): lax.ppermute(value, AXES, swap)]
  transfers between devices with their start and end apart: 14 -> 16, of which waited for: 4 -> 5; matrix products, arithmetic and copies ran while one was open for 0% -> 0% of each run, Pallas kernels for 39% -> 33%
where the time goes in v2:
time: 41.4 us; the launch traced here: 41.9 us
  starting transfers between devices  17 us (41%)
  Pallas kernels  16.7 us (40%)
  waiting for transfers between devices  6.7 us (16%)
  between operations  1.42 us (3%)
    ppermute x8, starting transfers between devices, swapped(): return lax.ppermute(values, 'member', [(i, i ^ k) for i in range(count)])  8.53 us
    ppermute x8, starting transfers between devices, exchange(): lax.ppermute(value, AXES, swap)  8.48 us
    ppermute x8, waiting for transfers between devices, swapped(): return lax.ppermute(values, 'member', [(i, i ^ k) for i in range(count)])  5.49 us
    pallas_call x1, Pallas kernels, shards(): pl.pallas_call(functools.partial(tables_kernel, rows * tiles, SEA_STEP /...  2.47 us
    pallas_call x1, Pallas kernels, shards(): pl.pallas_call(interior_kernel, name='interior', cost_estimate=cost(2.5),...  2.37 us
    pallas_call x1, Pallas kernels, shards(): pl.pallas_call(last_chain_kernel, name='last_chain', cost_estimate=cost(2...  2.05 us
    pallas_call x1, Pallas kernels, shards(): pl.pallas_call(first_chain_kernel, name='first_chain', cost_estimate=cost...  1.89 us
    pallas_call x1, Pallas kernels, shards(): pl.pallas_call(second_chain_kernel, name='second_chain', cost_estimate=co...  1.63 us
  transfers between devices with their start and end apart: 16, of which 5 were waited for; matrix products, arithmetic and copies ran while one was open for 0% of the time, Pallas kernels for 33%

profile of v2, /device:TPU:0, one launch (start us, length us, event | category | flops | bytes accessed | tf_op | source)
XLA Modules:
  0.0 41.9 jit_solution(6256983196587214025)
XLA Ops:
  0.6 1.3 %pack_rows.1 = (f32[7,72,256]{2,1,0:T(8,128)S(1)}, f32[7,72,256]{2,1,0:T(8,128)S(1)}, f32[3,8,256]{2,1,0:T(8,128)S(1)}) custom-call(f32[1,4,8,72,256]{4,3,2,1,0:T(8,128)} %air.3, f32[1,4,62,8,256]{4,3,2,1,0:T(8,128)} %bitcast.2), custom_call_target="tpu_custom_call" | custom-call | bytes 3500000 | tf_op jit(solution)/shard_map/pack_rows/pallas_call | solution.py:507
  1.9 3.1 %collective-permute-start.5 = (f32[7,72,256]{2,1,0:T(8,128)S(1)}, f32[7,72,256]{2,1,0:T(8,128)S(1)}, u32[]{:S(2)}, u32[]{:S(2)}) collective-permute-start(f32[7,72,256]{2,1,0:T(8,128)S(1)} %get-tuple-element.49), channel_id=1, source_target_pairs={{0,1},{1,0},{2,3},{3,2},{4,5},{5,4},{6,7},{7,6},{8,9},{9,8},{10,11... | collective-permute-start | bytes 1548296 | tf_op jit(solution)/shard_map/ppermute | solution.py:455
  5.0 0.0 collective-permute-start.4
  5.7 0.6 %collective-permute-start = (f32[3,8,256]{2,1,0:T(8,128)S(1)}, f32[3,8,256]{2,1,0:T(8,128)S(1)}, u32[]{:S(2)}, u32[]{:S(2)}) collective-permute-start(f32[3,8,256]{2,1,0:T(8,128)S(1)} %owner_surface.1), channel_id=1, source_target_pairs={{0,4},{4,0},{8,12},{12,8},{16,20},{20,16},{24,28},{28,24},{1,5},{5... | collective-permute-start | bytes 73736 | tf_op jit(solution)/shard_map/ppermute | solution.py:460
  6.3 0.8 %collective-permute-done = f32[3,8,256]{2,1,0:T(8,128)S(1)} collective-permute-done((f32[3,8,256]{2,1,0:T(8,128)S(1)}, f32[3,8,256]{2,1,0:T(8,128)S(1)}, u32[]{:S(2)}, u32[]{:S(2)}) %collective-permute-start) | collective-permute-done | bytes 24608 | tf_op jit(solution)/shard_map/ppermute | solution.py:460
  7.1 1.5 %collective-permute-start.1 = (f32[3,8,256]{2,1,0:T(8,128)S(1)}, f32[3,8,256]{2,1,0:T(8,128)S(1)}, u32[]{:S(2)}, u32[]{:S(2)}) collective-permute-start(f32[3,8,256]{2,1,0:T(8,128)S(1)} %add.6.top_a), channel_id=1, source_target_pairs={{0,8},{4,12},{8,0},{12,4},{16,24},{20,28},{24,16},{28,20},{1,9},{5... | collective-permute-start | bytes 73736 | tf_op jit(solution)/shard_map/ppermute | solution.py:460
  8.6 1.5 %collective-permute-start.2 = (f32[3,8,256]{2,1,0:T(8,128)S(1)}, f32[3,8,256]{2,1,0:T(8,128)S(1)}, u32[]{:S(2)}, u32[]{:S(2)}) collective-permute-start(f32[3,8,256]{2,1,0:T(8,128)S(1)} %add.6.top_a), channel_id=1, source_target_pairs={{0,16},{4,20},{8,24},{12,28},{16,0},{20,4},{24,8},{28,12},{1,17},{... | collective-permute-start | bytes 73736 | tf_op jit(solution)/shard_map/ppermute | solution.py:460
  10.1 0.5 %collective-permute-start.3 = (f32[3,8,256]{2,1,0:T(8,128)S(1)}, f32[3,8,256]{2,1,0:T(8,128)S(1)}, u32[]{:S(2)}, u32[]{:S(2)}) collective-permute-start(f32[3,8,256]{2,1,0:T(8,128)S(1)} %add.6.top_a), channel_id=1, source_target_pairs={{0,24},{4,28},{8,16},{12,20},{16,8},{20,12},{24,0},{28,4},{1,25},{... | collective-permute-start | bytes 73736 | tf_op jit(solution)/shard_map/ppermute | solution.py:460
  10.6 2.5 %tables.1 = (f32[5,16,4,72,256]{4,3,2,1,0:T(8,128)S(1)}, bf16[72,240]{1,0:T(8,128)(2,1)S(1)}, f32[4,2,64,8,128]{4,3,2,1,0:T(8,128)S(1)}, bf16[64,192]{1,0:T(8,12...) custom-call(s32[1]{0:T(128)S(6)} %copy.37.owner, ...), custom_call_target="tpu_custom_call" | custom-call | bytes 7000000 | tf_op jit(solution)/shard_map/tables/pallas_call | solution.py:529
  13.1 0.0 collective-permute-done.1.top_b
  13.1 0.0 collective-permute-done.2.top_c
  13.1 1.7 %collective-permute-done.3.top_d = f32[3,8,256]{2,1,0:T(8,128)S(1)} collective-permute-done((f32[3,8,256]{2,1,0:T(8,128)S(1)}, f32[3,8,256]{2,1,0:T(8,128)S(1)}, u32[]{:S(2)}, u32[]{:S(2)}) %collective-permute-start.3) | collective-permute-done | bytes 24608 | tf_op jit(solution)/shard_map/ppermute | solution.py:460
  14.9 0.1 surface.1
  14.9 3.1 %collective-permute-start.6 = (f32[88,256]{1,0:T(8,128)S(1)}, f32[88,256]{1,0:T(8,128)S(1)}, u32[]{:S(2)}, u32[]{:S(2)}) collective-permute-start(f32[88,256]{1,0:T(8,128)S(1)} %get-tuple-element.56), channel_id=1, source_target_pairs={{0,1},{1,0},{2,3},{3,2},{4,5},{5,4},{6,7},{7,6},{8,9},{9,8},{10,11... | collective-permute-start | bytes 270344 | tf_op jit(solution)/shard_map/ppermute | solution.py:455
  18.0 0.0 collective-permute-start.7
  18.0 0.8 %first_interior.1 = (f32[5,16,4,72,256]{4,3,2,1,0:T(8,128)S(1)}, f32[16,4,1,256]{3,2,1,0:T(1,128)S(1)}, f32[4,72,256]{2,1,0:T(8,128)S(1)}, f32[4,72,256]{2,1,0:T(8,128)S(1)}) custom-call(bf16[72,240]{1,0:T(8,128)(2,1)S(1)} %get-tuple-element.41.weights, f32[16,1,256]{2,1,0:T(1,128)S(1)} %get-tuple-element.42.turn, ...), custom_call_target="tpu_custom_call", output_to_operand_aliasing={{0}: (4, {})} | custom-call | bytes 1750000 | tf_op jit(solution)/shard_map/first_interior/pallas_call | solution.py:570
  18.8 0.7 %collective-permute-start.8 = (f32[4,72,256]{2,1,0:T(8,128)S(1)}, f32[4,72,256]{2,1,0:T(8,128)S(1)}, u32[]{:S(2)}, u32[]{:S(2)}) collective-permute-start(f32[4,72,256]{2,1,0:T(8,128)S(1)} %get-tuple-element.60), channel_id=1, source_target_pairs={{0,1},{1,0},{2,3},{3,2},{4,5},{5,4},{6,7},{7,6},{8,9},{9,8},{10,11... | collective-permute-start | bytes 884744 | tf_op jit(solution)/shard_map/ppermute | solution.py:455
  19.4 0.0 collective-permute-done.5.near
  19.4 0.0 collective-permute-start.9
  19.4 2.4 %interior.1 = (f32[5,16,4,72,256]{4,3,2,1,0:T(8,128)S(1)}, f32[16,4,1,256]{3,2,1,0:T(1,128)S(1)}) custom-call(bf16[72,240]{1,0:T(8,128)(2,1)S(1)} %get-tuple-element.41.weights, f32[16,1,256]{2,1,0:T(1,128)S(1)} %get-tuple-element.42.turn, f32[16,1,256]{2,1,0:T(1,128)S(1)} %get-tuple-element.43.valid, ...), custom_call_target="tpu_custom_call", output_to_operand_aliasing={{0}: (5, {}), {1}: (6, {})} | custom-call | bytes 8750000 | tf_op jit(solution)/shard_map/interior/pallas_call | solution.py:583
  21.8 0.0 collective-permute-done.4.far
  21.8 1.9 %first_chain.1 = (f32[5,16,4,72,256]{4,3,2,1,0:T(8,128)S(1)}, f32[16,4,1,256]{3,2,1,0:T(1,128)S(1)}) custom-call(bf16[72,240]{1,0:T(8,128)(2,1)S(1)} %get-tuple-element.41.weights, f32[16,1,256]{2,1,0:T(1,128)S(1)} %get-tuple-element.42.turn, f32[16,1,256]{2,1,0:T(1,128)S(1)} %get-tuple-element.43.valid, ...), custom_call_target="tpu_custom_call", output_to_operand_aliasing={{0}: (5, {}), {1}: (6, {})} | custom-call | bytes 7000000 | tf_op jit(solution)/shard_map/first_chain/pallas_call | solution.py:595
  23.7 0.0 collective-permute-done.6.near_rest
  23.7 0.0 collective-permute-done.7.far_rest
  23.8 1.6 %second_chain.1 = (f32[5,16,1,256]{3,2,1,0:T(1,128)S(1)}, f32[5,16,4,72,256]{4,3,2,1,0:T(8,128)S(1)}, f32[16,4,1,256]{3,2,1,0:T(1,128)S(1)}, f32[4,72,256]{2,1,0:T(8,128)S(1)}, f32[4,72,256]{2,1,0:T(8,128)S(1)}) custom-call(bf16[72,240]{1,0:T(8,128)(2,1)S(1)} %get-tuple-element.41.weights, ...), custom_call_target="tpu_custom_call", output_to_operand_aliasing={{0}: (7, {}), {1}: (8, {}), {2}: (9, {})} | custom-call | bytes 5250000 | tf_op jit(solution)/shard_map/second_chain/pallas_call | solution.py:619
  25.4 1.7 %collective-permute-start.14 = (f32[4,72,256]{2,1,0:T(8,128)S(1)}, f32[4,72,256]{2,1,0:T(8,128)S(1)}, u32[]{:S(2)}, u32[]{:S(2)}) collective-permute-start(f32[4,72,256]{2,1,0:T(8,128)S(1)} %get-tuple-element.67), channel_id=1, source_target_pairs={{0,1},{1,0},{2,3},{3,2},{4,5},{5,4},{6,7},{7,6},{8,9},{9,8},{10,11... | collective-permute-start | bytes 884744 | tf_op jit(solution)/shard_map/ppermute | solution.py:455
  27.0 0.0 collective-permute-start.15
  27.0 1.2 %collective-permute-done.8.near = f32[4,72,256]{2,1,0:T(8,128)S(1)} collective-permute-done((f32[4,72,256]{2,1,0:T(8,128)S(1)}, f32[4,72,256]{2,1,0:T(8,128)S(1)}, u32[]{:S(2)}, u32[]{:S(2)}) %collective-permute-start.8) | collective-permute-done | bytes 294944 | tf_op jit(solution)/shard_map/ppermute | solution.py:455
  28.2 0.0 collective-permute-done.9.far
  28.2 1.5 %third_chain.1 = (f32[5,16,4,72,256]{4,3,2,1,0:T(8,128)S(1)}, f32[16,4,1,256]{3,2,1,0:T(1,128)S(1)}, f32[4,8,256]{2,1,0:T(8,128)S(1)}) custom-call(bf16[72,240]{1,0:T(8,128)(2,1)S(1)} %get-tuple-element.41.weights, f32[16,1,256]{2,1,0:T(1,128)S(1)} %get-tuple-element.42.turn, ...), custom_call_target="tpu_custom_call", output_to_operand_aliasing={{0}: (6, {}), {1}: (7, {})} | custom-call | bytes 5250000 | tf_op jit(solution)/shard_map/third_chain/pallas_call | solution.py:632
  29.8 0.1 collective-permute-start.10
  29.9 1.0 %finish.1 = (f32[5,16,4,72,256]{4,3,2,1,0:T(8,128)S(1)}, f32[4,8,256]{2,1,0:T(8,128)S(1)}) custom-call(bf16[72,240]{1,0:T(8,128)(2,1)S(1)} %get-tuple-element.41.weights, f32[16,1,256]{2,1,0:T(1,128)S(1)} %get-tuple-element.42.turn, f32[16,1,256]{2,1,0:T(1,128)S(1)} %get-tuple-element.43.valid, ...), custom_call_target="tpu_custom_call", output_to_operand_aliasing={{0}: (5, {})} | custom-call | bytes 3500000 | tf_op jit(solution)/shard_map/finish/pallas_call | solution.py:646
  30.9 0.2 collective-permute-done.10
  31.1 0.7 %collective-permute-start.11 = (f32[4,8,256]{2,1,0:T(8,128)S(1)}, f32[4,8,256]{2,1,0:T(8,128)S(1)}, u32[]{:S(2)}, u32[]{:S(2)}) collective-permute-start(f32[4,8,256]{2,1,0:T(8,128)S(1)} %add.7.flux_a), channel_id=1, source_target_pairs={{0,8},{4,12},{8,0},{12,4},{16,24},{20,28},{24,16},{28,20},{1,9},{5... | collective-permute-start | bytes 98312 | tf_op jit(solution)/shard_map/ppermute | solution.py:460
  31.8 3.7 %collective-permute-start.12 = (f32[4,8,256]{2,1,0:T(8,128)S(1)}, f32[4,8,256]{2,1,0:T(8,128)S(1)}, u32[]{:S(2)}, u32[]{:S(2)}) collective-permute-start(f32[4,8,256]{2,1,0:T(8,128)S(1)} %add.7.flux_a), channel_id=1, source_target_pairs={{0,16},{4,20},{8,24},{12,28},{16,0},{20,4},{24,8},{28,12},{1,17},{... | collective-permute-start | bytes 98312 | tf_op jit(solution)/shard_map/ppermute | solution.py:460
  35.5 0.0 collective-permute-start.13
  35.5 0.0 collective-permute-done.14.near
  35.5 0.0 collective-permute-done.15.far
  35.5 2.0 %last_chain.1 = (f32[5,16,4,72,256]{4,3,2,1,0:T(8,128)S(1)}, f32[1,4,8,72,256]{4,3,2,1,0:T(8,128)}) custom-call(bf16[72,240]{1,0:T(8,128)(2,1)S(1)} %get-tuple-element.41.weights, f32[16,1,256]{2,1,0:T(1,128)S(1)} %get-tuple-element.42.turn, f32[16,1,256]{2,1,0:T(1,128)S(1)} %get-tuple-element.43.valid, ...), custom_call_target="tpu_custom_call", output_to_operand_aliasing={{0}: (6, {})} | custom-call | bytes 8750000 | tf_op jit(solution)/shard_map/last_chain/pallas_call | solution.py:661
  37.5 0.0 collective-permute-done.11.flux_b
  37.5 0.0 collective-permute-done.12.flux_c
  37.6 2.7 %collective-permute-done.13.flux_d = f32[4,8,256]{2,1,0:T(8,128)S(1)} collective-permute-done((f32[4,8,256]{2,1,0:T(8,128)S(1)}, f32[4,8,256]{2,1,0:T(8,128)S(1)}, u32[]{:S(2)}, u32[]{:S(2)}) %collective-permute-start.13) | collective-permute-done | bytes 32800 | tf_op jit(solution)/shard_map/ppermute | solution.py:460
  40.3 1.6 %sea_step.1 = (f32[1,4,62,8,256]{4,3,2,1,0:T(8,128)}, f32[1,4,8,72,256]{4,3,2,1,0:T(8,128)}) custom-call(f32[4,2,64,8,128]{4,3,2,1,0:T(8,128)S(1)} %ocean.1.base, f32[62,8,128]{2,1,0:T(8,128)S(1)} %get-tuple-element.55.column, f32[4,8,256]{2,1,0:T(8,128)S(1)} %add.7.flux_a, ...), custom_call_target="tpu_custom_call", output_to_operand_aliasing={{1}: (7, {})} | custom-call | bytes 5250000 | tf_op jit(solution)/shard_map/sea_step/pallas_call | solution.py:673
  (4 shorter events, 0.0 us)
Async XLA Ops:
  1.9 17.5 %collective-permute-start.5 = (f32[7,72,256]{2,1,0:T(8,128)S(1)}, f32[7,72,256]{2,1,0:T(8,128)S(1)}, u32[]{:S(2)}, u32[]{:S(2)}) collective-permute-start(f32[7,72,256]{2,1,0:T(8,128)S(1)} %get-tuple-element.49), channel_id=1, source_target_pairs={{0,1},{1,0},{2,3},{3,2},{4,5},{5,4},{6,7},{7,6},{8,9},{9,8},{10,11... | collective-permute-start | bytes 1548296 | tf_op jit(solution)/shard_map/ppermute | solution.py:455
  5.0 16.8 %collective-permute-start.4 = (f32[7,72,256]{2,1,0:T(8,128)S(1)}, f32[7,72,256]{2,1,0:T(8,128)S(1)}, u32[]{:S(2)}, u32[]{:S(2)}) collective-permute-start(f32[7,72,256]{2,1,0:T(8,128)S(1)} %get-tuple-element.48), channel_id=1, source_target_pairs={{0,4},{1,2},{2,1},{3,7},{4,0},{5,6},{6,5},{7,3},{8,12},{9,10},{10,... | collective-permute-start | bytes 1548296 | tf_op jit(solution)/shard_map/ppermute | solution.py:455
  5.7 1.4 %collective-permute-start = (f32[3,8,256]{2,1,0:T(8,128)S(1)}, f32[3,8,256]{2,1,0:T(8,128)S(1)}, u32[]{:S(2)}, u32[]{:S(2)}) collective-permute-start(f32[3,8,256]{2,1,0:T(8,128)S(1)} %owner_surface.1), channel_id=1, source_target_pairs={{0,4},{4,0},{8,12},{12,8},{16,20},{20,16},{24,28},{28,24},{1,5},{5... | collective-permute-start | bytes 73736 | tf_op jit(solution)/shard_map/ppermute | solution.py:460
  7.1 6.0 %collective-permute-start.1 = (f32[3,8,256]{2,1,0:T(8,128)S(1)}, f32[3,8,256]{2,1,0:T(8,128)S(1)}, u32[]{:S(2)}, u32[]{:S(2)}) collective-permute-start(f32[3,8,256]{2,1,0:T(8,128)S(1)} %add.6.top_a), channel_id=1, source_target_pairs={{0,8},{4,12},{8,0},{12,4},{16,24},{20,28},{24,16},{28,20},{1,9},{5... | collective-permute-start | bytes 73736 | tf_op jit(solution)/shard_map/ppermute | solution.py:460
  8.6 4.5 %collective-permute-start.2 = (f32[3,8,256]{2,1,0:T(8,128)S(1)}, f32[3,8,256]{2,1,0:T(8,128)S(1)}, u32[]{:S(2)}, u32[]{:S(2)}) collective-permute-start(f32[3,8,256]{2,1,0:T(8,128)S(1)} %add.6.top_a), channel_id=1, source_target_pairs={{0,16},{4,20},{8,24},{12,28},{16,0},{20,4},{24,8},{28,12},{1,17},{... | collective-permute-start | bytes 73736 | tf_op jit(solution)/shard_map/ppermute | solution.py:460
  10.1 4.7 %collective-permute-start.3 = (f32[3,8,256]{2,1,0:T(8,128)S(1)}, f32[3,8,256]{2,1,0:T(8,128)S(1)}, u32[]{:S(2)}, u32[]{:S(2)}) collective-permute-start(f32[3,8,256]{2,1,0:T(8,128)S(1)} %add.6.top_a), channel_id=1, source_target_pairs={{0,24},{4,28},{8,16},{12,20},{16,8},{20,12},{24,0},{28,4},{1,25},{... | collective-permute-start | bytes 73736 | tf_op jit(solution)/shard_map/ppermute | solution.py:460
  14.9 8.8 %collective-permute-start.6 = (f32[88,256]{1,0:T(8,128)S(1)}, f32[88,256]{1,0:T(8,128)S(1)}, u32[]{:S(2)}, u32[]{:S(2)}) collective-permute-start(f32[88,256]{1,0:T(8,128)S(1)} %get-tuple-element.56), channel_id=1, source_target_pairs={{0,1},{1,0},{2,3},{3,2},{4,5},{5,4},{6,7},{7,6},{8,9},{9,8},{10,11... | collective-permute-start | bytes 270344 | tf_op jit(solution)/shard_map/ppermute | solution.py:455
  18.0 5.8 %collective-permute-start.7 = (f32[88,256]{1,0:T(8,128)S(1)}, f32[88,256]{1,0:T(8,128)S(1)}, u32[]{:S(2)}, u32[]{:S(2)}) collective-permute-start(f32[88,256]{1,0:T(8,128)S(1)} %get-tuple-element.57), channel_id=1, source_target_pairs={{0,4},{1,2},{2,1},{3,7},{4,0},{5,6},{6,5},{7,3},{8,12},{9,10},{10,... | collective-permute-start | bytes 270344 | tf_op jit(solution)/shard_map/ppermute | solution.py:455
  18.8 9.5 %collective-permute-start.8 = (f32[4,72,256]{2,1,0:T(8,128)S(1)}, f32[4,72,256]{2,1,0:T(8,128)S(1)}, u32[]{:S(2)}, u32[]{:S(2)}) collective-permute-start(f32[4,72,256]{2,1,0:T(8,128)S(1)} %get-tuple-element.60), channel_id=1, source_target_pairs={{0,1},{1,0},{2,3},{3,2},{4,5},{5,4},{6,7},{7,6},{8,9},{9,8},{10,11... | collective-permute-start | bytes 884744 | tf_op jit(solution)/shard_map/ppermute | solution.py:455
  19.4 8.8 %collective-permute-start.9 = (f32[4,72,256]{2,1,0:T(8,128)S(1)}, f32[4,72,256]{2,1,0:T(8,128)S(1)}, u32[]{:S(2)}, u32[]{:S(2)}) collective-permute-start(f32[4,72,256]{2,1,0:T(8,128)S(1)} %get-tuple-element.61), channel_id=1, source_target_pairs={{0,4},{1,2},{2,1},{3,7},{4,0},{5,6},{6,5},{7,3},{8,12},{9,10},{10,... | collective-permute-start | bytes 884744 | tf_op jit(solution)/shard_map/ppermute | solution.py:455
  25.4 10.1 %collective-permute-start.14 = (f32[4,72,256]{2,1,0:T(8,128)S(1)}, f32[4,72,256]{2,1,0:T(8,128)S(1)}, u32[]{:S(2)}, u32[]{:S(2)}) collective-permute-start(f32[4,72,256]{2,1,0:T(8,128)S(1)} %get-tuple-element.67), channel_id=1, source_target_pairs={{0,1},{1,0},{2,3},{3,2},{4,5},{5,4},{6,7},{7,6},{8,9},{9,8},{10,11... | collective-permute-start | bytes 884744 | tf_op jit(solution)/shard_map/ppermute | solution.py:455
  27.0 8.4 %collective-permute-start.15 = (f32[4,72,256]{2,1,0:T(8,128)S(1)}, f32[4,72,256]{2,1,0:T(8,128)S(1)}, u32[]{:S(2)}, u32[]{:S(2)}) collective-permute-start(f32[4,72,256]{2,1,0:T(8,128)S(1)} %get-tuple-element.68), channel_id=1, source_target_pairs={{0,4},{1,2},{2,1},{3,7},{4,0},{5,6},{6,5},{7,3},{8,12},{9,10},{10,... | collective-permute-start | bytes 884744 | tf_op jit(solution)/shard_map/ppermute | solution.py:455
  29.8 1.3 %collective-permute-start.10 = (f32[4,8,256]{2,1,0:T(8,128)S(1)}, f32[4,8,256]{2,1,0:T(8,128)S(1)}, u32[]{:S(2)}, u32[]{:S(2)}) collective-permute-start(f32[4,8,256]{2,1,0:T(8,128)S(1)} %get-tuple-element.64.flux_in), channel_id=1, source_target_pairs={{0,4},{4,0},{8,12},{12,8},{16,20},{20,16},{24,28},{28,24},{1,5},{5... | collective-permute-start | bytes 98312 | tf_op jit(solution)/shard_map/ppermute | solution.py:460
  31.1 6.5 %collective-permute-start.11 = (f32[4,8,256]{2,1,0:T(8,128)S(1)}, f32[4,8,256]{2,1,0:T(8,128)S(1)}, u32[]{:S(2)}, u32[]{:S(2)}) collective-permute-start(f32[4,8,256]{2,1,0:T(8,128)S(1)} %add.7.flux_a), channel_id=1, source_target_pairs={{0,8},{4,12},{8,0},{12,4},{16,24},{20,28},{24,16},{28,20},{1,9},{5... | collective-permute-start | bytes 98312 | tf_op jit(solution)/shard_map/ppermute | solution.py:460
  31.8 5.8 %collective-permute-start.12 = (f32[4,8,256]{2,1,0:T(8,128)S(1)}, f32[4,8,256]{2,1,0:T(8,128)S(1)}, u32[]{:S(2)}, u32[]{:S(2)}) collective-permute-start(f32[4,8,256]{2,1,0:T(8,128)S(1)} %add.7.flux_a), channel_id=1, source_target_pairs={{0,16},{4,20},{8,24},{12,28},{16,0},{20,4},{24,8},{28,12},{1,17},{... | collective-permute-start | bytes 98312 | tf_op jit(solution)/shard_map/ppermute | solution.py:460
  35.5 4.8 %collective-permute-start.13 = (f32[4,8,256]{2,1,0:T(8,128)S(1)}, f32[4,8,256]{2,1,0:T(8,128)S(1)}, u32[]{:S(2)}, u32[]{:S(2)}) collective-permute-start(f32[4,8,256]{2,1,0:T(8,128)S(1)} %add.7.flux_a), channel_id=1, source_target_pairs={{0,24},{4,28},{8,16},{12,20},{16,8},{20,12},{24,0},{28,4},{1,25},{... | collective-permute-start | bytes 98312 | tf_op jit(solution)/shard_map/ppermute | solution.py:460

commit v3 on v2

--- a/solution.py
+++ b/solution.py
@@ -218,30 +218,50 @@
         copy.wait()
 
 
-def ocean_kernel(owner, land, sea_weights, base_in, after, base, staged):
-    del base_in, after
+def ocean_kernel(owner, land, sea_weights, base_in, state, air_in, base, air_next, sea_next, staged,
+                 sems, sea_sems):
+    del base_in, air_in
     held, halves, rows = base.shape[2], base.shape[1], base.shape[3]
     depth = staged.shape[1] // 3
-
-    @pl.when(lax.axis_index("member") == owner[0])
+    levels = sea_next.shape[2]
+    owns = lax.axis_index("member") == owner[0]
+    copies = [send_row(state, air_next, place, sems.at[k]) for k, place in enumerate((0, rows - 1))]
+
+    @pl.when(jnp.logical_not(owns))
+    def _():
+        stores = [
+            pltpu.make_async_copy(
+                base.at[:, h, pl.ds(0, levels)],
+                sea_next.at[0, :, :, :, pl.ds(h * LANES, LANES)],
+                sea_sems.at[h],
+            )
+            for h in range(halves)
+        ]
+        for store in stores:
+            store.start()
+        for store in stores:
+            store.wait()
+
+    @pl.when(owns)
     def _():
         flat = base.reshape(FIELDS, halves, held * rows, LANES)
 
-        def body(row, carry):
+        for row in range(rows):
             own = pl.ds(row, held, stride=rows)
-            at_sea = land[pl.ds(row, 1)] == 1.0
+            at_sea = land[row : row + 1] == 1.0
             for f in range(FIELDS):
+                slot = staged.at[(row * FIELDS + f) % staged.shape[0]]
                 cells = jnp.concatenate([flat[f, h, own] for h in range(halves)], axis=1)
                 for offset in range(0, held, 16):
                     part = slice(offset, min(offset + 16, held))
-                    stage(cells[part], staged.at[f], offset, depth)
-                mixed = jnp.dot(sea_weights[...], staged[f], preferred_element_type=F32)
+                    stage(cells[part], slot, offset, depth)
+                mixed = jnp.dot(sea_weights[...], slot[...], preferred_element_type=F32)
                 kept = jnp.where(at_sea, mixed, cells)
                 for h in range(halves):
                     flat[f, h, own] = kept[:, h * LANES : (h + 1) * LANES]
-            return carry
-
-        lax.fori_loop(0, rows, body, 0)
+
+    for copy in copies:
+        copy.wait()
 
 
 def surface_kernel(top_a, top_b, top_c, top_d, rate, state, surface, first, second):
@@ -407,24 +427,24 @@
         copy.wait()
 
 
-def sea_kernel(base, column, flux_a, flux_b, flux_c, flux_d, state, air_in, sea_next, air_next,
-               result, sems, air_sems):
-    del air_in
-    rows, levels = air_next.shape[2], column.shape[0]
-    copies = [
-        send_row(state, air_next, place, air_sems.at[k]) for k, place in enumerate((0, rows - 1))
-    ]
-    for f in range(FIELDS):
-        mean = (flux_a[f] + flux_b[f]) + (flux_c[f] + flux_d[f])
-        for h in range(base.shape[1]):
-            part = mean[:, h * LANES : (h + 1) * LANES]
-            for level in range(levels):
-                result[f, h, level] = base[f, h, level] + column[level] * part
-            place = sea_next.at[0, f, :, :, pl.ds(h * LANES, LANES)]
-            copies.append(pltpu.make_async_copy(result.at[f, h], place, sems.at[f, h]))
-            copies[-1].start()
-    for copy in copies:
-        copy.wait()
+def sea_kernel(owner, base, column, flux_a, flux_b, flux_c, flux_d, sea_in, sea_next, result, sems):
+    del sea_in
+    levels = column.shape[0]
+
+    @pl.when(lax.axis_index("member") == owner[0])
+    def _():
+        copies = []
+        for f in range(FIELDS):
+            mean = (flux_a[f] + flux_b[f]) + (flux_c[f] + flux_d[f])
+            for h in range(base.shape[1]):
+                part = mean[:, h * LANES : (h + 1) * LANES]
+                for level in range(levels):
+                    result[f, h, level] = base[f, h, level] + column[level] * part
+                place = sea_next.at[0, f, :, :, pl.ds(h * LANES, LANES)]
+                copies.append(pltpu.make_async_copy(result.at[f, h], place, sems.at[f, h]))
+                copies[-1].start()
+        for copy in copies:
+            copy.wait()
 
 
 def pairings(members, tiles):
@@ -466,7 +486,8 @@
         other = swapped(values, k)
         values = (values if then is None or k > 1 else then()) + other
         k *= 2
-    return [values] + [swapped(values, other) for other in range(k, lax.axis_size("member"), k)]
+    others = range(lax.axis_size("member") - k, 0, -k)
+    return [values] + [swapped(values, other) for other in others]
 
 
 def shards(
@@ -604,18 +625,6 @@
         compiler_params=params(),
     )(*tables, surface, arrived[1], state, total)
 
-    base = pl.pallas_call(
-        ocean_kernel,
-        name="ocean",
-        cost_estimate=cost(1.5),
-        out_shape=base_type,
-        in_specs=[SMEM] + [VMEM] * 4,
-        out_specs=VMEM,
-        input_output_aliases={3: 0},
-        scratch_shapes=[pltpu.VMEM((FIELDS, 3 * sea_depth, lon), BF16)],
-        compiler_params=params(),
-    )(owner_map, land, sea_weights, base, total)
-
     surface, state, total, *fourth_rows = pl.pallas_call(
         second_chain_kernel,
         name="second_chain",
@@ -670,21 +679,36 @@
         compiler_params=params(),
     )(*tables, surface, *arrived_fourth, state)
 
-    sea_next, air_next = pl.pallas_call(
+    base, air_next, sea_next = pl.pallas_call(
+        ocean_kernel,
+        name="ocean",
+        cost_estimate=cost(1.5),
+        out_shape=(base_type, air_type, sea_type),
+        in_specs=[SMEM] + [VMEM] * 4 + [ANY],
+        out_specs=(VMEM, ANY, ANY),
+        input_output_aliases={3: 0, 5: 1},
+        scratch_shapes=[
+            pltpu.VMEM((2 * FIELDS, 3 * sea_depth, lon), BF16),
+            pltpu.SemaphoreType.DMA((2,)),
+            pltpu.SemaphoreType.DMA((halves,)),
+        ],
+        compiler_params=params(),
+    )(owner_map, land, sea_weights, base, state, air_next)
+
+    sea_next = pl.pallas_call(
         sea_kernel,
         name="sea_step",
         cost_estimate=cost(1.5),
-        out_shape=(sea_type, air_type),
-        in_specs=[VMEM] * 7 + [ANY],
-        out_specs=(ANY, ANY),
-        input_output_aliases={7: 1},
+        out_shape=sea_type,
+        in_specs=[SMEM] + [VMEM] * 6 + [ANY],
+        out_specs=ANY,
+        input_output_aliases={7: 0},
         scratch_shapes=[
             pltpu.VMEM((FIELDS, halves, sea_levels, rows, LANES), F32),
             pltpu.SemaphoreType.DMA((FIELDS, halves)),
-            pltpu.SemaphoreType.DMA((2,)),
         ],
         compiler_params=params(),
-    )(base, column, *flux_parts, state, air_next)
+    )(owner_map, base, column, *flux_parts, sea_next)
     return (air_next, jnp.swapaxes(sea_next, 2, 3))
 
 

time: 41.4 us -> 38.5 us (0.930)
  waiting for transfers between devices: 6.7 us -> 2.13 us
  Pallas kernels: 16.7 us -> 17.8 us
    ppermute x8, waiting for transfers between devices: 5.49 us -> 1.75 us  [swapped(): return lax.ppermute(values, 'member', [(i, i ^ k) for i in range(count)])]
    pallas_call x1, Pallas kernels: 0.02 us -> 1.24 us  [shards(): pl.pallas_call(ocean_kernel, name='ocean', cost_estimate=cost(1.5), out_s...]
    ppermute x8, starting transfers between devices: 8.48 us -> 9.45 us  [exchange(): lax.ppermute(value, AXES, swap)]
    ppermute x8, waiting for transfers between devices: 1.22 us -> 0.38 us  [exchange(): lax.ppermute(value, AXES, swap)]
    ppermute x8, starting transfers between devices: 8.53 us -> 7.95 us  [swapped(): return lax.ppermute(values, 'member', [(i, i ^ k) for i in range(count)])]
  transfers between devices with their start and end apart: 16 -> 16, of which waited for: 5 -> 6; matrix products, arithmetic and copies ran while one was open for 0% -> 0% of each run, Pallas kernels for 33% -> 39%
where the time goes in v3:
time: 38.5 us; the launch traced here: 38.7 us
  Pallas kernels  17.8 us (46%)
  starting transfers between devices  17.4 us (45%)
  waiting for transfers between devices  2.13 us (6%)
  between operations  1.4 us (4%)
    ppermute x8, starting transfers between devices, exchange(): lax.ppermute(value, AXES, swap)  9.45 us
    ppermute x8, starting transfers between devices, swapped(): return lax.ppermute(values, 'member', [(i, i ^ k) for i in range(count)])  7.95 us
    pallas_call x1, Pallas kernels, shards(): pl.pallas_call(functools.partial(tables_kernel, rows * tiles, SEA_STEP /...  2.47 us
    pallas_call x1, Pallas kernels, shards(): pl.pallas_call(interior_kernel, name='interior', cost_estimate=cost(2.5),...  2.38 us
    pallas_call x1, Pallas kernels, shards(): pl.pallas_call(last_chain_kernel, name='last_chain', cost_estimate=cost(2...  2.06 us
    pallas_call x1, Pallas kernels, shards(): pl.pallas_call(first_chain_kernel, name='first_chain', cost_estimate=cost...  1.89 us
    ppermute x8, waiting for transfers between devices, swapped(): return lax.ppermute(values, 'member', [(i, i ^ k) for i in range(count)])  1.75 us
    pallas_call x1, Pallas kernels, shards(): pl.pallas_call(second_chain_kernel, name='second_chain', cost_estimate=co...  1.64 us
  transfers between devices with their start and end apart: 16, of which 6 were waited for; matrix products, arithmetic and copies ran while one was open for 0% of the time, Pallas kernels for 39%

profile of v3, /device:TPU:0, one launch (start us, length us, event | category | flops | bytes accessed | tf_op | source)
XLA Modules:
  0.0 38.7 jit_solution(11972949869727054634)
XLA Ops:
  0.6 1.3 %pack_rows.1 = (f32[7,72,256]{2,1,0:T(8,128)S(1)}, f32[7,72,256]{2,1,0:T(8,128)S(1)}, f32[3,8,256]{2,1,0:T(8,128)S(1)}) custom-call(f32[1,4,8,72,256]{4,3,2,1,0:T(8,128)} %air.3, f32[1,4,62,8,256]{4,3,2,1,0:T(8,128)} %bitcast.2), custom_call_target="tpu_custom_call" | custom-call | bytes 3500000 | tf_op jit(solution)/shard_map/pack_rows/pallas_call | solution.py:528
  1.9 3.1 %collective-permute-start = (f32[7,72,256]{2,1,0:T(8,128)S(1)}, f32[7,72,256]{2,1,0:T(8,128)S(1)}, u32[]{:S(2)}, u32[]{:S(2)}) collective-permute-start(f32[7,72,256]{2,1,0:T(8,128)S(1)} %get-tuple-element.45), channel_id=1, source_target_pairs={{0,1},{1,0},{2,3},{3,2},{4,5},{5,4},{6,7},{7,6},{8,9},{9,8},{10,11... | collective-permute-start | bytes 1548296 | tf_op jit(solution)/shard_map/ppermute | solution.py:475
  5.0 0.0 collective-permute-start.1
  5.7 0.6 %collective-permute-start.2 = (f32[3,8,256]{2,1,0:T(8,128)S(1)}, f32[3,8,256]{2,1,0:T(8,128)S(1)}, u32[]{:S(2)}, u32[]{:S(2)}) collective-permute-start(f32[3,8,256]{2,1,0:T(8,128)S(1)} %owner_surface.1), channel_id=1, source_target_pairs={{0,4},{4,0},{8,12},{12,8},{16,20},{20,16},{24,28},{28,24},{1,5},{5... | collective-permute-start | bytes 73736 | tf_op jit(solution)/shard_map/ppermute | solution.py:480
  6.3 0.8 %collective-permute-done.2 = f32[3,8,256]{2,1,0:T(8,128)S(1)} collective-permute-done((f32[3,8,256]{2,1,0:T(8,128)S(1)}, f32[3,8,256]{2,1,0:T(8,128)S(1)}, u32[]{:S(2)}, u32[]{:S(2)}) %collective-permute-start.2) | collective-permute-done | bytes 24608 | tf_op jit(solution)/shard_map/ppermute | solution.py:480
  7.1 2.4 %collective-permute-start.3 = (f32[3,8,256]{2,1,0:T(8,128)S(1)}, f32[3,8,256]{2,1,0:T(8,128)S(1)}, u32[]{:S(2)}, u32[]{:S(2)}) collective-permute-start(f32[3,8,256]{2,1,0:T(8,128)S(1)} %add.6.top_a), channel_id=1, source_target_pairs={{0,24},{4,28},{8,16},{12,20},{16,8},{20,12},{24,0},{28,4},{1,25},{... | collective-permute-start | bytes 73736 | tf_op jit(solution)/shard_map/ppermute | solution.py:480
  9.6 0.5 %collective-permute-start.4 = (f32[3,8,256]{2,1,0:T(8,128)S(1)}, f32[3,8,256]{2,1,0:T(8,128)S(1)}, u32[]{:S(2)}, u32[]{:S(2)}) collective-permute-start(f32[3,8,256]{2,1,0:T(8,128)S(1)} %add.6.top_a), channel_id=1, source_target_pairs={{0,16},{4,20},{8,24},{12,28},{16,0},{20,4},{24,8},{28,12},{1,17},{... | collective-permute-start | bytes 73736 | tf_op jit(solution)/shard_map/ppermute | solution.py:480
  10.1 0.5 %collective-permute-start.5 = (f32[3,8,256]{2,1,0:T(8,128)S(1)}, f32[3,8,256]{2,1,0:T(8,128)S(1)}, u32[]{:S(2)}, u32[]{:S(2)}) collective-permute-start(f32[3,8,256]{2,1,0:T(8,128)S(1)} %add.6.top_a), channel_id=1, source_target_pairs={{0,8},{4,12},{8,0},{12,4},{16,24},{20,28},{24,16},{28,20},{1,9},{5... | collective-permute-start | bytes 73736 | tf_op jit(solution)/shard_map/ppermute | solution.py:480
  10.6 2.5 %tables.1 = (f32[5,16,4,72,256]{4,3,2,1,0:T(8,128)S(1)}, bf16[72,240]{1,0:T(8,128)(2,1)S(1)}, f32[4,2,64,8,128]{4,3,2,1,0:T(8,128)S(1)}, bf16[64,192]{1,0:T(8,12...) custom-call(s32[1]{0:T(128)S(6)} %copy.39.owner, ...), custom_call_target="tpu_custom_call" | custom-call | bytes 7000000 | tf_op jit(solution)/shard_map/tables/pallas_call | solution.py:550
  13.1 0.0 collective-permute-done.3.top_b
  13.1 0.3 collective-permute-done.4.top_c
  13.4 0.5 %collective-permute-done.5.top_d = f32[3,8,256]{2,1,0:T(8,128)S(1)} collective-permute-done((f32[3,8,256]{2,1,0:T(8,128)S(1)}, f32[3,8,256]{2,1,0:T(8,128)S(1)}, u32[]{:S(2)}, u32[]{:S(2)}) %collective-permute-start.5) | collective-permute-done | bytes 24608 | tf_op jit(solution)/shard_map/ppermute | solution.py:480
  13.9 0.1 surface.1
  14.0 3.1 %collective-permute-start.6 = (f32[88,256]{1,0:T(8,128)S(1)}, f32[88,256]{1,0:T(8,128)S(1)}, u32[]{:S(2)}, u32[]{:S(2)}) collective-permute-start(f32[88,256]{1,0:T(8,128)S(1)} %get-tuple-element.50), channel_id=1, source_target_pairs={{0,1},{1,0},{2,3},{3,2},{4,5},{5,4},{6,7},{7,6},{8,9},{9,8},{10,11... | collective-permute-start | bytes 270344 | tf_op jit(solution)/shard_map/ppermute | solution.py:475
  17.0 0.0 collective-permute-start.7
  17.0 0.7 %first_interior.1 = (f32[5,16,4,72,256]{4,3,2,1,0:T(8,128)S(1)}, f32[16,4,1,256]{3,2,1,0:T(1,128)S(1)}, f32[4,72,256]{2,1,0:T(8,128)S(1)}, f32[4,72,256]{2,1,0:T(8,128)S(1)}) custom-call(bf16[72,240]{1,0:T(8,128)(2,1)S(1)} %get-tuple-element.42.weights, f32[16,1,256]{2,1,0:T(1,128)S(1)} %get-tuple-element.43.turn, ...), custom_call_target="tpu_custom_call", output_to_operand_aliasing={{0}: (4, {})} | custom-call | bytes 1750000 | tf_op jit(solution)/shard_map/first_interior/pallas_call | solution.py:591
  17.8 0.7 %collective-permute-start.10 = (f32[4,72,256]{2,1,0:T(8,128)S(1)}, f32[4,72,256]{2,1,0:T(8,128)S(1)}, u32[]{:S(2)}, u32[]{:S(2)}) collective-permute-start(f32[4,72,256]{2,1,0:T(8,128)S(1)} %get-tuple-element.62), channel_id=1, source_target_pairs={{0,1},{1,0},{2,3},{3,2},{4,5},{5,4},{6,7},{7,6},{8,9},{9,8},{10,11... | collective-permute-start | bytes 884744 | tf_op jit(solution)/shard_map/ppermute | solution.py:475
  18.5 0.0 collective-permute-done.near
  18.5 0.0 collective-permute-start.11
  18.5 2.4 %interior.1 = (f32[5,16,4,72,256]{4,3,2,1,0:T(8,128)S(1)}, f32[16,4,1,256]{3,2,1,0:T(1,128)S(1)}) custom-call(bf16[72,240]{1,0:T(8,128)(2,1)S(1)} %get-tuple-element.42.weights, f32[16,1,256]{2,1,0:T(1,128)S(1)} %get-tuple-element.43.turn, f32[16,1,256]{2,1,0:T(1,128)S(1)} %get-tuple-element.44.valid, ...), custom_call_target="tpu_custom_call", output_to_operand_aliasing={{0}: (5, {}), {1}: (6, {})} | custom-call | bytes 8750000 | tf_op jit(solution)/shard_map/interior/pallas_call | solution.py:604
  20.9 0.0 collective-permute-done.1.far
  20.9 1.9 %first_chain.1 = (f32[5,16,4,72,256]{4,3,2,1,0:T(8,128)S(1)}, f32[16,4,1,256]{3,2,1,0:T(1,128)S(1)}) custom-call(bf16[72,240]{1,0:T(8,128)(2,1)S(1)} %get-tuple-element.42.weights, f32[16,1,256]{2,1,0:T(1,128)S(1)} %get-tuple-element.43.turn, f32[16,1,256]{2,1,0:T(1,128)S(1)} %get-tuple-element.44.valid, ...), custom_call_target="tpu_custom_call", output_to_operand_aliasing={{0}: (5, {}), {1}: (6, {})} | custom-call | bytes 7000000 | tf_op jit(solution)/shard_map/first_chain/pallas_call | solution.py:616
  22.8 0.0 collective-permute-done.6.near_rest
  22.8 0.0 collective-permute-done.7.far_rest
  22.8 1.6 %second_chain.1 = (f32[5,16,1,256]{3,2,1,0:T(1,128)S(1)}, f32[5,16,4,72,256]{4,3,2,1,0:T(8,128)S(1)}, f32[16,4,1,256]{3,2,1,0:T(1,128)S(1)}, f32[4,72,256]{2,1,0:T(8,128)S(1)}, f32[4,72,256]{2,1,0:T(8,128)S(1)}) custom-call(bf16[72,240]{1,0:T(8,128)(2,1)S(1)} %get-tuple-element.42.weights, ...), custom_call_target="tpu_custom_call", output_to_operand_aliasing={{0}: (7, {}), {1}: (8, {}), {2}: (9, {})} | custom-call | bytes 5250000 | tf_op jit(solution)/shard_map/second_chain/pallas_call | solution.py:628
  24.4 2.6 %collective-permute-start.8 = (f32[4,72,256]{2,1,0:T(8,128)S(1)}, f32[4,72,256]{2,1,0:T(8,128)S(1)}, u32[]{:S(2)}, u32[]{:S(2)}) collective-permute-start(f32[4,72,256]{2,1,0:T(8,128)S(1)} %get-tuple-element.60), channel_id=1, source_target_pairs={{0,1},{1,0},{2,3},{3,2},{4,5},{5,4},{6,7},{7,6},{8,9},{9,8},{10,11... | collective-permute-start | bytes 884744 | tf_op jit(solution)/shard_map/ppermute | solution.py:475
  27.0 0.0 collective-permute-start.9
  27.1 0.2 collective-permute-done.10.near
  27.3 0.0 collective-permute-done.11.far
  27.3 1.5 %third_chain.1 = (f32[5,16,4,72,256]{4,3,2,1,0:T(8,128)S(1)}, f32[16,4,1,256]{3,2,1,0:T(1,128)S(1)}, f32[4,8,256]{2,1,0:T(8,128)S(1)}) custom-call(bf16[72,240]{1,0:T(8,128)(2,1)S(1)} %get-tuple-element.42.weights, f32[16,1,256]{2,1,0:T(1,128)S(1)} %get-tuple-element.43.turn, ...), custom_call_target="tpu_custom_call", output_to_operand_aliasing={{0}: (6, {}), {1}: (7, {})} | custom-call | bytes 5250000 | tf_op jit(solution)/shard_map/third_chain/pallas_call | solution.py:641
  28.8 0.3 collective-permute-start.12
  29.2 1.0 %finish.1 = (f32[5,16,4,72,256]{4,3,2,1,0:T(8,128)S(1)}, f32[4,8,256]{2,1,0:T(8,128)S(1)}) custom-call(bf16[72,240]{1,0:T(8,128)(2,1)S(1)} %get-tuple-element.42.weights, f32[16,1,256]{2,1,0:T(1,128)S(1)} %get-tuple-element.43.turn, f32[16,1,256]{2,1,0:T(1,128)S(1)} %get-tuple-element.44.valid, ...), custom_call_target="tpu_custom_call", output_to_operand_aliasing={{0}: (5, {})} | custom-call | bytes 3500000 | tf_op jit(solution)/shard_map/finish/pallas_call | solution.py:655
  30.2 0.0 collective-permute-done.12
  30.2 2.7 %collective-permute-start.13 = (f32[4,8,256]{2,1,0:T(8,128)S(1)}, f32[4,8,256]{2,1,0:T(8,128)S(1)}, u32[]{:S(2)}, u32[]{:S(2)}) collective-permute-start(f32[4,8,256]{2,1,0:T(8,128)S(1)} %add.7.flux_a), channel_id=1, source_target_pairs={{0,24},{4,28},{8,16},{12,20},{16,8},{20,12},{24,0},{28,4},{1,25},{... | collective-permute-start | bytes 98312 | tf_op jit(solution)/shard_map/ppermute | solution.py:480
  32.9 0.5 %collective-permute-start.14 = (f32[4,8,256]{2,1,0:T(8,128)S(1)}, f32[4,8,256]{2,1,0:T(8,128)S(1)}, u32[]{:S(2)}, u32[]{:S(2)}) collective-permute-start(f32[4,8,256]{2,1,0:T(8,128)S(1)} %add.7.flux_a), channel_id=1, source_target_pairs={{0,16},{4,20},{8,24},{12,28},{16,0},{20,4},{24,8},{28,12},{1,17},{... | collective-permute-start | bytes 98312 | tf_op jit(solution)/shard_map/ppermute | solution.py:480
  33.4 0.4 collective-permute-start.15
  33.8 0.1 collective-permute-done.8.near
  33.9 0.0 collective-permute-done.9.far
  33.9 2.1 %last_chain.1 = (f32[5,16,4,72,256]{4,3,2,1,0:T(8,128)S(1)}, f32[1,4,8,72,256]{4,3,2,1,0:T(8,128)}) custom-call(bf16[72,240]{1,0:T(8,128)(2,1)S(1)} %get-tuple-element.42.weights, f32[16,1,256]{2,1,0:T(1,128)S(1)} %get-tuple-element.43.turn, f32[16,1,256]{2,1,0:T(1,128)S(1)} %get-tuple-element.44.valid, ...), custom_call_target="tpu_custom_call", output_to_operand_aliasing={{0}: (6, {})} | custom-call | bytes 8750000 | tf_op jit(solution)/shard_map/last_chain/pallas_call | solution.py:670
  36.0 1.2 %ocean.1 = (f32[4,2,64,8,128]{4,3,2,1,0:T(8,128)S(1)}, f32[1,4,8,72,256]{4,3,2,1,0:T(8,128)}, f32[1,4,62,8,256]{4,3,2,1,0:T(8,128)}) custom-call(s32[1]{0:T(128)S(6)} %copy.39.owner, f32[8,256]{1,0:T(8,128)S(1)} %get-tuple-element.39.land, bf16[64,192]{1,0:T(8,128)(2,1)S(1)} %get-tuple-element.40.sea_weights, ...), custom_call_target="tpu_custom_call", output_to_operand_aliasing={{0}: (3, {}), {1}: (5, {})} | custom-call | bytes 5250000 | tf_op jit(solution)/shard_map/ocean/pallas_call | solution.py:682
  37.2 0.0 collective-permute-done.13.flux_b
  37.2 0.0 collective-permute-done.14.flux_c
  37.3 0.1 collective-permute-done.15.flux_d
  37.3 1.4 %sea_step.1 = f32[1,4,62,8,256]{4,3,2,1,0:T(8,128)} custom-call(s32[1]{0:T(128)S(6)} %copy.39.owner, f32[4,2,64,8,128]{4,3,2,1,0:T(8,128)S(1)} %get-tuple-element.72.base, f32[62,8,128]{2,1,0:T(8,128)S(1)} %get-tuple-element.73.column, f32[4,8,256]{2,1,0:T(8,128)S(1)} %add.7.flux_a, ...), custom_call_target="tpu_custom_call", output_to_operand_aliasing={{}: (7, {})} | custom-call | bytes 5250000 | tf_op jit(solution)/shard_map/sea_step/pallas_call | solution.py:698
  (3 shorter events, 0.0 us)
Async XLA Ops:
  1.9 16.6 %collective-permute-start = (f32[7,72,256]{2,1,0:T(8,128)S(1)}, f32[7,72,256]{2,1,0:T(8,128)S(1)}, u32[]{:S(2)}, u32[]{:S(2)}) collective-permute-start(f32[7,72,256]{2,1,0:T(8,128)S(1)} %get-tuple-element.45), channel_id=1, source_target_pairs={{0,1},{1,0},{2,3},{3,2},{4,5},{5,4},{6,7},{7,6},{8,9},{9,8},{10,11... | collective-permute-start | bytes 1548296 | tf_op jit(solution)/shard_map/ppermute | solution.py:475
  5.0 15.9 %collective-permute-start.1 = (f32[7,72,256]{2,1,0:T(8,128)S(1)}, f32[7,72,256]{2,1,0:T(8,128)S(1)}, u32[]{:S(2)}, u32[]{:S(2)}) collective-permute-start(f32[7,72,256]{2,1,0:T(8,128)S(1)} %get-tuple-element.46), channel_id=1, source_target_pairs={{0,4},{1,2},{2,1},{3,7},{4,0},{5,6},{6,5},{7,3},{8,12},{9,10},{10,... | collective-permute-start | bytes 1548296 | tf_op jit(solution)/shard_map/ppermute | solution.py:475
  5.7 1.4 %collective-permute-start.2 = (f32[3,8,256]{2,1,0:T(8,128)S(1)}, f32[3,8,256]{2,1,0:T(8,128)S(1)}, u32[]{:S(2)}, u32[]{:S(2)}) collective-permute-start(f32[3,8,256]{2,1,0:T(8,128)S(1)} %owner_surface.1), channel_id=1, source_target_pairs={{0,4},{4,0},{8,12},{12,8},{16,20},{20,16},{24,28},{28,24},{1,5},{5... | collective-permute-start | bytes 73736 | tf_op jit(solution)/shard_map/ppermute | solution.py:480
  7.1 6.0 %collective-permute-start.3 = (f32[3,8,256]{2,1,0:T(8,128)S(1)}, f32[3,8,256]{2,1,0:T(8,128)S(1)}, u32[]{:S(2)}, u32[]{:S(2)}) collective-permute-start(f32[3,8,256]{2,1,0:T(8,128)S(1)} %add.6.top_a), channel_id=1, source_target_pairs={{0,24},{4,28},{8,16},{12,20},{16,8},{20,12},{24,0},{28,4},{1,25},{... | collective-permute-start | bytes 73736 | tf_op jit(solution)/shard_map/ppermute | solution.py:480
  9.6 3.8 %collective-permute-start.4 = (f32[3,8,256]{2,1,0:T(8,128)S(1)}, f32[3,8,256]{2,1,0:T(8,128)S(1)}, u32[]{:S(2)}, u32[]{:S(2)}) collective-permute-start(f32[3,8,256]{2,1,0:T(8,128)S(1)} %add.6.top_a), channel_id=1, source_target_pairs={{0,16},{4,20},{8,24},{12,28},{16,0},{20,4},{24,8},{28,12},{1,17},{... | collective-permute-start | bytes 73736 | tf_op jit(solution)/shard_map/ppermute | solution.py:480
  10.1 3.8 %collective-permute-start.5 = (f32[3,8,256]{2,1,0:T(8,128)S(1)}, f32[3,8,256]{2,1,0:T(8,128)S(1)}, u32[]{:S(2)}, u32[]{:S(2)}) collective-permute-start(f32[3,8,256]{2,1,0:T(8,128)S(1)} %add.6.top_a), channel_id=1, source_target_pairs={{0,8},{4,12},{8,0},{12,4},{16,24},{20,28},{24,16},{28,20},{1,9},{5... | collective-permute-start | bytes 73736 | tf_op jit(solution)/shard_map/ppermute | solution.py:480
  14.0 8.8 %collective-permute-start.6 = (f32[88,256]{1,0:T(8,128)S(1)}, f32[88,256]{1,0:T(8,128)S(1)}, u32[]{:S(2)}, u32[]{:S(2)}) collective-permute-start(f32[88,256]{1,0:T(8,128)S(1)} %get-tuple-element.50), channel_id=1, source_target_pairs={{0,1},{1,0},{2,3},{3,2},{4,5},{5,4},{6,7},{7,6},{8,9},{9,8},{10,11... | collective-permute-start | bytes 270344 | tf_op jit(solution)/shard_map/ppermute | solution.py:475
  17.0 5.7 %collective-permute-start.7 = (f32[88,256]{1,0:T(8,128)S(1)}, f32[88,256]{1,0:T(8,128)S(1)}, u32[]{:S(2)}, u32[]{:S(2)}) collective-permute-start(f32[88,256]{1,0:T(8,128)S(1)} %get-tuple-element.51), channel_id=1, source_target_pairs={{0,4},{1,2},{2,1},{3,7},{4,0},{5,6},{6,5},{7,3},{8,12},{9,10},{10,... | collective-permute-start | bytes 270344 | tf_op jit(solution)/shard_map/ppermute | solution.py:475
  17.8 9.5 %collective-permute-start.10 = (f32[4,72,256]{2,1,0:T(8,128)S(1)}, f32[4,72,256]{2,1,0:T(8,128)S(1)}, u32[]{:S(2)}, u32[]{:S(2)}) collective-permute-start(f32[4,72,256]{2,1,0:T(8,128)S(1)} %get-tuple-element.62), channel_id=1, source_target_pairs={{0,1},{1,0},{2,3},{3,2},{4,5},{5,4},{6,7},{7,6},{8,9},{9,8},{10,11... | collective-permute-start | bytes 884744 | tf_op jit(solution)/shard_map/ppermute | solution.py:475
  18.5 8.8 %collective-permute-start.11 = (f32[4,72,256]{2,1,0:T(8,128)S(1)}, f32[4,72,256]{2,1,0:T(8,128)S(1)}, u32[]{:S(2)}, u32[]{:S(2)}) collective-permute-start(f32[4,72,256]{2,1,0:T(8,128)S(1)} %get-tuple-element.63), channel_id=1, source_target_pairs={{0,4},{1,2},{2,1},{3,7},{4,0},{5,6},{6,5},{7,3},{8,12},{9,10},{10,... | collective-permute-start | bytes 884744 | tf_op jit(solution)/shard_map/ppermute | solution.py:475
  24.4 9.5 %collective-permute-start.8 = (f32[4,72,256]{2,1,0:T(8,128)S(1)}, f32[4,72,256]{2,1,0:T(8,128)S(1)}, u32[]{:S(2)}, u32[]{:S(2)}) collective-permute-start(f32[4,72,256]{2,1,0:T(8,128)S(1)} %get-tuple-element.60), channel_id=1, source_target_pairs={{0,1},{1,0},{2,3},{3,2},{4,5},{5,4},{6,7},{7,6},{8,9},{9,8},{10,11... | collective-permute-start | bytes 884744 | tf_op jit(solution)/shard_map/ppermute | solution.py:475
  27.0 6.9 %collective-permute-start.9 = (f32[4,72,256]{2,1,0:T(8,128)S(1)}, f32[4,72,256]{2,1,0:T(8,128)S(1)}, u32[]{:S(2)}, u32[]{:S(2)}) collective-permute-start(f32[4,72,256]{2,1,0:T(8,128)S(1)} %get-tuple-element.61), channel_id=1, source_target_pairs={{0,4},{1,2},{2,1},{3,7},{4,0},{5,6},{6,5},{7,3},{8,12},{9,10},{10,... | collective-permute-start | bytes 884744 | tf_op jit(solution)/shard_map/ppermute | solution.py:475
  28.8 1.4 %collective-permute-start.12 = (f32[4,8,256]{2,1,0:T(8,128)S(1)}, f32[4,8,256]{2,1,0:T(8,128)S(1)}, u32[]{:S(2)}, u32[]{:S(2)}) collective-permute-start(f32[4,8,256]{2,1,0:T(8,128)S(1)} %get-tuple-element.66.flux_in), channel_id=1, source_target_pairs={{0,4},{4,0},{8,12},{12,8},{16,20},{20,16},{24,28},{28,24},{1,5},{5... | collective-permute-start | bytes 98312 | tf_op jit(solution)/shard_map/ppermute | solution.py:480
  30.2 7.0 %collective-permute-start.13 = (f32[4,8,256]{2,1,0:T(8,128)S(1)}, f32[4,8,256]{2,1,0:T(8,128)S(1)}, u32[]{:S(2)}, u32[]{:S(2)}) collective-permute-start(f32[4,8,256]{2,1,0:T(8,128)S(1)} %add.7.flux_a), channel_id=1, source_target_pairs={{0,24},{4,28},{8,16},{12,20},{16,8},{20,12},{24,0},{28,4},{1,25},{... | collective-permute-start | bytes 98312 | tf_op jit(solution)/shard_map/ppermute | solution.py:480
  32.9 4.3 %collective-permute-start.14 = (f32[4,8,256]{2,1,0:T(8,128)S(1)}, f32[4,8,256]{2,1,0:T(8,128)S(1)}, u32[]{:S(2)}, u32[]{:S(2)}) collective-permute-start(f32[4,8,256]{2,1,0:T(8,128)S(1)} %add.7.flux_a), channel_id=1, source_target_pairs={{0,16},{4,20},{8,24},{12,28},{16,0},{20,4},{24,8},{28,12},{1,17},{... | collective-permute-start | bytes 98312 | tf_op jit(solution)/shard_map/ppermute | solution.py:480
  33.4 3.9 %collective-permute-start.15 = (f32[4,8,256]{2,1,0:T(8,128)S(1)}, f32[4,8,256]{2,1,0:T(8,128)S(1)}, u32[]{:S(2)}, u32[]{:S(2)}) collective-permute-start(f32[4,8,256]{2,1,0:T(8,128)S(1)} %add.7.flux_a), channel_id=1, source_target_pairs={{0,8},{4,12},{8,0},{12,4},{16,24},{20,28},{24,16},{28,20},{1,9},{5... | collective-permute-start | bytes 98312 | tf_op jit(solution)/shard_map/ppermute | solution.py:480

commit v4 on v3

--- a/solution.py
+++ b/solution.py
@@ -17,8 +17,8 @@
 SIGNS = (1.0, 1.0, -1.0, -1.0)
 FIELDS = 4
 LANES = 128
-AHEAD = 2
-EARLY = 3
+AHEAD = 0
+EARLY = (3, 3)
 
 F32 = jnp.float32
 BF16 = jnp.bfloat16
@@ -119,25 +119,23 @@
         stage_dynamics(center, outer, inner, sign, turn[place], slot)
         flux = surface_flux(center, surface, place)
         own = NSUB <= place < NSUB + rows
+        kind = 0 if own else 1 if place < NSUB else 2
         for f in range(FIELDS):
-            mixed = jnp.dot(weights[...], slot[f], preferred_element_type=F32)
-            surface_level = mixed[0:1] + (AIR_STEP * SIGNS[f]) * flux[f]
-            if own:
-                if count_flux:
-                    total[place, f] = total[place, f] + flux[f]
-                target[f] = mixed
-                target[f, 0:1] = surface_level
-            else:
-                target[f] = valid[place] * mixed
-                target[f, 0:1] = valid[place] * surface_level
+            if own and count_flux:
+                total[place, f] = total[place, f] + flux[f]
+            mixed = jnp.dot(weights[kind], slot[f], preferred_element_type=F32)
+            added = (AIR_STEP * SIGNS[f]) * flux[f]
+            target[f] = mixed
+            target[f, 0:1] = mixed[0:1] + (added if own else valid[place] * added)
 
 
 def pack_kernel(air, sea, first, second, top, sems, top_sems):
     rows = air.shape[2]
     north_first, _ = tile_state(rows)
     copies = []
-    for d, fields in enumerate((FIELDS, EARLY)):
+    for d in range(2):
         for side, out in enumerate((first, second)):
+            fields = FIELDS if d == 0 else EARLY[side]
             row = own_row(north_first, rows, d if side == 0 else rows - 1 - d)
             copies.append(
                 pltpu.make_async_copy(
@@ -161,20 +159,49 @@
     owned_top[...] = jnp.where(owns, top[...], 0.0)
 
 
-def tables_kernel(row_total, scale, owner, air, sea, land_in, transfer, air_mixing_in, sea_mixing_in,
-                  state, weights, base, sea_weights, column, turn, valid, rate, land,
-                  land_here, transfer_here, air_mixing, sea_mixing, sems, sea_sems, small_sems):
+def sea_tables_kernel(scale, owner, sea, land_in, sea_mixing_in, top_in, base, sea_weights, column, land, top,
+                      land_here, sea_mixing, sems, small_sems):
+    rows, levels = land.shape[0], sea.shape[2]
+    held, halves = base.shape[2], base.shape[1]
+    small = [
+        pltpu.make_async_copy(source, here, small_sems.at[k])
+        for k, (source, here) in enumerate(((sea_mixing_in, sea_mixing), (land_in, land_here)))
+    ]
+    loads = [
+        pltpu.make_async_copy(
+            sea.at[0, :, :, :, pl.ds(h * LANES, LANES)],
+            base.at[:, h, pl.ds(0, levels)],
+            sems.at[h],
+        )
+        for h in range(halves)
+    ]
+    for copy in small + loads:
+        copy.start()
+    top[...] = top_in[...]
+    if held > levels:
+        base[:, :, levels:] = jnp.zeros((FIELDS, halves, held - levels, rows, LANES), F32)
+    for copy in small:
+        copy.wait()
+    land[...] = land_here[...].astype(F32)
+    sea_weights[...] = mixing_parts(sea_mixing[...], 0.5)
+    factor = jnp.where(lax.axis_index("member") == owner[0], 0.5 * scale, 0.0)
+    first_column = jnp.broadcast_to(sea_mixing[:, 0:1], (levels, LANES))
+    for level in range(levels):
+        value = first_column[level : level + 1] + (1.0 if level == 0 else 0.0)
+        column[level] = factor * jnp.broadcast_to(value, (rows, LANES))
+    for copy in loads:
+        copy.wait()
+
+
+def tables_kernel(row_total, air, transfer, air_mixing_in, land, after, state, weights, turn, valid, rate,
+                  transfer_here, air_mixing, sems, small_sems):
+    del after
     rows, lon = air.shape[2], air.shape[4]
-    levels = sea.shape[2]
-    held, halves = base.shape[2], base.shape[1]
-    places = rows + 2 * NSUB
+    halves, places = lon // LANES, rows + 2 * NSUB
     north_first, first_row = tile_state(rows)
     small = [
         pltpu.make_async_copy(source, here, small_sems.at[k])
-        for k, (source, here) in enumerate((
-            (air_mixing_in, air_mixing), (sea_mixing_in, sea_mixing),
-            (land_in, land_here), (transfer, transfer_here),
-        ))
+        for k, (source, here) in enumerate(((air_mixing_in, air_mixing), (transfer, transfer_here)))
     ]
     copies = []
     for place in range(rows):
@@ -182,18 +209,8 @@
         copies.append(
             pltpu.make_async_copy(air.at[0, :, row], state.at[0, NSUB + place], sems.at[place])
         )
-    loads = [
-        pltpu.make_async_copy(
-            sea.at[0, :, :, :, pl.ds(h * LANES, LANES)],
-            base.at[:, h, pl.ds(0, levels)],
-            sea_sems.at[h],
-        )
-        for h in range(halves)
-    ]
-    for copy in small + copies + loads:
+    for copy in small + copies:
         copy.start()
-    if held > levels:
-        base[:, :, levels:] = jnp.zeros((FIELDS, halves, held - levels, rows, LANES), F32)
     line = lax.broadcasted_iota(jnp.int32, (places, LANES), 0) - NSUB
     index = first_row + jnp.where(north_first, rows - 1 - line, line)
     latitude = math.pi * ((index.astype(F32) + 0.5) / row_total - 0.5)
@@ -205,27 +222,22 @@
         valid[place] = jnp.concatenate([inside[part]] * halves, axis=1)
     for copy in small:
         copy.wait()
-    weights[...] = mixing_parts(air_mixing[...], 0.5 * DIFFUSE)
-    sea_weights[...] = mixing_parts(sea_mixing[...], 0.5)
-    factor = jnp.where(lax.axis_index("member") == owner[0], 0.5 * scale, 0.0)
-    first_column = jnp.broadcast_to(sea_mixing[:, 0:1], (levels, LANES))
-    for level in range(levels):
-        value = first_column[level : level + 1] + (1.0 if level == 0 else 0.0)
-        column[level] = factor * jnp.broadcast_to(value, (rows, LANES))
-    land[...] = land_here[...].astype(F32)
+    parts = mixing_parts(air_mixing[...], 0.5 * DIFFUSE)
+    weights[0] = parts
+    for side, place in enumerate((NSUB - 1, NSUB + rows)):
+        exists = valid[place, 0:1, 0:1].astype(BF16)
+        weights[1 + side] = parts * exists
     rate[...] = transfer_here[...] * land[...]
-    for copy in copies + loads:
+    for copy in copies:
         copy.wait()
 
 
-def ocean_kernel(owner, land, sea_weights, base_in, state, air_in, base, air_next, sea_next, staged,
-                 sems, sea_sems):
-    del base_in, air_in
+def ocean_kernel(owner, land, sea_weights, base_in, base, sea_next, staged, sea_sems):
+    del base_in
     held, halves, rows = base.shape[2], base.shape[1], base.shape[3]
     depth = staged.shape[1] // 3
     levels = sea_next.shape[2]
     owns = lax.axis_index("member") == owner[0]
-    copies = [send_row(state, air_next, place, sems.at[k]) for k, place in enumerate((0, rows - 1))]
 
     @pl.when(jnp.logical_not(owns))
     def _():
@@ -260,9 +272,6 @@
                 for h in range(halves):
                     flat[f, h, own] = kept[:, h * LANES : (h + 1) * LANES]
 
-    for copy in copies:
-        copy.wait()
-
 
 def surface_kernel(top_a, top_b, top_c, top_d, rate, state, surface, first, second):
     levels = state.shape[3]
@@ -277,16 +286,16 @@
         surface[1, NSUB + place] = jnp.tanh(surface[0, NSUB + place])
         surface[4, NSUB + place] = rate[row]
     for side, out in enumerate((first, second)):
-        for f in range(EARLY, FIELDS):
+        early = EARLY[side]
+        for f in range(early, FIELDS):
             place = NSUB + 1 if side == 0 else last - 1
-            out[(f - EARLY) * levels : (f - EARLY + 1) * levels] = state[0, place, f]
-        out[(FIELDS - EARLY) * levels :] = jnp.zeros(
-            (out.shape[0] - (FIELDS - EARLY) * levels, out.shape[1]), F32
-        )
+            out[(f - early) * levels : (f - early + 1) * levels] = state[0, place, f]
+        start = (FIELDS - early) * levels
+        out[start:] = jnp.zeros((out.shape[0] - start, out.shape[1]), F32)
         for d in range(NSUB - 1):
             place = NSUB + d if side == 0 else last - d
             for k, kept in enumerate((0, 2, 3, 4)):
-                at = (FIELDS - EARLY) * levels + 4 * d + k
+                at = start + 4 * d + k
                 out[at : at + 1] = surface[kept, place]
 
 
@@ -362,16 +371,17 @@
         copy.start()
 
     def row_of(side, f):
-        if f < EARLY:
+        early = EARLY[side]
+        if f < early:
             return (near, far)[side][FIELDS + f]
-        return rest[side][(f - EARLY) * levels : (f - EARLY + 1) * levels]
+        return rest[side][(f - early) * levels : (f - early + 1) * levels]
 
     take_rows(2, state, valid, [functools.partial(row_of, side) for side in range(2)])
     for side in range(2):
         for d in range(NSUB - 1):
             place = NSUB - 1 - d if side == 0 else places - NSUB + d
             for k, kept in enumerate((0, 2, 3, 4)):
-                at = (FIELDS - EARLY) * levels + 4 * d + k
+                at = (FIELDS - EARLY[side]) * levels + 4 * d + k
                 surface[kept, place] = rest[side][at : at + 1]
             surface[1, place] = jnp.tanh(surface[0, place])
     updates = []
@@ -427,13 +437,28 @@
         copy.wait()
 
 
-def sea_kernel(owner, base, column, flux_a, flux_b, flux_c, flux_d, sea_in, sea_next, result, sems):
-    del sea_in
+def send_last_rows(state, air_next, sems):
+    rows = air_next.shape[2]
+    return [send_row(state, air_next, place, sems.at[k]) for k, place in enumerate((0, rows - 1))]
+
+
+def last_rows_kernel(owner, state, air_in, air_next, sems):
+    del air_in
+
+    @pl.when(lax.axis_index("member") != owner[0])
+    def _():
+        for copy in send_last_rows(state, air_next, sems):
+            copy.wait()
+
+
+def sea_kernel(owner, base, column, flux_a, flux_b, flux_c, flux_d, state, sea_in, air_in, sea_next, air_next,
+               result, sems, air_sems):
+    del sea_in, air_in
     levels = column.shape[0]
 
     @pl.when(lax.axis_index("member") == owner[0])
     def _():
-        copies = []
+        copies = send_last_rows(state, air_next, air_sems)
         for f in range(FIELDS):
             mean = (flux_a[f] + flux_b[f]) + (flux_c[f] + flux_d[f])
             for h in range(base.shape[1]):
@@ -480,13 +505,13 @@
     return lax.ppermute(values, "member", [(i, i ^ k) for i in range(count)])
 
 
-def member_parts(values, then=None):
+def member_parts(values, then=None, order=1):
     k = 1
     while lax.axis_size("member") > 4 * k:
         other = swapped(values, k)
-        values = (values if then is None or k > 1 else then()) + other
+        values = (values if then is None or k > 1 else then(values)) + other
         k *= 2
-    others = range(lax.axis_size("member") - k, 0, -k)
+    others = list(range(k, lax.axis_size("member"), k))[::order]
     return [values] + [swapped(values, other) for other in others]
 
 
@@ -513,10 +538,13 @@
     column_type = pltpu.VMEM((sea_levels, rows, LANES), F32)
     sea_weight_type = pltpu.VMEM((held, 3 * sea_depth), BF16)
     cell_type = pltpu.VMEM((rows, lon), F32)
+    top_type = pltpu.VMEM((3, rows, lon), F32)
     flux_type = pltpu.VMEM((FIELDS, rows, lon), F32)
     air_type, sea_type = pltpu.HBM(atmos_state.shape, F32), pltpu.HBM(sea_slots.shape, F32)
-    topped = pltpu.VMEM((ceil_to((FIELDS - EARLY) * levels + 4 * (NSUB - 1), 8), lon), F32)
-    near_type = jax.ShapeDtypeStruct((FIELDS + EARLY, levels, lon), F32)
+    topped = [
+        pltpu.VMEM((ceil_to((FIELDS - early) * levels + 4 * (NSUB - 1), 8), lon), F32) for early in EARLY
+    ]
+    near_types = [jax.ShapeDtypeStruct((FIELDS + early, levels, lon), F32) for early in EARLY]
     staged = pltpu.VMEM((2, FIELDS, 3 * depth, lon), BF16)
     atmos_state, sea_slots, land_cells, transfer, air_square, sea_square = [
         pltpu.with_memory_space_constraint(value, pltpu.HBM)
@@ -529,7 +557,7 @@
         pack_kernel,
         name="pack_rows",
         cost_estimate=cost(1),
-        out_shape=(near_type, near_type, pltpu.VMEM((3, rows, lon), F32)),
+        out_shape=(*near_types, top_type),
         in_specs=[ANY, ANY],
         out_specs=(ANY, ANY, VMEM),
         scratch_shapes=[pltpu.SemaphoreType.DMA((4,)), pltpu.SemaphoreType.DMA((3,))],
@@ -539,49 +567,78 @@
         owner_kernel,
         name="owner_surface",
         cost_estimate=cost(0.1),
-        out_shape=pltpu.VMEM((3, rows, lon), F32),
+        out_shape=top_type,
         in_specs=[SMEM, VMEM],
         out_specs=VMEM,
         compiler_params=params(),
     )(owner_map, top)
     arrived = exchange((near, far), swaps)
-    top_parts = member_parts(top)
-
-    state, weights, base, sea_weights, column, turn, valid, rate, land = pl.pallas_call(
-        functools.partial(tables_kernel, rows * tiles, SEA_STEP / (NSUB * members)),
+    base, sea_weights, column, land = None, None, None, None
+
+    def sea_tables(top):
+        nonlocal base, sea_weights, column, land
+        base, sea_weights, column, land, again = pl.pallas_call(
+            functools.partial(sea_tables_kernel, SEA_STEP / (NSUB * members)),
+            name="sea_tables",
+            cost_estimate=cost(1),
+            out_shape=(base_type, sea_weight_type, column_type, cell_type, top_type),
+            in_specs=[SMEM, ANY, ANY, ANY, VMEM],
+            out_specs=(VMEM,) * 5,
+            scratch_shapes=[
+                pltpu.VMEM((rows, lon), jnp.int32),
+                pltpu.VMEM(sea_mixing.shape, F32),
+                pltpu.SemaphoreType.DMA((halves,)),
+                pltpu.SemaphoreType.DMA((2,)),
+            ],
+            compiler_params=params(),
+        )(owner_map, sea_slots, land_cells, sea_square, top)
+        return again
+
+    top_parts = member_parts(top, sea_tables, -1)
+
+    base, sea_next = pl.pallas_call(
+        ocean_kernel,
+        name="ocean",
+        cost_estimate=cost(1.2),
+        out_shape=(base_type, sea_type),
+        in_specs=[SMEM] + [VMEM] * 3,
+        out_specs=(VMEM, ANY),
+        input_output_aliases={3: 0},
+        scratch_shapes=[
+            pltpu.VMEM((2 * FIELDS, 3 * sea_depth, lon), BF16),
+            pltpu.SemaphoreType.DMA((halves,)),
+        ],
+        compiler_params=params(),
+    )(owner_map, land, sea_weights, base)
+
+    state, weights, turn, valid, rate = pl.pallas_call(
+        functools.partial(tables_kernel, rows * tiles),
         name="tables",
-        cost_estimate=cost(2),
+        cost_estimate=cost(1.5),
         out_shape=(
             state_type,
-            pltpu.VMEM((ceil_to(levels, 8), 3 * depth), BF16),
-            base_type,
-            sea_weight_type,
-            column_type,
+            pltpu.VMEM((3, ceil_to(levels, 8), 3 * depth), BF16),
             table_type,
             table_type,
             cell_type,
-            cell_type,
         ),
-        in_specs=[SMEM] + [ANY] * 6,
-        out_specs=(VMEM,) * 9,
+        in_specs=[ANY] * 3 + [VMEM] * 2,
+        out_specs=(VMEM,) * 5,
         scratch_shapes=[
-            pltpu.VMEM((rows, lon), jnp.int32),
             pltpu.VMEM((rows, lon), F32),
             pltpu.VMEM(air_mixing.shape, F32),
-            pltpu.VMEM(sea_mixing.shape, F32),
             pltpu.SemaphoreType.DMA((rows,)),
-            pltpu.SemaphoreType.DMA((halves,)),
-            pltpu.SemaphoreType.DMA((4,)),
+            pltpu.SemaphoreType.DMA((2,)),
         ],
         compiler_params=params(),
-    )(owner_map, atmos_state, sea_slots, land_cells, transfer, air_square, sea_square)
+    )(atmos_state, transfer, air_square, land, base)
     tables = (weights, turn, valid)
 
     surface, *rest_rows = pl.pallas_call(
         surface_kernel,
         name="surface",
         cost_estimate=cost(0.3),
-        out_shape=(surface_type, topped, topped),
+        out_shape=(surface_type, *topped),
         in_specs=[VMEM] * 6,
         out_specs=(VMEM,) * 3,
         compiler_params=params(),
@@ -650,7 +707,7 @@
         compiler_params=params(),
     )(*tables, surface, *arrived_third, state, total)
 
-    def finish():
+    def finish(flux):
         nonlocal state
         state, again = pl.pallas_call(
             finish_kernel,
@@ -665,7 +722,7 @@
         )(*tables, surface, flux, state)
         return again
 
-    flux_parts = member_parts(flux, finish)
+    flux_parts = member_parts(flux, finish, -1)
 
     state, air_next = pl.pallas_call(
         last_chain_kernel,
@@ -679,36 +736,33 @@
         compiler_params=params(),
     )(*tables, surface, *arrived_fourth, state)
 
-    base, air_next, sea_next = pl.pallas_call(
-        ocean_kernel,
-        name="ocean",
-        cost_estimate=cost(1.5),
-        out_shape=(base_type, air_type, sea_type),
-        in_specs=[SMEM] + [VMEM] * 4 + [ANY],
-        out_specs=(VMEM, ANY, ANY),
-        input_output_aliases={3: 0, 5: 1},
-        scratch_shapes=[
-            pltpu.VMEM((2 * FIELDS, 3 * sea_depth, lon), BF16),
-            pltpu.SemaphoreType.DMA((2,)),
-            pltpu.SemaphoreType.DMA((halves,)),
-        ],
-        compiler_params=params(),
-    )(owner_map, land, sea_weights, base, state, air_next)
-
-    sea_next = pl.pallas_call(
+    air_next = pl.pallas_call(
+        last_rows_kernel,
+        name="last_rows",
+        cost_estimate=cost(0.6),
+        out_shape=air_type,
+        in_specs=[SMEM, VMEM, ANY],
+        out_specs=ANY,
+        input_output_aliases={2: 0},
+        scratch_shapes=[pltpu.SemaphoreType.DMA((2,))],
+        compiler_params=params(),
+    )(owner_map, state, air_next)
+
+    sea_next, air_next = pl.pallas_call(
         sea_kernel,
         name="sea_step",
         cost_estimate=cost(1.5),
-        out_shape=sea_type,
-        in_specs=[SMEM] + [VMEM] * 6 + [ANY],
-        out_specs=ANY,
-        input_output_aliases={7: 0},
+        out_shape=(sea_type, air_type),
+        in_specs=[SMEM] + [VMEM] * 7 + [ANY, ANY],
+        out_specs=(ANY, ANY),
+        input_output_aliases={8: 0, 9: 1},
         scratch_shapes=[
             pltpu.VMEM((FIELDS, halves, sea_levels, rows, LANES), F32),
             pltpu.SemaphoreType.DMA((FIELDS, halves)),
+            pltpu.SemaphoreType.DMA((2,)),
         ],
         compiler_params=params(),
-    )(owner_map, base, column, *flux_parts, sea_next)
+    )(owner_map, base, column, *flux_parts, state, sea_next, air_next)
     return (air_next, jnp.swapaxes(sea_next, 2, 3))
 
 

time: 38.5 us -> 37.7 us (0.979); the launches traced: 38.7 us -> 37.5 us
  starting transfers between devices: 17.4 us -> 16.4 us
  waiting for transfers between devices: 2.13 us -> 1.73 us
    pallas_call x2 -> x4, Pallas kernels: 3.71 us -> 5.51 us  [the longest x1 1.72 us: shards(): pl.pallas_call(functools.partial(tables_kernel, rows * tiles), name='tabl...]
    ppermute x8, waiting for transfers between devices: 1.75 us -> 0.28 us  [swapped(): return lax.ppermute(values, 'member', [(i, i ^ k) for i in range(count)])]
    pallas_call x1, Pallas kernels: 1.38 us -> 0.11 us  [shards(): pl.pallas_call(sea_kernel, name='sea_step', cost_estimate=cost(1.5), out_...]
    ppermute x8, waiting for transfers between devices: 0.38 us -> 1.45 us  [exchange(): lax.ppermute(value, AXES, swap)]
    ppermute x8, starting transfers between devices: 9.45 us -> 8.58 us  [exchange(): lax.ppermute(value, AXES, swap)]
    pallas_call x1, Pallas kernels: 0.75 us -> 0.15 us  [shards(): pl.pallas_call(first_interior_kernel, name='first_interior', cost_estimat...]
    pallas_call x1, Pallas kernels: 2.38 us -> 2.82 us  [shards(): pl.pallas_call(interior_kernel, name='interior', cost_estimate=cost(2.5),...]
  transfers between devices with their start and end apart: 16 -> 16, of which waited for: 6 -> 3; matrix products, arithmetic and copies ran while one was open for 0% -> 0% of each run, Pallas kernels for 39% -> 44%
where the time goes in v4:
time: 37.7 us; the launch traced here: 37.5 us
  Pallas kernels  17.9 us (47%)
  starting transfers between devices  16.4 us (44%)
  waiting for transfers between devices  1.73 us (5%)
  between operations  1.44 us (4%)
    ppermute x8, starting transfers between devices, exchange(): lax.ppermute(value, AXES, swap)  8.58 us
    ppermute x8, starting transfers between devices, swapped(): return lax.ppermute(values, 'member', [(i, i ^ k) for i in range(count)])  7.87 us
    pallas_call x1, Pallas kernels, shards(): pl.pallas_call(interior_kernel, name='interior', cost_estimate=cost(2.5),...  2.82 us
    pallas_call x1, Pallas kernels, shards(): pl.pallas_call(last_chain_kernel, name='last_chain', cost_estimate=cost(2...  1.93 us
    pallas_call x1, Pallas kernels, shards(): pl.pallas_call(first_chain_kernel, name='first_chain', cost_estimate=cost...  1.88 us
    pallas_call x1, Pallas kernels, shards(): pl.pallas_call(functools.partial(tables_kernel, rows * tiles), name='tabl...  1.72 us
    pallas_call x1, Pallas kernels, sea_tables(): pl.pallas_call(functools.partial(sea_tables_kernel, SEA_STEP / (NSUB * me...  1.64 us
    pallas_call x1, Pallas kernels, shards(): pl.pallas_call(second_chain_kernel, name='second_chain', cost_estimate=co...  1.6 us
  transfers between devices with their start and end apart: 16, of which 3 were waited for; matrix products, arithmetic and copies ran while one was open for 0% of the time, Pallas kernels for 44%

profile of v4, /device:TPU:0, one launch (start us, length us, event | category | flops | bytes accessed | tf_op | source)
XLA Modules:
  0.0 37.5 jit_solution(17598621889737473004)
XLA Ops:
  0.6 1.3 %pack_rows.1 = (f32[7,72,256]{2,1,0:T(8,128)S(1)}, f32[7,72,256]{2,1,0:T(8,128)S(1)}, f32[3,8,256]{2,1,0:T(8,128)S(1)}) custom-call(f32[1,4,8,72,256]{4,3,2,1,0:T(8,128)} %air.3, f32[1,4,62,8,256]{4,3,2,1,0:T(8,128)} %bitcast.2), custom_call_target="tpu_custom_call" | custom-call | bytes 3500000 | tf_op jit(solution)/shard_map/pack_rows/pallas_call | solution.py:556
  1.9 3.1 %collective-permute-start = (f32[7,72,256]{2,1,0:T(8,128)S(1)}, f32[7,72,256]{2,1,0:T(8,128)S(1)}, u32[]{:S(2)}, u32[]{:S(2)}) collective-permute-start(f32[7,72,256]{2,1,0:T(8,128)S(1)} %get-tuple-element.50), channel_id=1, source_target_pairs={{0,1},{1,0},{2,3},{3,2},{4,5},{5,4},{6,7},{7,6},{8,9},{9,8},{10,11... | collective-permute-start | bytes 1548296 | tf_op jit(solution)/shard_map/ppermute | solution.py:500
  5.0 0.0 collective-permute-start.1
  5.7 0.6 %collective-permute-start.2 = (f32[3,8,256]{2,1,0:T(8,128)S(1)}, f32[3,8,256]{2,1,0:T(8,128)S(1)}, u32[]{:S(2)}, u32[]{:S(2)}) collective-permute-start(f32[3,8,256]{2,1,0:T(8,128)S(1)} %owner_surface.1.top_in), channel_id=1, source_target_pairs={{0,4},{4,0},{8,12},{12,8},{16,20},{20,16},{24,28},{28,24},{1,5},{5... | collective-permute-start | bytes 73736 | tf_op jit(solution)/shard_map/ppermute | solution.py:505
  6.3 1.6 %sea_tables.1 = (f32[4,2,64,8,128]{4,3,2,1,0:T(8,128)S(1)}, bf16[64,192]{1,0:T(8,128)(2,1)S(1)}, f32[62,8,128]{2,1,0:T(8,128)S(1)}, f32[8,256]{1,0:T(8,128)S(1)}, f32[3,8,256]{2,1,0:T(8,128)S(1)}) custom-call(s32[1]{0:T(128)S(6)} %copy.41.owner, f32[1,4,62,8,256]{4,3,2,1,0:T(8,128)} %bitcast.3, s32[8,256]{1,0:T(8,128)} %land_in.1, f32[62,62]{1,0:T(8,128)} %sea_mixing_in.1, ...), custom_call_target="tpu_custom_call" | custom-call | bytes 3500000 | tf_op jit(solution)/shard_map/sea_tables/pallas_call | solution.py:580
  7.9 0.0 collective-permute-done.2
  7.9 2.5 %collective-permute-start.3 = (f32[3,8,256]{2,1,0:T(8,128)S(1)}, f32[3,8,256]{2,1,0:T(8,128)S(1)}, u32[]{:S(2)}, u32[]{:S(2)}) collective-permute-start(f32[3,8,256]{2,1,0:T(8,128)S(1)} %add.6.top_a), channel_id=1, source_target_pairs={{0,24},{4,28},{8,16},{12,20},{16,8},{20,12},{24,0},{28,4},{1,25},{... | collective-permute-start | bytes 73736 | tf_op jit(solution)/shard_map/ppermute | solution.py:505
  10.4 0.5 %collective-permute-start.4 = (f32[3,8,256]{2,1,0:T(8,128)S(1)}, f32[3,8,256]{2,1,0:T(8,128)S(1)}, u32[]{:S(2)}, u32[]{:S(2)}) collective-permute-start(f32[3,8,256]{2,1,0:T(8,128)S(1)} %add.6.top_a), channel_id=1, source_target_pairs={{0,16},{4,20},{8,24},{12,28},{16,0},{20,4},{24,8},{28,12},{1,17},{... | collective-permute-start | bytes 73736 | tf_op jit(solution)/shard_map/ppermute | solution.py:505
  10.9 0.5 %collective-permute-start.5 = (f32[3,8,256]{2,1,0:T(8,128)S(1)}, f32[3,8,256]{2,1,0:T(8,128)S(1)}, u32[]{:S(2)}, u32[]{:S(2)}) collective-permute-start(f32[3,8,256]{2,1,0:T(8,128)S(1)} %add.6.top_a), channel_id=1, source_target_pairs={{0,8},{4,12},{8,0},{12,4},{16,24},{20,28},{24,16},{28,20},{1,9},{5... | collective-permute-start | bytes 73736 | tf_op jit(solution)/shard_map/ppermute | solution.py:505
  11.5 1.3 %ocean.1 = (f32[4,2,64,8,128]{4,3,2,1,0:T(8,128)S(1)}, f32[1,4,62,8,256]{4,3,2,1,0:T(8,128)}) custom-call(s32[1]{0:T(128)S(6)} %copy.41.owner, f32[8,256]{1,0:T(8,128)S(1)} %get-tuple-element.42.land, bf16[64,192]{1,0:T(8,128)(2,1)S(1)} %get-tuple-element.43.sea_weights, ...), custom_call_target="tpu_custom_call", output_to_operand_aliasing={{0}: (3, {})} | custom-call | bytes 4200000 | tf_op jit(solution)/shard_map/ocean/pallas_call | solution.py:599
  12.8 1.7 %tables.1 = (f32[5,16,4,72,256]{4,3,2,1,0:T(8,128)S(1)}, bf16[3,72,240]{2,1,0:T(8,128)(2,1)S(1)}, f32[16,1,256]{2,1,0:T(1,128)S(1)}, f32[16,1,256]{2,1,0:T(1,128)S(1)}, f32[8,256]{1,0:T(8,128)S(1)}) custom-call(f32[1,4,8,72,256]{4,3,2,1,0:T(8,128)} %air.3, f32[8,256]{1,0:T(8,128)} %transfer.1, f32[72,72]{1,0:T(8,128)} %air_mixing_in.1, ...), custom_call_target="tpu_custom_call" | custom-call | bytes 5250000 | tf_op jit(solution)/shard_map/tables/pallas_call | solution.py:614
  14.5 0.0 collective-permute-done.3.top_b
  14.5 0.0 collective-permute-done.4.top_c
  14.5 0.2 collective-permute-done.5.top_d
  14.8 0.1 surface.1
  14.9 2.7 %collective-permute-start.6 = (f32[88,256]{1,0:T(8,128)S(1)}, f32[88,256]{1,0:T(8,128)S(1)}, u32[]{:S(2)}, u32[]{:S(2)}) collective-permute-start(f32[88,256]{1,0:T(8,128)S(1)} %get-tuple-element.55), channel_id=1, source_target_pairs={{0,1},{1,0},{2,3},{3,2},{4,5},{5,4},{6,7},{7,6},{8,9},{9,8},{10,11... | collective-permute-start | bytes 270344 | tf_op jit(solution)/shard_map/ppermute | solution.py:500
  17.6 0.0 collective-permute-start.7
  17.6 0.2 first_interior.1
  17.8 1.0 %collective-permute-start.8 = (f32[4,72,256]{2,1,0:T(8,128)S(1)}, f32[4,72,256]{2,1,0:T(8,128)S(1)}, u32[]{:S(2)}, u32[]{:S(2)}) collective-permute-start(f32[4,72,256]{2,1,0:T(8,128)S(1)} %get-tuple-element.65), channel_id=1, source_target_pairs={{0,1},{1,0},{2,3},{3,2},{4,5},{5,4},{6,7},{7,6},{8,9},{9,8},{10,11... | collective-permute-start | bytes 884744 | tf_op jit(solution)/shard_map/ppermute | solution.py:500
  18.8 0.0 collective-permute-done.near
  18.8 0.0 collective-permute-start.9
  18.8 2.8 %interior.1 = (f32[5,16,4,72,256]{4,3,2,1,0:T(8,128)S(1)}, f32[16,4,1,256]{3,2,1,0:T(1,128)S(1)}) custom-call(bf16[3,72,240]{2,1,0:T(8,128)(2,1)S(1)} %get-tuple-element.47.weights, f32[16,1,256]{2,1,0:T(1,128)S(1)} %get-tuple-element.48.turn, f32[16,1,256]{2,1,0:T(1,128)S(1)} %get-tuple-element.49.valid, ...), custom_call_target="tpu_custom_call", output_to_operand_aliasing={{0}: (5, {}), {1}: (6, {})} | custom-call | bytes 8750000 | tf_op jit(solution)/shard_map/interior/pallas_call | solution.py:661
  21.6 0.0 collective-permute-done.1.far
  21.6 1.9 %first_chain.1 = (f32[5,16,4,72,256]{4,3,2,1,0:T(8,128)S(1)}, f32[16,4,1,256]{3,2,1,0:T(1,128)S(1)}) custom-call(bf16[3,72,240]{2,1,0:T(8,128)(2,1)S(1)} %get-tuple-element.47.weights, f32[16,1,256]{2,1,0:T(1,128)S(1)} %get-tuple-element.48.turn, f32[16,1,256]{2,1,0:T(1,128)S(1)} %get-tuple-element.49.valid, ...), custom_call_target="tpu_custom_call", output_to_operand_aliasing={{0}: (5, {}), {1}: (6, {})} | custom-call | bytes 7000000 | tf_op jit(solution)/shard_map/first_chain/pallas_call | solution.py:673
  23.5 0.0 collective-permute-done.6.near_rest
  23.5 0.0 collective-permute-done.7.far_rest
  23.5 1.6 %second_chain.1 = (f32[5,16,1,256]{3,2,1,0:T(1,128)S(1)}, f32[5,16,4,72,256]{4,3,2,1,0:T(8,128)S(1)}, f32[16,4,1,256]{3,2,1,0:T(1,128)S(1)}, f32[4,72,256]{2,1,0:T(8,128)S(1)}, f32[4,72,256]{2,1,0:T(8,128)S(1)}) custom-call(bf16[3,72,240]{2,1,0:T(8,128)(2,1)S(1)} %get-tuple-element.47.weights, ...), custom_call_target="tpu_custom_call", output_to_operand_aliasing={{0}: (7, {}), {1}: (8, {}), {2}: (9, {})} | custom-call | bytes 5250000 | tf_op jit(solution)/shard_map/second_chain/pallas_call | solution.py:685
  25.1 1.8 %collective-permute-start.14 = (f32[4,72,256]{2,1,0:T(8,128)S(1)}, f32[4,72,256]{2,1,0:T(8,128)S(1)}, u32[]{:S(2)}, u32[]{:S(2)}) collective-permute-start(f32[4,72,256]{2,1,0:T(8,128)S(1)} %get-tuple-element.72), channel_id=1, source_target_pairs={{0,1},{1,0},{2,3},{3,2},{4,5},{5,4},{6,7},{7,6},{8,9},{9,8},{10,11... | collective-permute-start | bytes 884744 | tf_op jit(solution)/shard_map/ppermute | solution.py:500
  26.9 0.0 collective-permute-start.15
  26.9 0.4 %collective-permute-done.8.near = f32[4,72,256]{2,1,0:T(8,128)S(1)} collective-permute-done((f32[4,72,256]{2,1,0:T(8,128)S(1)}, f32[4,72,256]{2,1,0:T(8,128)S(1)}, u32[]{:S(2)}, u32[]{:S(2)}) %collective-permute-start.8) | collective-permute-done | bytes 294944 | tf_op jit(solution)/shard_map/ppermute | solution.py:500
  27.2 0.0 collective-permute-done.9.far
  27.2 1.5 %third_chain.1 = (f32[5,16,4,72,256]{4,3,2,1,0:T(8,128)S(1)}, f32[16,4,1,256]{3,2,1,0:T(1,128)S(1)}, f32[4,8,256]{2,1,0:T(8,128)S(1)}) custom-call(bf16[3,72,240]{2,1,0:T(8,128)(2,1)S(1)} %get-tuple-element.47.weights, f32[16,1,256]{2,1,0:T(1,128)S(1)} %get-tuple-element.48.turn, ...), custom_call_target="tpu_custom_call", output_to_operand_aliasing={{0}: (6, {}), {1}: (7, {})} | custom-call | bytes 5250000 | tf_op jit(solution)/shard_map/third_chain/pallas_call | solution.py:698
  28.7 0.2 collective-permute-start.10
  28.9 1.0 %finish.1 = (f32[5,16,4,72,256]{4,3,2,1,0:T(8,128)S(1)}, f32[4,8,256]{2,1,0:T(8,128)S(1)}) custom-call(bf16[3,72,240]{2,1,0:T(8,128)(2,1)S(1)} %get-tuple-element.47.weights, f32[16,1,256]{2,1,0:T(1,128)S(1)} %get-tuple-element.48.turn, f32[16,1,256]{2,1,0:T(1,128)S(1)} %get-tuple-element.49.valid, ...), custom_call_target="tpu_custom_call", output_to_operand_aliasing={{0}: (5, {})} | custom-call | bytes 3500000 | tf_op jit(solution)/shard_map/finish/pallas_call | solution.py:712
  29.9 0.0 collective-permute-done.10
  30.0 2.5 %collective-permute-start.11 = (f32[4,8,256]{2,1,0:T(8,128)S(1)}, f32[4,8,256]{2,1,0:T(8,128)S(1)}, u32[]{:S(2)}, u32[]{:S(2)}) collective-permute-start(f32[4,8,256]{2,1,0:T(8,128)S(1)} %add.7.flux_a), channel_id=1, source_target_pairs={{0,24},{4,28},{8,16},{12,20},{16,8},{20,12},{24,0},{28,4},{1,25},{... | collective-permute-start | bytes 98312 | tf_op jit(solution)/shard_map/ppermute | solution.py:505
  32.5 0.6 %collective-permute-start.12 = (f32[4,8,256]{2,1,0:T(8,128)S(1)}, f32[4,8,256]{2,1,0:T(8,128)S(1)}, u32[]{:S(2)}, u32[]{:S(2)}) collective-permute-start(f32[4,8,256]{2,1,0:T(8,128)S(1)} %add.7.flux_a), channel_id=1, source_target_pairs={{0,16},{4,20},{8,24},{12,28},{16,0},{20,4},{24,8},{28,12},{1,17},{... | collective-permute-start | bytes 98312 | tf_op jit(solution)/shard_map/ppermute | solution.py:505
  33.1 0.4 %collective-permute-start.13 = (f32[4,8,256]{2,1,0:T(8,128)S(1)}, f32[4,8,256]{2,1,0:T(8,128)S(1)}, u32[]{:S(2)}, u32[]{:S(2)}) collective-permute-start(f32[4,8,256]{2,1,0:T(8,128)S(1)} %add.7.flux_a), channel_id=1, source_target_pairs={{0,8},{4,12},{8,0},{12,4},{16,24},{20,28},{24,16},{28,20},{1,9},{5... | collective-permute-start | bytes 98312 | tf_op jit(solution)/shard_map/ppermute | solution.py:505
  33.5 1.1 %collective-permute-done.14.near = f32[4,72,256]{2,1,0:T(8,128)S(1)} collective-permute-done((f32[4,72,256]{2,1,0:T(8,128)S(1)}, f32[4,72,256]{2,1,0:T(8,128)S(1)}, u32[]{:S(2)}, u32[]{:S(2)}) %collective-permute-start.14) | collective-permute-done | bytes 294944 | tf_op jit(solution)/shard_map/ppermute | solution.py:500
  34.6 0.0 collective-permute-done.15.far
  34.6 1.9 %last_chain.1 = (f32[5,16,4,72,256]{4,3,2,1,0:T(8,128)S(1)}, f32[1,4,8,72,256]{4,3,2,1,0:T(8,128)}) custom-call(bf16[3,72,240]{2,1,0:T(8,128)(2,1)S(1)} %get-tuple-element.47.weights, f32[16,1,256]{2,1,0:T(1,128)S(1)} %get-tuple-element.48.turn, f32[16,1,256]{2,1,0:T(1,128)S(1)} %get-tuple-element.49.valid, ...), custom_call_target="tpu_custom_call", output_to_operand_aliasing={{0}: (6, {})} | custom-call | bytes 8750000 | tf_op jit(solution)/shard_map/last_chain/pallas_call | solution.py:727
  36.5 0.8 %last_rows.1.air_in = f32[1,4,8,72,256]{4,3,2,1,0:T(8,128)} custom-call(s32[1]{0:T(128)S(6)} %copy.41.owner, f32[5,16,4,72,256]{4,3,2,1,0:T(8,128)S(1)} %get-tuple-element.75.state, f32[1,4,8,72,256]{4,3,2,1,0:T(8,128)} %get-tuple-element.77.air_in), custom_call_target="tpu_custom_call", output_to_operand_aliasing={{}: (2, {})} | custom-call | bytes 2100000 | tf_op jit(solution)/shard_map/last_rows/pallas_call | solution.py:739
  37.4 0.0 collective-permute-done.11.flux_b
  37.4 0.0 collective-permute-done.12.flux_c
  37.4 0.0 collective-permute-done.13.flux_d
  37.4 0.1 sea_step.1
  (3 shorter events, 0.0 us)
Async XLA Ops:
  1.9 16.8 %collective-permute-start = (f32[7,72,256]{2,1,0:T(8,128)S(1)}, f32[7,72,256]{2,1,0:T(8,128)S(1)}, u32[]{:S(2)}, u32[]{:S(2)}) collective-permute-start(f32[7,72,256]{2,1,0:T(8,128)S(1)} %get-tuple-element.50), channel_id=1, source_target_pairs={{0,1},{1,0},{2,3},{3,2},{4,5},{5,4},{6,7},{7,6},{8,9},{9,8},{10,11... | collective-permute-start | bytes 1548296 | tf_op jit(solution)/shard_map/ppermute | solution.py:500
  5.0 16.6 %collective-permute-start.1 = (f32[7,72,256]{2,1,0:T(8,128)S(1)}, f32[7,72,256]{2,1,0:T(8,128)S(1)}, u32[]{:S(2)}, u32[]{:S(2)}) collective-permute-start(f32[7,72,256]{2,1,0:T(8,128)S(1)} %get-tuple-element.51), channel_id=1, source_target_pairs={{0,4},{1,2},{2,1},{3,7},{4,0},{5,6},{6,5},{7,3},{8,12},{9,10},{10,... | collective-permute-start | bytes 1548296 | tf_op jit(solution)/shard_map/ppermute | solution.py:500
  5.7 2.2 %collective-permute-start.2 = (f32[3,8,256]{2,1,0:T(8,128)S(1)}, f32[3,8,256]{2,1,0:T(8,128)S(1)}, u32[]{:S(2)}, u32[]{:S(2)}) collective-permute-start(f32[3,8,256]{2,1,0:T(8,128)S(1)} %owner_surface.1.top_in), channel_id=1, source_target_pairs={{0,4},{4,0},{8,12},{12,8},{16,20},{20,16},{24,28},{28,24},{1,5},{5... | collective-permute-start | bytes 73736 | tf_op jit(solution)/shard_map/ppermute | solution.py:505
  7.9 6.6 %collective-permute-start.3 = (f32[3,8,256]{2,1,0:T(8,128)S(1)}, f32[3,8,256]{2,1,0:T(8,128)S(1)}, u32[]{:S(2)}, u32[]{:S(2)}) collective-permute-start(f32[3,8,256]{2,1,0:T(8,128)S(1)} %add.6.top_a), channel_id=1, source_target_pairs={{0,24},{4,28},{8,16},{12,20},{16,8},{20,12},{24,0},{28,4},{1,25},{... | collective-permute-start | bytes 73736 | tf_op jit(solution)/shard_map/ppermute | solution.py:505
  10.4 4.1 %collective-permute-start.4 = (f32[3,8,256]{2,1,0:T(8,128)S(1)}, f32[3,8,256]{2,1,0:T(8,128)S(1)}, u32[]{:S(2)}, u32[]{:S(2)}) collective-permute-start(f32[3,8,256]{2,1,0:T(8,128)S(1)} %add.6.top_a), channel_id=1, source_target_pairs={{0,16},{4,20},{8,24},{12,28},{16,0},{20,4},{24,8},{28,12},{1,17},{... | collective-permute-start | bytes 73736 | tf_op jit(solution)/shard_map/ppermute | solution.py:505
  10.9 3.8 %collective-permute-start.5 = (f32[3,8,256]{2,1,0:T(8,128)S(1)}, f32[3,8,256]{2,1,0:T(8,128)S(1)}, u32[]{:S(2)}, u32[]{:S(2)}) collective-permute-start(f32[3,8,256]{2,1,0:T(8,128)S(1)} %add.6.top_a), channel_id=1, source_target_pairs={{0,8},{4,12},{8,0},{12,4},{16,24},{20,28},{24,16},{28,20},{1,9},{5... | collective-permute-start | bytes 73736 | tf_op jit(solution)/shard_map/ppermute | solution.py:505
  14.9 8.6 %collective-permute-start.6 = (f32[88,256]{1,0:T(8,128)S(1)}, f32[88,256]{1,0:T(8,128)S(1)}, u32[]{:S(2)}, u32[]{:S(2)}) collective-permute-start(f32[88,256]{1,0:T(8,128)S(1)} %get-tuple-element.55), channel_id=1, source_target_pairs={{0,1},{1,0},{2,3},{3,2},{4,5},{5,4},{6,7},{7,6},{8,9},{9,8},{10,11... | collective-permute-start | bytes 270344 | tf_op jit(solution)/shard_map/ppermute | solution.py:500
  17.6 5.9 %collective-permute-start.7 = (f32[88,256]{1,0:T(8,128)S(1)}, f32[88,256]{1,0:T(8,128)S(1)}, u32[]{:S(2)}, u32[]{:S(2)}) collective-permute-start(f32[88,256]{1,0:T(8,128)S(1)} %get-tuple-element.56), channel_id=1, source_target_pairs={{0,4},{1,2},{2,1},{3,7},{4,0},{5,6},{6,5},{7,3},{8,12},{9,10},{10,... | collective-permute-start | bytes 270344 | tf_op jit(solution)/shard_map/ppermute | solution.py:500
  17.8 9.5 %collective-permute-start.8 = (f32[4,72,256]{2,1,0:T(8,128)S(1)}, f32[4,72,256]{2,1,0:T(8,128)S(1)}, u32[]{:S(2)}, u32[]{:S(2)}) collective-permute-start(f32[4,72,256]{2,1,0:T(8,128)S(1)} %get-tuple-element.65), channel_id=1, source_target_pairs={{0,1},{1,0},{2,3},{3,2},{4,5},{5,4},{6,7},{7,6},{8,9},{9,8},{10,11... | collective-permute-start | bytes 884744 | tf_op jit(solution)/shard_map/ppermute | solution.py:500
  18.8 8.5 %collective-permute-start.9 = (f32[4,72,256]{2,1,0:T(8,128)S(1)}, f32[4,72,256]{2,1,0:T(8,128)S(1)}, u32[]{:S(2)}, u32[]{:S(2)}) collective-permute-start(f32[4,72,256]{2,1,0:T(8,128)S(1)} %get-tuple-element.66), channel_id=1, source_target_pairs={{0,4},{1,2},{2,1},{3,7},{4,0},{5,6},{6,5},{7,3},{8,12},{9,10},{10,... | collective-permute-start | bytes 884744 | tf_op jit(solution)/shard_map/ppermute | solution.py:500
  25.1 9.5 %collective-permute-start.14 = (f32[4,72,256]{2,1,0:T(8,128)S(1)}, f32[4,72,256]{2,1,0:T(8,128)S(1)}, u32[]{:S(2)}, u32[]{:S(2)}) collective-permute-start(f32[4,72,256]{2,1,0:T(8,128)S(1)} %get-tuple-element.72), channel_id=1, source_target_pairs={{0,1},{1,0},{2,3},{3,2},{4,5},{5,4},{6,7},{7,6},{8,9},{9,8},{10,11... | collective-permute-start | bytes 884744 | tf_op jit(solution)/shard_map/ppermute | solution.py:500
  26.9 7.7 %collective-permute-start.15 = (f32[4,72,256]{2,1,0:T(8,128)S(1)}, f32[4,72,256]{2,1,0:T(8,128)S(1)}, u32[]{:S(2)}, u32[]{:S(2)}) collective-permute-start(f32[4,72,256]{2,1,0:T(8,128)S(1)} %get-tuple-element.73), channel_id=1, source_target_pairs={{0,4},{1,2},{2,1},{3,7},{4,0},{5,6},{6,5},{7,3},{8,12},{9,10},{10,... | collective-permute-start | bytes 884744 | tf_op jit(solution)/shard_map/ppermute | solution.py:500
  28.7 1.3 %collective-permute-start.10 = (f32[4,8,256]{2,1,0:T(8,128)S(1)}, f32[4,8,256]{2,1,0:T(8,128)S(1)}, u32[]{:S(2)}, u32[]{:S(2)}) collective-permute-start(f32[4,8,256]{2,1,0:T(8,128)S(1)} %get-tuple-element.69.flux_in), channel_id=1, source_target_pairs={{0,4},{4,0},{8,12},{12,8},{16,20},{20,16},{24,28},{28,24},{1,5},{5... | collective-permute-start | bytes 98312 | tf_op jit(solution)/shard_map/ppermute | solution.py:505
  30.0 7.4 %collective-permute-start.11 = (f32[4,8,256]{2,1,0:T(8,128)S(1)}, f32[4,8,256]{2,1,0:T(8,128)S(1)}, u32[]{:S(2)}, u32[]{:S(2)}) collective-permute-start(f32[4,8,256]{2,1,0:T(8,128)S(1)} %add.7.flux_a), channel_id=1, source_target_pairs={{0,24},{4,28},{8,16},{12,20},{16,8},{20,12},{24,0},{28,4},{1,25},{... | collective-permute-start | bytes 98312 | tf_op jit(solution)/shard_map/ppermute | solution.py:505
  32.5 4.9 %collective-permute-start.12 = (f32[4,8,256]{2,1,0:T(8,128)S(1)}, f32[4,8,256]{2,1,0:T(8,128)S(1)}, u32[]{:S(2)}, u32[]{:S(2)}) collective-permute-start(f32[4,8,256]{2,1,0:T(8,128)S(1)} %add.7.flux_a), channel_id=1, source_target_pairs={{0,16},{4,20},{8,24},{12,28},{16,0},{20,4},{24,8},{28,12},{1,17},{... | collective-permute-start | bytes 98312 | tf_op jit(solution)/shard_map/ppermute | solution.py:505
  33.1 4.3 %collective-permute-start.13 = (f32[4,8,256]{2,1,0:T(8,128)S(1)}, f32[4,8,256]{2,1,0:T(8,128)S(1)}, u32[]{:S(2)}, u32[]{:S(2)}) collective-permute-start(f32[4,8,256]{2,1,0:T(8,128)S(1)} %add.7.flux_a), channel_id=1, source_target_pairs={{0,8},{4,12},{8,0},{12,4},{16,24},{20,28},{24,16},{28,20},{1,9},{5... | collective-permute-start | bytes 98312 | tf_op jit(solution)/shard_map/ppermute | solution.py:505

commit v5 on v4

--- a/solution.py
+++ b/solution.py
@@ -17,7 +17,7 @@
 SIGNS = (1.0, 1.0, -1.0, -1.0)
 FIELDS = 4
 LANES = 128
-AHEAD = 0
+AHEAD = 6
 EARLY = (3, 3)
 
 F32 = jnp.float32
@@ -154,12 +154,13 @@
         copy.wait()
 
 
-def owner_kernel(owner, top, owned_top):
-    owns = lax.axis_index("member") == owner[0]
-    owned_top[...] = jnp.where(owns, top[...], 0.0)
-
-
-def sea_tables_kernel(scale, owner, sea, land_in, sea_mixing_in, top_in, base, sea_weights, column, land, top,
+def owner_kernel(owner, top, other, owned_top):
+    member = lax.axis_index("member")
+    here = jnp.where(owner[0] == member, top[...], 0.0)
+    owned_top[...] = here + jnp.where(owner[0] == member + 1 - 2 * lax.rem(member, 2), other[...], 0.0)
+
+
+def sea_tables_kernel(scale, owner, sea, land_in, sea_mixing_in, base, sea_weights, column, land,
                       land_here, sea_mixing, sems, small_sems):
     rows, levels = land.shape[0], sea.shape[2]
     held, halves = base.shape[2], base.shape[1]
@@ -177,7 +178,6 @@
     ]
     for copy in small + loads:
         copy.start()
-    top[...] = top_in[...]
     if held > levels:
         base[:, :, levels:] = jnp.zeros((FIELDS, halves, held - levels, rows, LANES), F32)
     for copy in small:
@@ -232,36 +232,21 @@
         copy.wait()
 
 
-def ocean_kernel(owner, land, sea_weights, base_in, base, sea_next, staged, sea_sems):
-    del base_in
+def ocean_kernel(part_number, owner, land, sea_weights, base_in, after, base, staged):
+    del base_in, after
     held, halves, rows = base.shape[2], base.shape[1], base.shape[3]
     depth = staged.shape[1] // 3
-    levels = sea_next.shape[2]
-    owns = lax.axis_index("member") == owner[0]
-
-    @pl.when(jnp.logical_not(owns))
-    def _():
-        stores = [
-            pltpu.make_async_copy(
-                base.at[:, h, pl.ds(0, levels)],
-                sea_next.at[0, :, :, :, pl.ds(h * LANES, LANES)],
-                sea_sems.at[h],
-            )
-            for h in range(halves)
-        ]
-        for store in stores:
-            store.start()
-        for store in stores:
-            store.wait()
-
-    @pl.when(owns)
+    half = FIELDS // 2
+    fields = range(part_number * half, (part_number + 1) * half)
+
+    @pl.when(lax.axis_index("member") == owner[0])
     def _():
         flat = base.reshape(FIELDS, halves, held * rows, LANES)
 
         for row in range(rows):
             own = pl.ds(row, held, stride=rows)
             at_sea = land[row : row + 1] == 1.0
-            for f in range(FIELDS):
+            for f in fields:
                 slot = staged.at[(row * FIELDS + f) % staged.shape[0]]
                 cells = jnp.concatenate([flat[f, h, own] for h in range(halves)], axis=1)
                 for offset in range(0, held, 16):
@@ -392,8 +377,9 @@
         copy.wait()
 
 
-def third_chain_kernel(weights, turn, valid, surface, near, far, state_in, total_in, state, total, flux, staged):
-    del state_in, total_in
+def third_chain_kernel(weights, turn, valid, surface, near, far, state_in, total_in, after, state, total, flux,
+                       staged):
+    del state_in, total_in, after
     rows = state.shape[1] - 2 * NSUB
     north_first, _ = tile_state(rows)
     take_rows(3, state, valid, rows_from(near, far))
@@ -424,8 +410,25 @@
     return copy
 
 
-def last_chain_kernel(weights, turn, valid, surface, near, far, state_in, state, air_next, staged, sems):
+def last_chain_kernel(owner, weights, turn, valid, surface, near, far, base, state_in, state, air_next, sea_next,
+                      staged, sems, sea_sems):
     del state_in
+    levels = sea_next.shape[2]
+    stores = [
+        pltpu.make_async_copy(
+            base.at[:, h, pl.ds(0, levels)],
+            sea_next.at[0, :, :, :, pl.ds(h * LANES, LANES)],
+            sea_sems.at[h],
+        )
+        for h in range(base.shape[1])
+    ]
+    others = lax.axis_index("member") != owner[0]
+
+    @pl.when(others)
+    def _():
+        for store in stores:
+            store.start()
+
     rows = air_next.shape[2]
     copies = [send_row(state, air_next, place, sems.at[place]) for place in range(1, rows - 1)]
     take_rows(4, state, valid, rows_from(near, far))
@@ -435,6 +438,11 @@
     advance(state, surface, None, weights, staged, turn, valid, updates, False)
     for copy in copies:
         copy.wait()
+
+    @pl.when(others)
+    def _():
+        for store in stores:
+            store.wait()
 
 
 def send_last_rows(state, air_next, sems):
@@ -505,8 +513,7 @@
     return lax.ppermute(values, "member", [(i, i ^ k) for i in range(count)])
 
 
-def member_parts(values, then=None, order=1):
-    k = 1
+def member_parts(values, then=None, order=1, k=1):
     while lax.axis_size("member") > 4 * k:
         other = swapped(values, k)
         values = (values if then is None or k > 1 else then(values)) + other
@@ -563,53 +570,45 @@
         scratch_shapes=[pltpu.SemaphoreType.DMA((4,)), pltpu.SemaphoreType.DMA((3,))],
         compiler_params=params(),
     )(atmos_state, sea_slots)
+    arrived = exchange((near, far), swaps)
     top = pl.pallas_call(
         owner_kernel,
         name="owner_surface",
         cost_estimate=cost(0.1),
         out_shape=top_type,
-        in_specs=[SMEM, VMEM],
+        in_specs=[SMEM, VMEM, VMEM],
         out_specs=VMEM,
         compiler_params=params(),
-    )(owner_map, top)
-    arrived = exchange((near, far), swaps)
-    base, sea_weights, column, land = None, None, None, None
-
-    def sea_tables(top):
-        nonlocal base, sea_weights, column, land
-        base, sea_weights, column, land, again = pl.pallas_call(
-            functools.partial(sea_tables_kernel, SEA_STEP / (NSUB * members)),
-            name="sea_tables",
-            cost_estimate=cost(1),
-            out_shape=(base_type, sea_weight_type, column_type, cell_type, top_type),
-            in_specs=[SMEM, ANY, ANY, ANY, VMEM],
-            out_specs=(VMEM,) * 5,
-            scratch_shapes=[
-                pltpu.VMEM((rows, lon), jnp.int32),
-                pltpu.VMEM(sea_mixing.shape, F32),
-                pltpu.SemaphoreType.DMA((halves,)),
-                pltpu.SemaphoreType.DMA((2,)),
-            ],
+    )(owner_map, top, swapped(top, 1))
+    top_parts = member_parts(top, order=-1, k=2)
+    base, sea_weights, column, land = pl.pallas_call(
+        functools.partial(sea_tables_kernel, SEA_STEP / (NSUB * members)),
+        name="sea_tables",
+        cost_estimate=cost(1.5),
+        out_shape=(base_type, sea_weight_type, column_type, cell_type),
+        in_specs=[SMEM, ANY, ANY, ANY],
+        out_specs=(VMEM,) * 4,
+        scratch_shapes=[
+            pltpu.VMEM((rows, lon), jnp.int32),
+            pltpu.VMEM(sea_mixing.shape, F32),
+            pltpu.SemaphoreType.DMA((halves,)),
+            pltpu.SemaphoreType.DMA((2,)),
+        ],
+        compiler_params=params(),
+    )(owner_map, sea_slots, land_cells, sea_square)
+
+    def ocean(part, base, after):
+        return pl.pallas_call(
+            functools.partial(ocean_kernel, part),
+            name="ocean",
+            cost_estimate=cost(0.6),
+            out_shape=base_type,
+            in_specs=[SMEM] + [VMEM] * 4,
+            out_specs=VMEM,
+            input_output_aliases={3: 0},
+            scratch_shapes=[pltpu.VMEM((2 * FIELDS, 3 * sea_depth, lon), BF16)],
             compiler_params=params(),
-        )(owner_map, sea_slots, land_cells, sea_square, top)
-        return again
-
-    top_parts = member_parts(top, sea_tables, -1)
-
-    base, sea_next = pl.pallas_call(
-        ocean_kernel,
-        name="ocean",
-        cost_estimate=cost(1.2),
-        out_shape=(base_type, sea_type),
-        in_specs=[SMEM] + [VMEM] * 3,
-        out_specs=(VMEM, ANY),
-        input_output_aliases={3: 0},
-        scratch_shapes=[
-            pltpu.VMEM((2 * FIELDS, 3 * sea_depth, lon), BF16),
-            pltpu.SemaphoreType.DMA((halves,)),
-        ],
-        compiler_params=params(),
-    )(owner_map, land, sea_weights, base)
+        )(owner_map, land, sea_weights, base, after)
 
     state, weights, turn, valid, rate = pl.pallas_call(
         functools.partial(tables_kernel, rows * tiles),
@@ -695,17 +694,19 @@
     )(*tables, *arrived, *arrived_rest, surface, state, total)
     arrived_fourth = exchange(fourth_rows, swaps)
 
+    base = ocean(0, base, total)
+
     state, _, flux = pl.pallas_call(
         third_chain_kernel,
         name="third_chain",
         cost_estimate=cost(1.5),
         out_shape=(state_type, total_type, flux_type),
-        in_specs=[VMEM] * 8,
+        in_specs=[VMEM] * 9,
         out_specs=(VMEM,) * 3,
         input_output_aliases={6: 0, 7: 1},
         scratch_shapes=[staged],
         compiler_params=params(),
-    )(*tables, surface, *arrived_third, state, total)
+    )(*tables, surface, *arrived_third, state, total, base)
 
     def finish(flux):
         nonlocal state
@@ -724,17 +725,23 @@
 
     flux_parts = member_parts(flux, finish, -1)
 
-    state, air_next = pl.pallas_call(
+    base = ocean(1, base, state)
+
+    state, air_next, sea_next = pl.pallas_call(
         last_chain_kernel,
         name="last_chain",
         cost_estimate=cost(2.5),
-        out_shape=(state_type, air_type),
-        in_specs=[VMEM] * 7,
-        out_specs=(VMEM, ANY),
-        input_output_aliases={6: 0},
-        scratch_shapes=[staged, pltpu.SemaphoreType.DMA((rows,))],
-        compiler_params=params(),
-    )(*tables, surface, *arrived_fourth, state)
+        out_shape=(state_type, air_type, sea_type),
+        in_specs=[SMEM] + [VMEM] * 8,
+        out_specs=(VMEM, ANY, ANY),
+        input_output_aliases={8: 0},
+        scratch_shapes=[
+            staged,
+            pltpu.SemaphoreType.DMA((rows,)),
+            pltpu.SemaphoreType.DMA((halves,)),
+        ],
+        compiler_params=params(),
+    )(owner_map, *tables, surface, *arrived_fourth, base, state)
 
     air_next = pl.pallas_call(
         last_rows_kernel,

time: 37.7 us -> 37.6 us (level)
  waiting for transfers between devices: 1.73 us -> 2.88 us
  Pallas kernels: 17.9 us -> 16.8 us
    pallas_call x1, Pallas kernels: 0.15 us -> 1.64 us  [shards(): pl.pallas_call(first_interior_kernel, name='first_interior', cost_estimat...]
    pallas_call x2 -> x3, Pallas kernels: 2.94 us -> 1.64 us  [the longest x1 1.64 us: shards(): pl.pallas_call(functools.partial(sea_tables_kernel, SEA_STEP / (NSUB * me...]
    pallas_call x1, Pallas kernels: 2.82 us -> 1.52 us  [shards(): pl.pallas_call(interior_kernel, name='interior', cost_estimate=cost(2.5),...]
    ppermute x8, waiting for transfers between devices: 0.28 us -> 1.4 us  [swapped(): return lax.ppermute(values, 'member', [(i, i ^ k) for i in range(count)])]
  transfers between devices with their start and end apart: 16 -> 16, of which waited for: 3 -> 5; matrix products, arithmetic and copies ran while one was open for 0% -> 0% of each run, Pallas kernels for 44% -> 41%
where the time goes in v5:
time: 37.6 us; the launch traced here: 37.3 us
  Pallas kernels  16.8 us (45%)
  starting transfers between devices  16.2 us (43%)
  waiting for transfers between devices  2.88 us (8%)
  between operations  1.42 us (4%)
    ppermute x8, starting transfers between devices, exchange(): lax.ppermute(value, AXES, swap)  8.61 us
    ppermute x8, starting transfers between devices, swapped(): return lax.ppermute(values, 'member', [(i, i ^ k) for i in range(count)])  7.55 us
    pallas_call x1, Pallas kernels, shards(): pl.pallas_call(last_chain_kernel, name='last_chain', cost_estimate=cost(2...  1.96 us
    pallas_call x1, Pallas kernels, shards(): pl.pallas_call(first_chain_kernel, name='first_chain', cost_estimate=cost...  1.89 us
    pallas_call x1, Pallas kernels, shards(): pl.pallas_call(functools.partial(tables_kernel, rows * tiles), name='tabl...  1.72 us
    pallas_call x1, Pallas kernels, shards(): pl.pallas_call(first_interior_kernel, name='first_interior', cost_estimat...  1.64 us
    pallas_call x1, Pallas kernels, shards(): pl.pallas_call(functools.partial(sea_tables_kernel, SEA_STEP / (NSUB * me...  1.64 us
    pallas_call x1, Pallas kernels, shards(): pl.pallas_call(second_chain_kernel, name='second_chain', cost_estimate=co...  1.61 us
  transfers between devices with their start and end apart: 16, of which 5 were waited for; matrix products, arithmetic and copies ran while one was open for 0% of the time, Pallas kernels for 41%

profile of v5, /device:TPU:0, one launch (start us, length us, event | category | flops | bytes accessed | tf_op | source)
XLA Modules:
  0.0 37.3 jit_solution(8367133042330649955)
XLA Ops:
  0.6 1.3 %pack_rows.1 = (f32[7,72,256]{2,1,0:T(8,128)S(1)}, f32[7,72,256]{2,1,0:T(8,128)S(1)}, f32[3,8,256]{2,1,0:T(8,128)S(1)}) custom-call(f32[1,4,8,72,256]{4,3,2,1,0:T(8,128)} %air.3, f32[1,4,62,8,256]{4,3,2,1,0:T(8,128)} %bitcast.2), custom_call_target="tpu_custom_call" | custom-call | bytes 3500000 | tf_op jit(solution)/shard_map/pack_rows/pallas_call | solution.py:563
  1.9 3.1 %collective-permute-start = (f32[7,72,256]{2,1,0:T(8,128)S(1)}, f32[7,72,256]{2,1,0:T(8,128)S(1)}, u32[]{:S(2)}, u32[]{:S(2)}) collective-permute-start(f32[7,72,256]{2,1,0:T(8,128)S(1)} %get-tuple-element.45), channel_id=1, source_target_pairs={{0,1},{1,0},{2,3},{3,2},{4,5},{5,4},{6,7},{7,6},{8,9},{9,8},{10,11... | collective-permute-start | bytes 1548296 | tf_op jit(solution)/shard_map/ppermute | solution.py:508
  5.0 0.0 collective-permute-start.1
  5.0 0.5 %collective-permute-start.2 = (f32[3,8,256]{2,1,0:T(8,128)S(1)}, f32[3,8,256]{2,1,0:T(8,128)S(1)}, u32[]{:S(2)}, u32[]{:S(2)}) collective-permute-start(f32[3,8,256]{2,1,0:T(8,128)S(1)} %get-tuple-element.47.top), channel_id=1, source_target_pairs={{0,4},{4,0},{8,12},{12,8},{16,20},{20,16},{24,28},{28,24},{1,5},{5... | collective-permute-start | bytes 73736 | tf_op jit(solution)/shard_map/ppermute | solution.py:513
  6.2 0.8 %collective-permute-done.2.other = f32[3,8,256]{2,1,0:T(8,128)S(1)} collective-permute-done((f32[3,8,256]{2,1,0:T(8,128)S(1)}, f32[3,8,256]{2,1,0:T(8,128)S(1)}, u32[]{:S(2)}, u32[]{:S(2)}) %collective-permute-start.2) | collective-permute-done | bytes 24608 | tf_op jit(solution)/shard_map/ppermute | solution.py:513
  6.9 2.4 %collective-permute-start.3 = (f32[3,8,256]{2,1,0:T(8,128)S(1)}, f32[3,8,256]{2,1,0:T(8,128)S(1)}, u32[]{:S(2)}, u32[]{:S(2)}) collective-permute-start(f32[3,8,256]{2,1,0:T(8,128)S(1)} %owner_surface.1.top_a), channel_id=1, source_target_pairs={{0,24},{4,28},{8,16},{12,20},{16,8},{20,12},{24,0},{28,4},{1,25},{... | collective-permute-start | bytes 73736 | tf_op jit(solution)/shard_map/ppermute | solution.py:513
  9.4 0.5 %collective-permute-start.4 = (f32[3,8,256]{2,1,0:T(8,128)S(1)}, f32[3,8,256]{2,1,0:T(8,128)S(1)}, u32[]{:S(2)}, u32[]{:S(2)}) collective-permute-start(f32[3,8,256]{2,1,0:T(8,128)S(1)} %owner_surface.1.top_a), channel_id=1, source_target_pairs={{0,16},{4,20},{8,24},{12,28},{16,0},{20,4},{24,8},{28,12},{1,17},{... | collective-permute-start | bytes 73736 | tf_op jit(solution)/shard_map/ppermute | solution.py:513
  9.9 0.5 %collective-permute-start.5 = (f32[3,8,256]{2,1,0:T(8,128)S(1)}, f32[3,8,256]{2,1,0:T(8,128)S(1)}, u32[]{:S(2)}, u32[]{:S(2)}) collective-permute-start(f32[3,8,256]{2,1,0:T(8,128)S(1)} %owner_surface.1.top_a), channel_id=1, source_target_pairs={{0,8},{4,12},{8,0},{12,4},{16,24},{20,28},{24,16},{28,20},{1,9},{5... | collective-permute-start | bytes 73736 | tf_op jit(solution)/shard_map/ppermute | solution.py:513
  10.4 1.6 %sea_tables.1 = (f32[4,2,64,8,128]{4,3,2,1,0:T(8,128)S(1)}, bf16[64,192]{1,0:T(8,128)(2,1)S(1)}, f32[62,8,128]{2,1,0:T(8,128)S(1)}, f32[8,256]{1,0:T(8,128)S(1)}) custom-call(s32[1]{0:T(128)S(6)} %copy.43.owner, f32[1,4,62,8,256]{4,3,2,1,0:T(8,128)} %bitcast.3, s32[8,256]{1,0:T(8,128)} %land_in.1, f32[62,62]{1,0:T(8,128)} %sea_mixing_in.1), custom_call_target="tpu_custom_call" | custom-call | bytes 5250000 | tf_op jit(solution)/shard_map/sea_tables/pallas_call | solution.py:584
  12.1 1.7 %tables.1 = (f32[5,16,4,72,256]{4,3,2,1,0:T(8,128)S(1)}, bf16[3,72,240]{2,1,0:T(8,128)(2,1)S(1)}, f32[16,1,256]{2,1,0:T(1,128)S(1)}, f32[16,1,256]{2,1,0:T(1,128)S(1)}, f32[8,256]{1,0:T(8,128)S(1)}) custom-call(f32[1,4,8,72,256]{4,3,2,1,0:T(8,128)} %air.3, f32[8,256]{1,0:T(8,128)} %transfer.1, f32[72,72]{1,0:T(8,128)} %air_mixing_in.1, ...), custom_call_target="tpu_custom_call" | custom-call | bytes 5250000 | tf_op jit(solution)/shard_map/tables/pallas_call | solution.py:613
  13.8 0.0 collective-permute-done.3.top_b
  13.8 0.0 collective-permute-done.4.top_c
  13.8 0.0 collective-permute-done.5.top_d
  13.8 0.1 surface.1
  13.9 2.5 %collective-permute-start.6 = (f32[88,256]{1,0:T(8,128)S(1)}, f32[88,256]{1,0:T(8,128)S(1)}, u32[]{:S(2)}, u32[]{:S(2)}) collective-permute-start(f32[88,256]{1,0:T(8,128)S(1)} %get-tuple-element.50), channel_id=1, source_target_pairs={{0,1},{1,0},{2,3},{3,2},{4,5},{5,4},{6,7},{7,6},{8,9},{9,8},{10,11... | collective-permute-start | bytes 270344 | tf_op jit(solution)/shard_map/ppermute | solution.py:508
  16.4 0.0 collective-permute-start.7
  16.4 1.6 %first_interior.1 = (f32[5,16,4,72,256]{4,3,2,1,0:T(8,128)S(1)}, f32[16,4,1,256]{3,2,1,0:T(1,128)S(1)}, f32[4,72,256]{2,1,0:T(8,128)S(1)}, f32[4,72,256]{2,1,0:T(8,128)S(1)}) custom-call(bf16[3,72,240]{2,1,0:T(8,128)(2,1)S(1)} %get-tuple-element.42.weights, f32[16,1,256]{2,1,0:T(1,128)S(1)} %get-tuple-element.43.turn, ...), custom_call_target="tpu_custom_call", output_to_operand_aliasing={{0}: (4, {})} | custom-call | bytes 1750000 | tf_op jit(solution)/shard_map/first_interior/pallas_call | solution.py:647
  18.1 1.3 %collective-permute-start.8 = (f32[4,72,256]{2,1,0:T(8,128)S(1)}, f32[4,72,256]{2,1,0:T(8,128)S(1)}, u32[]{:S(2)}, u32[]{:S(2)}) collective-permute-start(f32[4,72,256]{2,1,0:T(8,128)S(1)} %get-tuple-element.61), channel_id=1, source_target_pairs={{0,1},{1,0},{2,3},{3,2},{4,5},{5,4},{6,7},{7,6},{8,9},{9,8},{10,11... | collective-permute-start | bytes 884744 | tf_op jit(solution)/shard_map/ppermute | solution.py:508
  19.3 0.0 collective-permute-done.near
  19.3 0.0 collective-permute-start.9
  19.3 1.5 %interior.1 = (f32[5,16,4,72,256]{4,3,2,1,0:T(8,128)S(1)}, f32[16,4,1,256]{3,2,1,0:T(1,128)S(1)}) custom-call(bf16[3,72,240]{2,1,0:T(8,128)(2,1)S(1)} %get-tuple-element.42.weights, f32[16,1,256]{2,1,0:T(1,128)S(1)} %get-tuple-element.43.turn, f32[16,1,256]{2,1,0:T(1,128)S(1)} %get-tuple-element.44.valid, ...), custom_call_target="tpu_custom_call", output_to_operand_aliasing={{0}: (5, {}), {1}: (6, {})} | custom-call | bytes 8750000 | tf_op jit(solution)/shard_map/interior/pallas_call | solution.py:660
  20.8 0.0 collective-permute-done.1.far
  20.9 1.9 %first_chain.1 = (f32[5,16,4,72,256]{4,3,2,1,0:T(8,128)S(1)}, f32[16,4,1,256]{3,2,1,0:T(1,128)S(1)}) custom-call(bf16[3,72,240]{2,1,0:T(8,128)(2,1)S(1)} %get-tuple-element.42.weights, f32[16,1,256]{2,1,0:T(1,128)S(1)} %get-tuple-element.43.turn, f32[16,1,256]{2,1,0:T(1,128)S(1)} %get-tuple-element.44.valid, ...), custom_call_target="tpu_custom_call", output_to_operand_aliasing={{0}: (5, {}), {1}: (6, {})} | custom-call | bytes 7000000 | tf_op jit(solution)/shard_map/first_chain/pallas_call | solution.py:672
  22.7 0.0 collective-permute-done.6.near_rest
  22.8 0.0 collective-permute-done.7.far_rest
  22.8 1.6 %second_chain.1 = (f32[5,16,1,256]{3,2,1,0:T(1,128)S(1)}, f32[5,16,4,72,256]{4,3,2,1,0:T(8,128)S(1)}, f32[16,4,1,256]{3,2,1,0:T(1,128)S(1)}, f32[4,72,256]{2,1,0:T(8,128)S(1)}, f32[4,72,256]{2,1,0:T(8,128)S(1)}) custom-call(bf16[3,72,240]{2,1,0:T(8,128)(2,1)S(1)} %get-tuple-element.42.weights, ...), custom_call_target="tpu_custom_call", output_to_operand_aliasing={{0}: (7, {}), {1}: (8, {}), {2}: (9, {})} | custom-call | bytes 5250000 | tf_op jit(solution)/shard_map/second_chain/pallas_call | solution.py:684
  24.4 1.8 %collective-permute-start.14 = (f32[4,72,256]{2,1,0:T(8,128)S(1)}, f32[4,72,256]{2,1,0:T(8,128)S(1)}, u32[]{:S(2)}, u32[]{:S(2)}) collective-permute-start(f32[4,72,256]{2,1,0:T(8,128)S(1)} %get-tuple-element.69), channel_id=1, source_target_pairs={{0,1},{1,0},{2,3},{3,2},{4,5},{5,4},{6,7},{7,6},{8,9},{9,8},{10,11... | collective-permute-start | bytes 884744 | tf_op jit(solution)/shard_map/ppermute | solution.py:508
  26.2 0.0 collective-permute-start.15
  26.2 1.4 %collective-permute-done.8.near = f32[4,72,256]{2,1,0:T(8,128)S(1)} collective-permute-done((f32[4,72,256]{2,1,0:T(8,128)S(1)}, f32[4,72,256]{2,1,0:T(8,128)S(1)}, u32[]{:S(2)}, u32[]{:S(2)}) %collective-permute-start.8) | collective-permute-done | bytes 294944 | tf_op jit(solution)/shard_map/ppermute | solution.py:508
  27.6 0.0 collective-permute-done.9.far
  27.6 1.5 %third_chain.1 = (f32[5,16,4,72,256]{4,3,2,1,0:T(8,128)S(1)}, f32[16,4,1,256]{3,2,1,0:T(1,128)S(1)}, f32[4,8,256]{2,1,0:T(8,128)S(1)}) custom-call(bf16[3,72,240]{2,1,0:T(8,128)(2,1)S(1)} %get-tuple-element.42.weights, f32[16,1,256]{2,1,0:T(1,128)S(1)} %get-tuple-element.43.turn, ...), custom_call_target="tpu_custom_call", output_to_operand_aliasing={{0}: (6, {}), {1}: (7, {})} | custom-call | bytes 5250000 | tf_op jit(solution)/shard_map/third_chain/pallas_call | solution.py:699
  29.0 0.1 collective-permute-start.10
  29.1 1.0 %finish.1 = (f32[5,16,4,72,256]{4,3,2,1,0:T(8,128)S(1)}, f32[4,8,256]{2,1,0:T(8,128)S(1)}) custom-call(bf16[3,72,240]{2,1,0:T(8,128)(2,1)S(1)} %get-tuple-element.42.weights, f32[16,1,256]{2,1,0:T(1,128)S(1)} %get-tuple-element.43.turn, f32[16,1,256]{2,1,0:T(1,128)S(1)} %get-tuple-element.44.valid, ...), custom_call_target="tpu_custom_call", output_to_operand_aliasing={{0}: (5, {})} | custom-call | bytes 3500000 | tf_op jit(solution)/shard_map/finish/pallas_call | solution.py:713
  30.1 0.2 collective-permute-done.10
  30.3 2.4 %collective-permute-start.11 = (f32[4,8,256]{2,1,0:T(8,128)S(1)}, f32[4,8,256]{2,1,0:T(8,128)S(1)}, u32[]{:S(2)}, u32[]{:S(2)}) collective-permute-start(f32[4,8,256]{2,1,0:T(8,128)S(1)} %add.3.flux_a), channel_id=1, source_target_pairs={{0,24},{4,28},{8,16},{12,20},{16,8},{20,12},{24,0},{28,4},{1,25},{... | collective-permute-start | bytes 98312 | tf_op jit(solution)/shard_map/ppermute | solution.py:513
  32.8 0.5 %collective-permute-start.12 = (f32[4,8,256]{2,1,0:T(8,128)S(1)}, f32[4,8,256]{2,1,0:T(8,128)S(1)}, u32[]{:S(2)}, u32[]{:S(2)}) collective-permute-start(f32[4,8,256]{2,1,0:T(8,128)S(1)} %add.3.flux_a), channel_id=1, source_target_pairs={{0,16},{4,20},{8,24},{12,28},{16,0},{20,4},{24,8},{28,12},{1,17},{... | collective-permute-start | bytes 98312 | tf_op jit(solution)/shard_map/ppermute | solution.py:513
  33.3 0.5 %collective-permute-start.13 = (f32[4,8,256]{2,1,0:T(8,128)S(1)}, f32[4,8,256]{2,1,0:T(8,128)S(1)}, u32[]{:S(2)}, u32[]{:S(2)}) collective-permute-start(f32[4,8,256]{2,1,0:T(8,128)S(1)} %add.3.flux_a), channel_id=1, source_target_pairs={{0,8},{4,12},{8,0},{12,4},{16,24},{20,28},{24,16},{28,20},{1,9},{5... | collective-permute-start | bytes 98312 | tf_op jit(solution)/shard_map/ppermute | solution.py:513
  33.8 0.1 collective-permute-done.14.near
  33.9 0.0 collective-permute-done.15.far
  33.9 2.0 %last_chain.1 = (f32[5,16,4,72,256]{4,3,2,1,0:T(8,128)S(1)}, f32[1,4,8,72,256]{4,3,2,1,0:T(8,128)}, f32[1,4,62,8,256]{4,3,2,1,0:T(8,128)}) custom-call(s32[1]{0:T(128)S(6)} %copy.43.owner, bf16[3,72,240]{2,1,0:T(8,128)(2,1)S(1)} %get-tuple-element.42.weights, f32[16,1,256]{2,1,0:T(1,128)S(1)} %get-tuple-element.43.turn, ...), custom_call_target="tpu_custom_call", output_to_operand_aliasing={{0}: (8, {})} | custom-call | bytes 8750000 | tf_op jit(solution)/shard_map/last_chain/pallas_call | solution.py:730
  35.8 0.8 %last_rows.1.air_in = f32[1,4,8,72,256]{4,3,2,1,0:T(8,128)} custom-call(s32[1]{0:T(128)S(6)} %copy.43.owner, f32[5,16,4,72,256]{4,3,2,1,0:T(8,128)S(1)} %get-tuple-element.71.state, f32[1,4,8,72,256]{4,3,2,1,0:T(8,128)} %get-tuple-element.73.air_in), custom_call_target="tpu_custom_call", output_to_operand_aliasing={{}: (2, {})} | custom-call | bytes 2100000 | tf_op jit(solution)/shard_map/last_rows/pallas_call | solution.py:746
  36.7 0.0 collective-permute-done.11.flux_b
  36.7 0.0 collective-permute-done.12.flux_c
  36.7 0.5 %collective-permute-done.13.flux_d = f32[4,8,256]{2,1,0:T(8,128)S(1)} collective-permute-done((f32[4,8,256]{2,1,0:T(8,128)S(1)}, f32[4,8,256]{2,1,0:T(8,128)S(1)}, u32[]{:S(2)}, u32[]{:S(2)}) %collective-permute-start.13) | collective-permute-done | bytes 32800 | tf_op jit(solution)/shard_map/ppermute | solution.py:513
  37.2 0.1 sea_step.1
  (4 shorter events, 0.0 us)
Async XLA Ops:
  1.9 17.4 %collective-permute-start = (f32[7,72,256]{2,1,0:T(8,128)S(1)}, f32[7,72,256]{2,1,0:T(8,128)S(1)}, u32[]{:S(2)}, u32[]{:S(2)}) collective-permute-start(f32[7,72,256]{2,1,0:T(8,128)S(1)} %get-tuple-element.45), channel_id=1, source_target_pairs={{0,1},{1,0},{2,3},{3,2},{4,5},{5,4},{6,7},{7,6},{8,9},{9,8},{10,11... | collective-permute-start | bytes 1548296 | tf_op jit(solution)/shard_map/ppermute | solution.py:508
  5.0 15.8 %collective-permute-start.1 = (f32[7,72,256]{2,1,0:T(8,128)S(1)}, f32[7,72,256]{2,1,0:T(8,128)S(1)}, u32[]{:S(2)}, u32[]{:S(2)}) collective-permute-start(f32[7,72,256]{2,1,0:T(8,128)S(1)} %get-tuple-element.46), channel_id=1, source_target_pairs={{0,4},{1,2},{2,1},{3,7},{4,0},{5,6},{6,5},{7,3},{8,12},{9,10},{10,... | collective-permute-start | bytes 1548296 | tf_op jit(solution)/shard_map/ppermute | solution.py:508
  5.0 1.9 %collective-permute-start.2 = (f32[3,8,256]{2,1,0:T(8,128)S(1)}, f32[3,8,256]{2,1,0:T(8,128)S(1)}, u32[]{:S(2)}, u32[]{:S(2)}) collective-permute-start(f32[3,8,256]{2,1,0:T(8,128)S(1)} %get-tuple-element.47.top), channel_id=1, source_target_pairs={{0,4},{4,0},{8,12},{12,8},{16,20},{20,16},{24,28},{28,24},{1,5},{5... | collective-permute-start | bytes 73736 | tf_op jit(solution)/shard_map/ppermute | solution.py:513
  6.9 6.9 %collective-permute-start.3 = (f32[3,8,256]{2,1,0:T(8,128)S(1)}, f32[3,8,256]{2,1,0:T(8,128)S(1)}, u32[]{:S(2)}, u32[]{:S(2)}) collective-permute-start(f32[3,8,256]{2,1,0:T(8,128)S(1)} %owner_surface.1.top_a), channel_id=1, source_target_pairs={{0,24},{4,28},{8,16},{12,20},{16,8},{20,12},{24,0},{28,4},{1,25},{... | collective-permute-start | bytes 73736 | tf_op jit(solution)/shard_map/ppermute | solution.py:513
  9.4 4.4 %collective-permute-start.4 = (f32[3,8,256]{2,1,0:T(8,128)S(1)}, f32[3,8,256]{2,1,0:T(8,128)S(1)}, u32[]{:S(2)}, u32[]{:S(2)}) collective-permute-start(f32[3,8,256]{2,1,0:T(8,128)S(1)} %owner_surface.1.top_a), channel_id=1, source_target_pairs={{0,16},{4,20},{8,24},{12,28},{16,0},{20,4},{24,8},{28,12},{1,17},{... | collective-permute-start | bytes 73736 | tf_op jit(solution)/shard_map/ppermute | solution.py:513
  9.9 3.9 %collective-permute-start.5 = (f32[3,8,256]{2,1,0:T(8,128)S(1)}, f32[3,8,256]{2,1,0:T(8,128)S(1)}, u32[]{:S(2)}, u32[]{:S(2)}) collective-permute-start(f32[3,8,256]{2,1,0:T(8,128)S(1)} %owner_surface.1.top_a), channel_id=1, source_target_pairs={{0,8},{4,12},{8,0},{12,4},{16,24},{20,28},{24,16},{28,20},{1,9},{5... | collective-permute-start | bytes 73736 | tf_op jit(solution)/shard_map/ppermute | solution.py:513
  13.9 8.8 %collective-permute-start.6 = (f32[88,256]{1,0:T(8,128)S(1)}, f32[88,256]{1,0:T(8,128)S(1)}, u32[]{:S(2)}, u32[]{:S(2)}) collective-permute-start(f32[88,256]{1,0:T(8,128)S(1)} %get-tuple-element.50), channel_id=1, source_target_pairs={{0,1},{1,0},{2,3},{3,2},{4,5},{5,4},{6,7},{7,6},{8,9},{9,8},{10,11... | collective-permute-start | bytes 270344 | tf_op jit(solution)/shard_map/ppermute | solution.py:508
  16.4 6.3 %collective-permute-start.7 = (f32[88,256]{1,0:T(8,128)S(1)}, f32[88,256]{1,0:T(8,128)S(1)}, u32[]{:S(2)}, u32[]{:S(2)}) collective-permute-start(f32[88,256]{1,0:T(8,128)S(1)} %get-tuple-element.51), channel_id=1, source_target_pairs={{0,4},{1,2},{2,1},{3,7},{4,0},{5,6},{6,5},{7,3},{8,12},{9,10},{10,... | collective-permute-start | bytes 270344 | tf_op jit(solution)/shard_map/ppermute | solution.py:508
  18.1 9.5 %collective-permute-start.8 = (f32[4,72,256]{2,1,0:T(8,128)S(1)}, f32[4,72,256]{2,1,0:T(8,128)S(1)}, u32[]{:S(2)}, u32[]{:S(2)}) collective-permute-start(f32[4,72,256]{2,1,0:T(8,128)S(1)} %get-tuple-element.61), channel_id=1, source_target_pairs={{0,1},{1,0},{2,3},{3,2},{4,5},{5,4},{6,7},{7,6},{8,9},{9,8},{10,11... | collective-permute-start | bytes 884744 | tf_op jit(solution)/shard_map/ppermute | solution.py:508
  19.3 8.2 %collective-permute-start.9 = (f32[4,72,256]{2,1,0:T(8,128)S(1)}, f32[4,72,256]{2,1,0:T(8,128)S(1)}, u32[]{:S(2)}, u32[]{:S(2)}) collective-permute-start(f32[4,72,256]{2,1,0:T(8,128)S(1)} %get-tuple-element.62), channel_id=1, source_target_pairs={{0,4},{1,2},{2,1},{3,7},{4,0},{5,6},{6,5},{7,3},{8,12},{9,10},{10,... | collective-permute-start | bytes 884744 | tf_op jit(solution)/shard_map/ppermute | solution.py:508
  24.4 9.5 %collective-permute-start.14 = (f32[4,72,256]{2,1,0:T(8,128)S(1)}, f32[4,72,256]{2,1,0:T(8,128)S(1)}, u32[]{:S(2)}, u32[]{:S(2)}) collective-permute-start(f32[4,72,256]{2,1,0:T(8,128)S(1)} %get-tuple-element.69), channel_id=1, source_target_pairs={{0,1},{1,0},{2,3},{3,2},{4,5},{5,4},{6,7},{7,6},{8,9},{9,8},{10,11... | collective-permute-start | bytes 884744 | tf_op jit(solution)/shard_map/ppermute | solution.py:508
  26.2 7.7 %collective-permute-start.15 = (f32[4,72,256]{2,1,0:T(8,128)S(1)}, f32[4,72,256]{2,1,0:T(8,128)S(1)}, u32[]{:S(2)}, u32[]{:S(2)}) collective-permute-start(f32[4,72,256]{2,1,0:T(8,128)S(1)} %get-tuple-element.70), channel_id=1, source_target_pairs={{0,4},{1,2},{2,1},{3,7},{4,0},{5,6},{6,5},{7,3},{8,12},{9,10},{10,... | collective-permute-start | bytes 884744 | tf_op jit(solution)/shard_map/ppermute | solution.py:508
  29.0 1.3 %collective-permute-start.10 = (f32[4,8,256]{2,1,0:T(8,128)S(1)}, f32[4,8,256]{2,1,0:T(8,128)S(1)}, u32[]{:S(2)}, u32[]{:S(2)}) collective-permute-start(f32[4,8,256]{2,1,0:T(8,128)S(1)} %get-tuple-element.64.flux_in), channel_id=1, source_target_pairs={{0,4},{4,0},{8,12},{12,8},{16,20},{20,16},{24,28},{28,24},{1,5},{5... | collective-permute-start | bytes 98312 | tf_op jit(solution)/shard_map/ppermute | solution.py:513
  30.3 6.4 %collective-permute-start.11 = (f32[4,8,256]{2,1,0:T(8,128)S(1)}, f32[4,8,256]{2,1,0:T(8,128)S(1)}, u32[]{:S(2)}, u32[]{:S(2)}) collective-permute-start(f32[4,8,256]{2,1,0:T(8,128)S(1)} %add.3.flux_a), channel_id=1, source_target_pairs={{0,24},{4,28},{8,16},{12,20},{16,8},{20,12},{24,0},{28,4},{1,25},{... | collective-permute-start | bytes 98312 | tf_op jit(solution)/shard_map/ppermute | solution.py:513
  32.8 4.0 %collective-permute-start.12 = (f32[4,8,256]{2,1,0:T(8,128)S(1)}, f32[4,8,256]{2,1,0:T(8,128)S(1)}, u32[]{:S(2)}, u32[]{:S(2)}) collective-permute-start(f32[4,8,256]{2,1,0:T(8,128)S(1)} %add.3.flux_a), channel_id=1, source_target_pairs={{0,16},{4,20},{8,24},{12,28},{16,0},{20,4},{24,8},{28,12},{1,17},{... | collective-permute-start | bytes 98312 | tf_op jit(solution)/shard_map/ppermute | solution.py:513
  33.3 3.9 %collective-permute-start.13 = (f32[4,8,256]{2,1,0:T(8,128)S(1)}, f32[4,8,256]{2,1,0:T(8,128)S(1)}, u32[]{:S(2)}, u32[]{:S(2)}) collective-permute-start(f32[4,8,256]{2,1,0:T(8,128)S(1)} %add.3.flux_a), channel_id=1, source_target_pairs={{0,8},{4,12},{8,0},{12,4},{16,24},{20,28},{24,16},{28,20},{1,9},{5... | collective-permute-start | bytes 98312 | tf_op jit(solution)/shard_map/ppermute | solution.py:513
